TPU v7x, 128 devices: a whole 4x4x4 slice. The times are simulated.
128 devices in a mesh: tm: 8 (over z, x_lo), space: 16 (over x_hi, y, core).
Axes of the slice: x: 4 (x_hi: 2, x_lo: 2; x = x_hi * 2 + x_lo), y: 4, z: 4, core: 2. Of those that a mesh axis runs over, the one named last changes fastest.
Arguments:
- activations: bfloat16 [1, 32, 1024, 1280], P(None, 'tm', 'space'), may hold values from -6 to 6
- grad_out: bfloat16 [1, 32, 1024, 1280], P(None, 'tm', 'space'), may hold values from -6 to 6
- norm_gain: float32 [1280], replicated, may hold values from 0.1 to 1.9
- qkv_weight: bfloat16 [1280, 3840], replicated, may hold values from -4 to 4, as said below
- out_weight: bfloat16 [1280, 1280], replicated, may hold values from -0.15625 to 0.15625
Outputs:
- grad_tokens: bfloat16 [1, 32, 1024, 1280], P(None, 'tm', 'space')
- qkv_grad: float32 [1280, 3840], P(('tm', 'space'))
- out_grad: float32 [1280, 1280], P(('tm', 'space'))
- gain_grad: float32 [1280], P(('tm', 'space'))
Inputs may be any that keep to these rules, and one draw needn't show every extreme that they name: `qkv_weight`: columns ordered (query, key, value), then head, then position in the head.
All inputs are finite; a program needn't handle non-finite values.
Results may differ from a plain program's by a relative error of at most 0.015.
The roundings to bfloat16 on the way count: a program that leaves them out, or rounds other values in their place, can miss the bound.
Values may be sent and summed in bfloat16 or wider, within the bound.
No kernel may reach another device: no remote copies, remote signals or barrier semaphores. Data moves between devices by JAX's collectives and lax.ppermute only.
A program may use at most 192 MiB of HBM per device.

v0:
```python
import math

import jax
import jax.numpy as jnp
from jax import lax
from jax.sharding import PartitionSpec as P

HEADS = 16
FRAMES = 32
VIDEOS = 1


def contract(form, left, right):
    return jnp.einsum(form, left, right, preferred_element_type=jnp.float32)


def on_device(activations, grad_out, norm_gain, qkv_weight, out_weight):
    local_x, local_cot = (
        lax.all_to_all(activations, "tm", split_axis=2, concat_axis=1, tiled=True),
        lax.all_to_all(grad_out, "tm", split_axis=2, concat_axis=1, tiled=True),
    )
    video_count, frame_count, place_count, model_width = local_x.shape
    head_size = model_width // HEADS
    token_count = video_count * frame_count * place_count
    inverse_root = 1.0 / math.sqrt(head_size)
    factor = 1.0 / math.sqrt(VIDEOS * FRAMES * activations.shape[2] * lax.axis_size("space"))
    x_wide = local_x.astype(jnp.float32)
    row_mean = jnp.mean(x_wide, axis=-1, keepdims=True)
    centred = x_wide - row_mean
    variance = jnp.mean(centred * centred, axis=-1, keepdims=True)
    inv_std = lax.rsqrt(variance + 1e-06)
    normalized = centred * inv_std
    gained = (normalized * norm_gain).astype(jnp.bfloat16)
    flat_norm = gained.reshape(token_count, model_width)
    qkv_all = jnp.dot(flat_norm, qkv_weight, preferred_element_type=jnp.float32).astype(
        jnp.bfloat16
    )
    qkv_all = qkv_all.reshape(video_count, frame_count, place_count, 3, HEADS, head_size)
    query_rows = qkv_all[:, :, :, 0]
    key_rows = qkv_all[:, :, :, 1]
    value_rows = qkv_all[:, :, :, 2]
    scores = contract("vfphe,vgphe->vphfg", query_rows, key_rows) * inverse_root
    row_max = jnp.max(scores, axis=-1, keepdims=True)
    shifted = jnp.exp(scores - row_max)
    attn_prob = shifted / jnp.sum(shifted, axis=-1, keepdims=True)
    prob_low = attn_prob.astype(jnp.bfloat16)
    attended = contract("vphfg,vgphe->vfphe", prob_low, value_rows).astype(jnp.bfloat16)
    attended = attended.reshape(token_count, model_width)
    cotangent = local_cot.reshape(token_count, model_width)
    out_term = lax.dot_general(
        attended, cotangent, (((0,), (0,)), ((), ())), preferred_element_type=jnp.float32
    )
    attn_grad = lax.dot_general(
        cotangent, out_weight, (((1,), (1,)), ((), ())), preferred_element_type=jnp.float32
    )
    attn_grad = attn_grad.astype(jnp.bfloat16).reshape(
        video_count, frame_count, place_count, HEADS, head_size
    )
    prob_grad = contract("vfphe,vgphe->vphfg", attn_grad, value_rows)
    score_grad = (
        attn_prob
        * (prob_grad - jnp.sum(prob_grad * attn_prob, axis=-1, keepdims=True))
        * inverse_root
    ).astype(jnp.bfloat16)
    value_grad = contract("vphfg,vfphe->vgphe", prob_low, attn_grad).astype(jnp.bfloat16)
    query_grad = contract("vphfg,vgphe->vfphe", score_grad, key_rows).astype(jnp.bfloat16)
    key_grad = contract("vphfg,vfphe->vgphe", score_grad, query_rows).astype(jnp.bfloat16)
    stacked = jnp.stack([query_grad, key_grad, value_grad], axis=3).reshape(
        token_count, 3 * model_width
    )
    qkv_term = lax.dot_general(
        flat_norm, stacked, (((0,), (0,)), ((), ())), preferred_element_type=jnp.float32
    )
    normed_grad = lax.dot_general(
        stacked, qkv_weight, (((1,), (1,)), ((), ())), preferred_element_type=jnp.float32
    )
    flat_hat = normalized.reshape(token_count, model_width)
    gain_term = jnp.sum(normed_grad * flat_hat, axis=0)
    scaled_grad = normed_grad * norm_gain
    flat_std = inv_std.reshape(token_count, 1)
    input_grad = flat_std * (
        scaled_grad
        - jnp.mean(scaled_grad, axis=-1, keepdims=True)
        - flat_hat * jnp.mean(scaled_grad * flat_hat, axis=-1, keepdims=True)
    )
    local_grad = (cotangent.astype(jnp.float32) + input_grad).astype(jnp.bfloat16)
    local_grad = local_grad.reshape(video_count, frame_count, place_count, model_width)
    grad_tokens = lax.all_to_all(local_grad, "tm", split_axis=1, concat_axis=2, tiled=True)
    qkv_part, out_part, gain_part = (
        lax.psum_scatter(qkv_term, ("tm", "space"), scatter_dimension=0, tiled=True),
        lax.psum_scatter(out_term, ("tm", "space"), scatter_dimension=0, tiled=True),
        lax.psum_scatter(gain_term, ("tm", "space"), scatter_dimension=0, tiled=True),
    )
    return (grad_tokens, qkv_part * factor, out_part * factor, gain_part * factor)


def solution(mesh):
    in_specs = (P(None, "tm", "space", None), P(None, "tm", "space", None), P(), P(), P())
    out_specs = (
        P(None, "tm", "space", None),
        P(("tm", "space"), None),
        P(("tm", "space"), None),
        P(("tm", "space")),
    )
    return jax.shard_map(
        on_device, mesh=mesh, in_specs=in_specs, out_specs=out_specs, check_vma=False
    )
```

profile of v0, /device:TPU:1, one launch (start us, length us, event | category | flops | bytes accessed | tf_op | source)
XLA Modules:
  0.0 363.8 jit_solution(16707422654973999331)
XLA Ops:
  7.2 0.0 copy-start
  7.2 2.6 copy.33
  9.8 6.8 %all-to-all-start.1 = ((bf16[1,4,64,1280]{3,1,0,2:T(4,128)(2,1)}), bf16[1,4,64,1280]{3,1,0,2:T(4,128)(2,1)}, u32[]{:S(2)}, u32[]{:S(2)}) async-start(bf16[1,4,64,1280]{3,1,0,2:T(4,128)(2,1)} %copy.33), calls=%async_computation.1 | async-start | bytes 1310720 | tf_op jit(solution)/shard_map/all_to_all | solution.py:19
  16.6 2.4 copy.31
  19.0 8.0 %all-to-all-done.1 = bf16[1,4,64,1280]{3,1,0,2:T(4,128)(2,1)} async-done(((bf16[1,4,64,1280]{3,1,0,2:T(4,128)(2,1)}), bf16[1,4,64,1280]{3,1,0,2:T(4,128)(2,1)}, u32[]{:S(2)}, u32[]{:S(2)}) %all-to-all-start.1) | async-done | bytes 655392 | tf_op jit(solution)/shard_map/all_to_all | solution.py:19
  27.0 4.2 %all-to-all-start = ((bf16[1,4,64,1280]{3,1,0,2:T(4,128)(2,1)}), bf16[1,4,64,1280]{3,1,0,2:T(4,128)(2,1)}, u32[]{:S(2)}, u32[]{:S(2)}) async-start(bf16[1,4,64,1280]{3,1,0,2:T(4,128)(2,1)} %copy.31), calls=%async_computation | async-start | bytes 1310720 | tf_op jit(solution)/shard_map/all_to_all | solution.py:20
  31.2 0.0 all-reduce.6.cloned.1.call-start
  31.2 2.2 copy.34
  33.4 1.2 convert.5
  34.6 0.0 copy-start.2
  34.6 1.1 copy-done.2
  35.7 0.3 bitcast_reduce_fusion
  36.0 0.1 div.25
  36.1 1.7 multiply_reduce_fusion.4
  37.8 2.8 all-to-all-done
  40.5 1.2 copy.32
  41.7 0.0 copy-start.7
  41.7 0.9 copy-done.7
  42.6 0.0 copy-done
  42.6 1.9 convolution_convert_fusion.1
  44.5 3.4 reshape.204
  47.9 0.1 rsqrt.17
  48.0 0.0 copy-done.16
  48.0 0.0 copy-done.3
  48.1 1.2 multiply_convert_fusion.1
  49.3 0.0 copy-done.4
  49.3 0.2 multiply_convert_fusion.2
  49.5 7.8 %convolution_convert_fusion = bf16[256,3840]{1,0:T(8,128)(2,1)} fusion(bf16[256,1280]{1,0:T(8,128)(2,1)S(1)} %multiply_convert_fusion.2, bf16[1280,3840]{1,0:T(8,128)(2,1)} %param.8), kind=kOutput, calls=%fused_computation.2 | convolution fusion | flops 2517565440 | bytes 12451840 | tf_op jit(solution)/shard_map/dot_general | solution.py:35
  57.3 6.6 %reshape.201 = bf16[1,32,8,3,16,80]{5,4,3,2,1,0:T(8,128)(2,1)S(1)} reshape(bf16[256,3840]{1,0:T(8,128)(2,1)} %convolution_convert_fusion) | data formatting | bytes 3932160 | tf_op jit(solution)/shard_map/reshape | solution.py:38
  63.9 0.0 copy-start.10
  63.9 2.0 fusion.41
  65.9 0.0 copy-done.10
  65.9 1.4 fusion.31
  67.3 0.0 copy-done.12
  67.3 4.8 %fusion.42 = (f32[8,16,32]{2,1,0:T(8,128)S(1)}, f32[8,16,32,32]{2,3,1,0:T(8,128)}) fusion(bf16[1,32,8,1,16,80]{5,4,3,2,1,0:T(8,128)(2,1)} %get-tuple-element.11, bf16[1,32,8,1,16,80]{5,4,3,2,1,0:T(8,128)(2,1)} %get-tuple-element.10), kind=kOutput, calls=%fused_computation.59 | convolution fusion | flops 21364768 | bytes 1851392 | tf_op jit(solution)/shard_map/sub | solution.py:44
  72.2 0.0 copy-done.11
  72.2 3.4 fusion.19
  75.6 4.8 %fusion.20 = bf16[1,32,8,1,16,80]{5,1,4,2,3,0:T(8,128)(2,1)} fusion(f32[8,16,32,32]{2,3,1,0:T(8,128)S(1)} %fusion.31, bf16[1,32,8,1,16,80]{5,4,3,2,1,0:T(8,128)(2,1)} %get-tuple-element.10, f32[8,16,32,32]{2,3,1,0:T(8,128)} %get-tuple-element.13, f32[8,16,32]{2,1,0:T(8,128)S(1)} %get-tuple-element.12), kind=kOutput, calls=%fused_computation.19 | convolution fusion | flops 22220832 | bytes 2375680 | tf_op jit(solution)/shard_map/vphfg,vfphe->vgphe/dot_general | solution.py:14
  80.4 5.0 %fusion.23 = bf16[1,32,8,1,16,80]{5,1,4,2,3,0:T(8,128)(2,1)} fusion(f32[8,16,32,32]{2,3,1,0:T(8,128)S(1)} %fusion.31, bf16[1,32,8,1,16,80]{5,4,3,2,1,0:T(8,128)(2,1)} %get-tuple-element.11, f32[8,16,32,32]{2,3,1,0:T(8,128)} %get-tuple-element.13, f32[8,16,32]{2,1,0:T(8,128)S(1)} %get-tuple-element.12), kind=kOutput, calls=%fused_computation.20 | convolution fusion | flops 22220832 | bytes 2375680 | tf_op jit(solution)/shard_map/vphfg,vgphe->vfphe/dot_general | solution.py:14
  85.3 0.0 copy-done.13
  85.4 2.5 fusion.18
  87.9 0.4 copy.45
  88.3 2.0 reshape.208
  90.3 2.6 pad_maximum_fusion
  92.9 3.1 copy.41
  96.1 5.1 %reshape.206 = bf16[256,3840]{1,0:T(8,128)(2,1)S(1)} reshape(bf16[1,32,8,3,16,80]{5,4,3,2,1,0:T(8,128)(2,1)} %copy.41) | data formatting | bytes 3932160 | tf_op jit(solution)/shard_map/reshape | solution.py:68
  101.2 0.0 copy-start.15
  101.2 3.8 %fusion.44 = f32[1280,1280]{1,0:T(8,128)} fusion(bf16[256,1280]{1,0:T(8,128)(2,1)S(1)} %copy-done.14, bf16[256,1280]{1,0:T(8,128)(2,1)S(1)} %bitcast.102), kind=kOutput, calls=%fused_computation.61 | convolution fusion | flops 838860800 | bytes 7864320 | tf_op jit(solution)/shard_map/dot_general | solution.py:50
  105.0 0.0 copy-done.15
  105.0 8.2 %fusion.43 = f32[1280,3840]{1,0:T(8,128)} fusion(bf16[256,1280]{1,0:T(8,128)(2,1)S(1)} %bitcast.103, bf16[256,3840]{1,0:T(8,128)(2,1)S(1)} %reshape.206), kind=kOutput, calls=%fused_computation.60 | convolution fusion | flops 2516582400 | bytes 22282240 | tf_op jit(solution)/shard_map/dot_general | solution.py:71
  113.2 0.0 all-reduce.6.cloned.1.call-update
  113.2 1.3 copy-done.5
  114.5 6.9 %multiply_reduce_fusion.2 = (f32[1280]{0:T(1024)S(1)}, f32[256]{0:T(256)S(1)}, f32[256]{0:T(256)S(1)}, f32[256,1280]{1,0:T(8,128)S(1)}) fusion(f32[1,4,8,8,1280]{4,3,1,2,0:T(8,128)S(1)} %copy-done.5, f32[256]{0:T(256)S(1)} %div.25, f32[256]{0:T(256)S(1)} %rsqrt.17, f32[1280]{0:T(1024)S(1)} %copy-done.16, bf16[256,3840]{1,0:T(8,128)(2,1)S(1)} %reshape.206, ...), kind=kOutput, calls=%fused_computation.25 | convolution fusion | flops 2519202048 | bytes 14432256 | tf_op jit(solution)/shard_map/dot_general | solution.py:74
  121.4 0.0 copy-start.1
  121.4 1.4 add_convert_fusion
  122.8 4.3 %all-to-all-start.2 = ((bf16[1,32,8,1280]{3,2,0,1:T(8,128)(2,1)}), bf16[1,32,8,1280]{3,2,0,1:T(8,128)(2,1)}, u32[]{:S(2)}, u32[]{:S(2)}) async-start(bf16[1,32,8,1280]{3,2,0,1:T(8,128)(2,1)} %bitcast.104), calls=%async_computation.2 | async-start | bytes 1310720 | tf_op jit(solution)/shard_map/all_to_all | solution.py:88
  127.1 72.1 %all-reduce.2 = f32[1280]{0:T(1024)S(1)} all-reduce(f32[1280]{0:T(1024)S(1)} %get-tuple-element.4), channel_id=4, replica_groups=mesh['tm'=8,'space'=16] {'tm','space'}, use_global_device_ids=true, to_apply=%region_10.0.clone | all-reduce | flops 1280 | bytes 10240
  199.2 0.6 dynamic-slice_multiply_fusion.2
  199.8 0.0 all-to-all-done.2
  199.8 2.0 copy.84
  201.7 151.9 %all-reduce.6.cloned.1.call-done = (f32[1280,3840]{1,0:T(8,128)}, f32[1280,1280]{1,0:T(8,128)}) async-done(((f32[1280,3840]{1,0:T(8,128)}, f32[1280,1280]{1,0:T(8,128)}), (f32[1280,3840]{1,0:T(8,128)}, f32[1280,1280]{1,0:T(8,128)})) %all-reduce.6.cloned.1.call-update) | async-done | bytes 26214416
  353.7 1.7 dynamic-slice_multiply_fusion
  355.4 1.5 dynamic-slice_multiply_fusion.1
  356.9 0.0 copy-done.1
  (18 shorter events, 0.1 us)
Async XLA Ops:
  7.2 35.4 %copy-start = (bf16[1280,1280]{1,0:T(8,128)(2,1)S(1)}, bf16[1280,1280]{1,0:T(8,128)(2,1)}, u32[]{:S(2)}) copy-start(bf16[1280,1280]{1,0:T(8,128)(2,1)} %param.9) | copy-start | bytes 9830404
  9.8 17.2 %all-to-all-start.1 = ((bf16[1,4,64,1280]{3,1,0,2:T(4,128)(2,1)}), bf16[1,4,64,1280]{3,1,0,2:T(4,128)(2,1)}, u32[]{:S(2)}, u32[]{:S(2)}) async-start(bf16[1,4,64,1280]{3,1,0,2:T(4,128)(2,1)} %copy.33), calls=%async_computation.1 | async-start | bytes 1310720 | tf_op jit(solution)/shard_map/all_to_all | solution.py:19
  27.0 13.6 %all-to-all-start = ((bf16[1,4,64,1280]{3,1,0,2:T(4,128)(2,1)}), bf16[1,4,64,1280]{3,1,0,2:T(4,128)(2,1)}, u32[]{:S(2)}, u32[]{:S(2)}) async-start(bf16[1,4,64,1280]{3,1,0,2:T(4,128)(2,1)} %copy.31), calls=%async_computation | async-start | bytes 1310720 | tf_op jit(solution)/shard_map/all_to_all | solution.py:20
  31.2 322.5 %all-reduce.6.cloned.1.call-start = ((), (), s32[]{:S(2)}) async-start(), calls=%async_computation.3 | async-start | bytes 52428800
  34.6 1.1 copy-start.2
  41.7 0.9 copy-start.7
  42.6 5.5 %copy-start.16 = (f32[1280]{0:T(1024)S(1)}, f32[1280]{0:T(1024)}, u32[]{:S(2)}) copy-start(f32[1280]{0:T(1024)} %param.7) | copy-start | bytes 15364
  44.5 3.6 copy-start.3
  44.5 4.8 %copy-start.4 = (f32[1,4,8,8,1280]{4,3,1,2,0:T(8,128)S(1)}, f32[1,4,8,8,1280]{4,3,1,2,0:T(8,128)}, u32[]{:S(2)}) copy-start(f32[1,4,8,8,1280]{4,3,1,2,0:T(8,128)} %copy.34) | copy-start | bytes 3932164
  63.9 2.0 copy-start.10
  65.9 1.4 copy-start.12
  67.3 4.9 %copy-start.11 = (bf16[32,8,16,80]{3,2,1,0:T(8,128)(2,1)S(1)}, bf16[32,8,16,80]{3,2,1,0:T(8,128)(2,1)}, u32[]{:S(2)}) copy-start(bf16[32,8,16,80]{3,2,1,0:T(8,128)(2,1)} %reshape.204) | copy-start | bytes 1966084
  80.4 5.0 %copy-start.13 = (bf16[1,32,8,1,16,80]{5,4,3,2,1,0:T(8,128)(2,1)S(1)}, bf16[1,32,8,1,16,80]{5,4,3,2,1,0:T(8,128)(2,1)}, u32[]{:S(2)}) copy-start(bf16[1,32,8,1,16,80]{5,4,3,2,1,0:T(8,128)(2,1)} %copy-done.12) | copy-start | bytes 1966084
  96.1 5.1 %copy-start.8 = (bf16[1,4,8,8,1280]{4,3,1,2,0:T(8,128)(2,1)S(1)}, bf16[1,4,8,8,1280]{4,3,1,2,0:T(8,128)(2,1)}, u32[]{:S(2)}) copy-start(bf16[1,4,8,8,1280]{4,3,1,2,0:T(8,128)(2,1)} %copy-done.7) | copy-start | bytes 1966084
  96.1 5.1 %copy-start.14 = (bf16[256,1280]{1,0:T(8,128)(2,1)S(1)}, bf16[256,1280]{1,0:T(8,128)(2,1)}, u32[]{:S(2)}) copy-start(bf16[256,1280]{1,0:T(8,128)(2,1)} %reshape.208) | copy-start | bytes 1966084
  101.2 3.8 %copy-start.15 = (bf16[1,8,4,8,1280]{4,3,2,1,0:T(8,128)(2,1)S(1)}, bf16[1,8,4,8,1280]{4,3,2,1,0:T(8,128)(2,1)}, u32[]{:S(2)}) copy-start(bf16[1,8,4,8,1280]{4,3,2,1,0:T(8,128)(2,1)} %multiply_convert_fusion.1) | copy-start | bytes 1966084
  113.2 1.3 copy-start.5
  114.5 6.9 %copy-start.6 = (f32[1,4,8,8,1280]{4,3,1,2,0:T(8,128)S(1)}, f32[1,4,8,8,1280]{4,3,1,2,0:T(8,128)}, u32[]{:S(2)}) copy-start(f32[1,4,8,8,1280]{4,3,1,2,0:T(8,128)} %copy.34) | copy-start | bytes 3932164
  114.5 6.9 %copy-start.9 = (bf16[1,4,8,8,1280]{4,3,1,2,0:T(8,128)(2,1)S(1)}, bf16[1,4,8,8,1280]{4,3,1,2,0:T(8,128)(2,1)}, u32[]{:S(2)}) copy-start(bf16[1,4,8,8,1280]{4,3,1,2,0:T(8,128)(2,1)} %copy-done.7) | copy-start | bytes 1966084
  121.4 235.5 %copy-start.1 = (bf16[1280,1280]{1,0:T(8,128)(2,1)S(1)}, bf16[1280,1280]{1,0:T(8,128)(2,1)}, u32[]{:S(2)}) copy-start(bf16[1280,1280]{1,0:T(8,128)(2,1)} %param.9) | copy-start | bytes 9830404
  122.8 77.0 %all-to-all-start.2 = ((bf16[1,32,8,1280]{3,2,0,1:T(8,128)(2,1)}), bf16[1,32,8,1280]{3,2,0,1:T(8,128)(2,1)}, u32[]{:S(2)}, u32[]{:S(2)}) async-start(bf16[1,32,8,1280]{3,2,0,1:T(8,128)(2,1)} %bitcast.104), calls=%async_computation.2 | async-start | bytes 1310720 | tf_op jit(solution)/shard_map/all_to_all | solution.py:88
Sparse Core Ops, SparseCore 0:
  113.3 240.2 all-reduce.5
where the time goes:
time: 365 us; the launch traced here: 364 us
  waiting for transfers between devices  163 us (45%)
  blocking collectives  72.1 us (20%)
  matrix products  50.4 us (14%)
  local copies, waits for them, and re-layouts  36.5 us (10%)
  starting transfers between devices  15.4 us (4%)
  between operations  14.2 us (4%)
  other arithmetic  12.5 us (3%)
    unnamed x2, waiting for transfers between devices  152 us
    unnamed x1, blocking collectives  72.1 us
    dot_general x5, matrix products, contract(): return jnp.einsum(form, left, right, preferred_element_type=jnp.float32)  17.1 us
    unnamed x36, local copies, waits for them, and re-layouts  8.3 us
    dot_general x1, matrix products, on_device(): lax.dot_general(flat_norm, stacked, (((0,), (0,)), ((), ())), preferred_e...  8.18 us
    all_to_all x1, waiting for transfers between devices, on_device(): lax.all_to_all(activations, 'tm', split_axis=2, concat_axis=1, tiled=True)  7.96 us
    dot_general x1, matrix products, on_device(): jnp.dot(flat_norm, qkv_weight, preferred_element_type=jnp.float32)  7.75 us
  transfers between devices with their start and end apart: 4, of which 3 were waited for; matrix products, arithmetic and copies ran while one was open for 5% of the time, Pallas kernels for 0%

commit v1 on v0

v1 whole, which is shorter than its diff:
```python
import functools
import math

import jax
import jax.numpy as jnp
from jax import lax
from jax.experimental import pallas as pl
from jax.experimental.pallas import tpu as pltpu
from jax.sharding import Mesh, PartitionSpec as P

D = 1280
HEADS = 16
HEAD = 80
HALF = 640
TOKENS = 256
INVERSE_ROOT = 1.0 / math.sqrt(HEAD)
FACTOR = 1.0 / math.sqrt(32 * 1024)
BF16, F32 = jnp.bfloat16, jnp.float32
ORDER_A = (("z", "y", "x"), ("y", "x", "z"))
ORDER_B = (("x", "y", "z"), ("x", "y", "z"))
WIDTH_A, WIDTH_B = 1920, 768
NN = (((1,), (0,)), ((), ()))
NT = (((1,), (1,)), ((), ()))
TN = (((0,), (0,)), ((), ()))


def dot(left, right, dims=NN):
    return lax.dot_general(left, right, dims, preferred_element_type=F32)


def call(body, outs, operands, scalars=0, flops=0, scratch=(), after=None, results=pltpu.VMEM,
         hbm=(), last=False):
    vmem = pl.BlockSpec(memory_space=pltpu.VMEM)
    smem = pl.BlockSpec(memory_space=pltpu.SMEM)
    count, tokens = len(operands), [] if last else [pltpu.VMEM((8, 128), F32)]
    size = sum(math.prod(o.shape) * o.dtype.itemsize for o in list(operands) + list(outs))
    given = list(operands) + ([] if after is None else list(after))
    spaces = [smem] * scalars + [vmem] * (len(given) - scalars)
    placed = [
        value if place < scalars else pltpu.with_memory_space_constraint(value, pltpu.VMEM)
        for place, value in enumerate(given)
    ]
    for place in hbm:
        spaces[place] = pl.BlockSpec(memory_space=pl.ANY)
        placed[place] = from_hbm(given[place])

    def run(*refs):
        results, rest = refs[len(placed):len(placed) + len(outs)], refs[len(placed) + len(outs):]
        if not last:
            rest[0][...] = jnp.zeros((8, 128), F32)
            rest = rest[1:]
        body(*refs[:count], *results, *rest)

    given = pl.pallas_call(
        run,
        out_shape=[results(o.shape, o.dtype) for o in outs] + tokens,
        in_specs=spaces,
        out_specs=[vmem] * (len(outs) + len(tokens)),
        scratch_shapes=scratch,
        compiler_params=pltpu.CompilerParams(vmem_limit_bytes=16 * 2**20),
        cost_estimate=pl.CostEstimate(
            flops=flops, bytes_accessed=size // 4 if flops else 1, transcendentals=0
        ),
    )(*placed)
    return list(given[:len(outs)]), list(given[len(outs):])


def late(value, after):
    vmem, anywhere = pl.BlockSpec(memory_space=pltpu.VMEM), pl.BlockSpec(memory_space=pl.ANY)

    def body(*refs):
        refs[-1][...] = jnp.zeros((8, 128), F32)

    value, token = pl.pallas_call(
        body,
        out_shape=[jax.ShapeDtypeStruct(value.shape, value.dtype), pltpu.VMEM((8, 128), F32)],
        in_specs=[anywhere] + [vmem] * len(after), out_specs=[anywhere, vmem],
        input_output_aliases={0: 0},
        compiler_params=pltpu.CompilerParams(vmem_limit_bytes=2**20),
        cost_estimate=pl.CostEstimate(flops=10**7, bytes_accessed=1, transcendentals=0),
    )(value, *[pltpu.with_memory_space_constraint(array, pltpu.VMEM) for array in after])
    return value, [token]


def from_hbm(value):
    return pltpu.with_memory_space_constraint(value, pltpu.HBM)


def shape(rows, columns, kind=BF16):
    return jax.ShapeDtypeStruct((rows, columns), kind)


def side(both_ref, which, columns=slice(None)):
    value = both_ref[:, 32 * which:32 * which + 32, columns]
    return value.reshape(TOKENS, value.shape[-1])


def normalize(both_ref):
    x_wide = side(both_ref, 0).astype(F32)
    centred = x_wide - jnp.mean(x_wide, axis=-1, keepdims=True)
    variance = jnp.mean(centred * centred, axis=-1, keepdims=True)
    inv_std = lax.rsqrt(variance + 1e-06)
    return centred * inv_std, inv_std


def half(place_ref, own):
    core = place_ref[3] if own else 1 - place_ref[3]
    return pl.ds(pl.multiple_of(core * HALF, 128), HALF)


def forward_body(place_ref, both_ref, gain_ref, weight_ref, gained_ref, qkv_ref, cot_ref,
                 held_ref, sems):
    pieces = [slice(step * HALF, (step + 1) * HALF) for step in range(6)]
    copies = [
        pltpu.make_async_copy(weight_ref.at[:, piece], held_ref.at[:, piece], sems.at[step])
        for step, piece in enumerate(pieces)
    ]
    for copy in copies[:2]:
        copy.start()
    normalized, _ = normalize(both_ref)
    gained = (normalized * gain_ref[...]).astype(BF16)
    gained_ref[...] = gained
    cot_ref[...] = side(both_ref, 1, half(place_ref, False))
    for step, (copy, piece) in enumerate(zip(copies, pieces)):
        copy.wait()
        if step + 2 < len(copies):
            copies[step + 2].start()
        qkv_ref[:, piece] = dot(gained, held_ref[:, piece]).astype(BF16)


def attention_body(group_ref, qkv_ref, both_ref, weight_ref, att_ref, stack_ref, ag_ref,
                   bias_ref):
    start = pl.multiple_of(group_ref[0] * HALF, 128)
    ag_ref[...] = dot(side(both_ref, 1), weight_ref[pl.ds(start, HALF), :], NT).astype(BF16)
    row = lax.broadcasted_iota(jnp.int32, (TOKENS, TOKENS), 0)
    column = lax.broadcasted_iota(jnp.int32, (TOKENS, TOKENS), 1)
    bias_ref[...] = jnp.where((row & 7) == (column & 7), 0.0, -1e30)
    tiles = [[[] for _ in range(5)] for _ in range(4)]
    for head in range(8):
        low, high = head * HEAD, (head + 1) * HEAD
        first, last = low // 128 * 128, -(-high // 128) * 128
        width = last - first
        lanes = lax.broadcasted_iota(jnp.int32, (1, width), 1) + first
        keep = jnp.where((lanes >= low) & (lanes < high), 1.0, 0.0).astype(BF16)

        def cut(part):
            return qkv_ref[:, pl.ds(pl.multiple_of(start + part * D + first, 128), width)] * keep

        query, key, value = cut(0), cut(1), cut(2)
        grad = ag_ref[:, first:last] * keep
        scores = dot(key, query, NT) + bias_ref[...]
        shifted = jnp.exp((scores - jnp.max(scores, axis=0, keepdims=True)) * INVERSE_ROOT)
        prob = shifted * (1.0 / jnp.sum(shifted, axis=0, keepdims=True))
        prob_low = prob.astype(BF16)
        prob_grad = dot(value, grad, NT)
        mixed = jnp.sum(prob_grad * prob, axis=0, keepdims=True)
        score_grad = (prob * (prob_grad - mixed) * INVERSE_ROOT).astype(BF16)
        results = (
            dot(prob_low, value, TN), dot(score_grad, key, TN), dot(score_grad, query),
            dot(prob_low, grad),
        )
        for kind, result in enumerate(results):
            for tile in range(width // 128):
                piece = result[:, tile * 128:(tile + 1) * 128]
                tiles[kind][first // 128 + tile].append(piece)
    for kind in range(4):
        for tile in range(5):
            total = sum(tiles[kind][tile][1:], tiles[kind][tile][0]).astype(BF16)
            if kind == 0:
                att_ref[:, tile * 128:(tile + 1) * 128] = total
            else:
                at = (kind - 1) * HALF + tile * 128
                stack_ref[:, at:at + 128] = total


def input_grad_body(place_ref, both_ref, gain_ref, weight_ref, mine_ref, other_ref, pick_ref,
                    grad_ref, keep, give, joined_ref):
    for own, stack_ref in ((True, mine_ref), (False, other_ref)):
        group = place_ref[3] if own else 1 - place_ref[3]
        for part in range(3):
            columns = pl.ds(pl.multiple_of(group * HALF + part * D, 128), HALF)
            joined_ref[:, columns] = stack_ref[:, part * HALF:(part + 1) * HALF]
    normed_grad = dot(joined_ref[...], weight_ref[...], NT)
    normalized, inv_std = normalize(both_ref)
    scaled = normed_grad * gain_ref[...]
    inner = scaled - jnp.mean(scaled, axis=-1, keepdims=True)
    inner -= normalized * jnp.mean(scaled * normalized, axis=-1, keepdims=True)
    grad_ref[...] = (side(both_ref, 1).astype(F32) + inv_std * inner).astype(BF16)
    gain = jnp.sum(normed_grad * normalized, axis=0, keepdims=True)
    high = gain.astype(BF16).astype(F32)
    middle = (gain - high).astype(BF16).astype(F32)
    row = lax.broadcasted_iota(jnp.int32, (16, D), 0)
    split = jnp.where(row == 2, gain - high - middle, 0.0)
    split = jnp.where(row == 0, high, jnp.where(row == 1, middle, split)).astype(BF16)
    blocks = []
    for block in range(4):
        rows = slice(block * 320, (block + 1) * 320)
        ordered = jnp.sum(dot(split, pick_ref[rows, :], NT), axis=0, keepdims=True)
        blocks.append(jnp.concatenate([ordered, jnp.zeros((1, 64), F32)], axis=1))
    even = (place_ref[1] & 1) == 0
    near = jnp.where(even, blocks[1], blocks[3])
    far = jnp.where(even, blocks[3], blocks[1])
    rest = jnp.zeros((6, 384), F32)
    keep[...] = jnp.concatenate([blocks[0], near, rest], axis=0)
    give[...] = jnp.concatenate([blocks[2], far, rest], axis=0)


def gain_body(keep, arrived, own, give):
    total = keep[...] + arrived[...]
    own[...] = total
    give[...] = jnp.concatenate([total[1:8], total[0:1]], axis=0)


def pick(source):
    lanes = lax.broadcasted_iota(jnp.int32, (source.shape[0], D), 1)
    return jnp.where(lanes == source, 1.0, 0.0).astype(BF16)


def relative_rows(place_ref, order, block):
    here = {"z": place_ref[0], "x": place_ref[1], "y": place_ref[2]}
    on_first = place_ref[3] == 0
    row = lax.broadcasted_iota(jnp.int32, (320, 1), 0)

    def count(value, size):
        return sum(jnp.where(value >= size * step, 1, 0) for step in (1, 2, 3))

    def offset(axis, at):
        if axis == "x":
            return (at & 1) * 160 + (at >> 1) * 80
        return at * (320 if axis == "z" else 20)

    second = count(row, 80)
    row = row - 80 * second
    third = count(row, 20)
    row = row - 20 * third
    for level, step in enumerate((block, second, third)):
        one, two = (
            offset(axes[level], (here[axes[level]] + step) & 3) for axes in order
        )
        row = row + jnp.where(on_first, one, two)
    return row


def ready_body(place_ref, pick_a, pick_b, pick_att, token):
    token[...] = jnp.zeros((8, 128), F32)
    for step in range(4):
        rows = slice(step * 320, (step + 1) * 320)
        pick_a[rows, :] = pick(relative_rows(place_ref, ORDER_A, step))
        feature = relative_rows(place_ref, ORDER_B, step)
        pick_b[rows, :] = pick(feature)
        feature = feature + place_ref[3] * HALF
        pick_att[rows, :] = pick(jnp.where(feature >= D, feature - D, feature))


def gained_body(pick_ref, own_ref, partner_ref, out):
    for step in range(4):
        rows = slice(step * 320, (step + 1) * 320)
        out[rows, :TOKENS] = dot(pick_ref[rows, :], own_ref[...], NT).astype(BF16)
        out[rows, TOKENS:] = dot(pick_ref[rows, :], partner_ref[...], NT).astype(BF16)


def turn_body(pick_att, mine, other, their_mine, their_other, att_out):
    sides = ((mine, other), (their_other, their_mine))
    for step in range(4):
        rows = slice(step * 320, (step + 1) * 320)
        for which, (first, second) in enumerate(sides):
            turned = dot(pick_att[rows, :HALF], first[...], NT)
            turned += dot(pick_att[rows, HALF:], second[...], NT)
            att_out[rows, which * TOKENS:(which + 1) * TOKENS] = turned.astype(BF16)


def term_a(rows, gained, stack, their_stack):
    return dot(gained[rows, :TOKENS], stack[...]) + dot(gained[rows, TOKENS:], their_stack[...])


def term_b(rows, place_ref, both, their_cot, att):
    outer = dot(att[rows, :TOKENS], side(both, 1, half(place_ref, True)))
    return outer + dot(att[rows, TOKENS:], their_cot[...])


def early_body(term, count, *refs):
    plus, minus = refs[count:]
    far = term(slice(640, 960), *refs[:count])
    plus[0:160, :] = far[0:160].astype(BF16)
    minus[0:160, :] = far[160:320].astype(BF16)
    plus[160:320, :] = term(slice(480, 640), *refs[:count]).astype(BF16)
    minus[160:320, :] = term(slice(960, 1120), *refs[:count]).astype(BF16)


def relay_body(term, count, *refs):
    from_minus, from_plus, plus, minus = refs[count:]
    up = term(slice(320, 480), *refs[:count]) + from_minus[0:160, :].astype(F32)
    down = term(slice(1120, 1280), *refs[:count]) + from_plus[0:160, :].astype(F32)
    plus[...] = up.astype(BF16)
    minus[...] = down.astype(BF16)


def own_body(term, count, *refs):
    from_minus, from_plus, own = refs[count:]
    total = term(slice(0, 320), *refs[:count])
    own[0:160, :] = total[0:160] + from_plus[160:320, :].astype(F32)
    own[160:320, :] = total[160:320] + from_minus[160:320, :].astype(F32)


def second_early_body(own, from_minus, from_plus, *refs):
    gains, (rest, plus, minus) = refs[:-3], refs[-3:]
    upper = own[0:160, :] + from_minus[...].astype(F32)
    lower = own[160:320, :] + from_plus[...].astype(F32)
    if gains:
        line = gains[0][0:1, :] + gains[1][0:1, :]
        row = lax.broadcasted_iota(jnp.int32, (320, 384), 0)
        lane = lax.broadcasted_iota(jnp.int32, (320, 384), 1)
        column = jnp.sum(jnp.where(row == lane, line, 0.0), axis=-1, keepdims=True)
        column = jnp.where(lane[:, :128] == 0, column, 0.0)
        upper = jnp.concatenate([upper, column[0:160]], axis=1)
        lower = jnp.concatenate([lower, column[160:320]], axis=1)
    rest[0:120, :] = upper[0:120]
    plus[40:80, :] = upper[120:160]
    plus[0:40, :] = lower[0:40]
    minus[0:80, :] = lower[40:120]
    rest[120:160, :] = lower[120:160]


def second_relay_body(rest, from_minus, from_plus, plus, minus, part):
    plus[...] = rest[80:120, :] + from_minus[0:40, :]
    minus[...] = rest[120:160, :] + from_plus[0:40, :]
    part[0:40, :] = rest[0:40, :] + from_plus[40:80, :]
    part[40:80, :] = rest[40:80, :] + from_minus[40:80, :]


def third_body(part, last_minus, last_plus, own, one, two, three):
    upper = part[0:40, :] + last_minus[...]
    lower = part[40:80, :] + last_plus[...]
    own[...] = upper[0:20]
    one[...] = upper[20:40]
    two[...] = lower[0:20]
    three[...] = lower[20:40]


def final_body(place_ref, *refs):
    on_first = place_ref[3] == 0
    blocks, outs = refs[:8], refs[8:]
    for first, columns in ((0, slice(0, WIDTH_A)), (4, slice(WIDTH_A, WIDTH_A + WIDTH_B))):
        total = blocks[first][...]
        for other in range(1, 4):
            total += blocks[first + other][...]
        low, high = total[0:10], total[10:20]
        outs[0][:, columns] = jnp.where(on_first, low, high)
        outs[1][:, columns] = jnp.where(on_first, high, low)


def assemble_body(place_ref, here, theirs, qkv_ref, out_ref, gain_ref):
    first = place_ref[3] == 0
    left = jnp.where(first, here[...], theirs[...]) * FACTOR
    right = jnp.where(first, theirs[...], here[...]) * FACTOR
    for which, value in enumerate((left, right)):
        out_ref[:, which * HALF:(which + 1) * HALF] = value[:, WIDTH_A:WIDTH_A + HALF]
        for part in range(3):
            at = part * D + which * HALF
            qkv_ref[:, at:at + HALF] = value[:, part * HALF:(part + 1) * HALF]
    both = left[:, WIDTH_A + HALF:] + right[:, WIDTH_A + HALF:]
    column = jnp.sum(both, axis=-1, keepdims=True)
    row = lax.broadcasted_iota(jnp.int32, (10, 10), 0)
    lane = lax.broadcasted_iota(jnp.int32, (10, 10), 1)
    gain_ref[...] = jnp.sum(jnp.where(row == lane, column, 0.0), axis=0, keepdims=True)


def send(value, order, level, step):
    pairs = []
    for source in range(128):
        spots = {
            "z": source // 32, "x": source // 16 % 2 + source // 8 % 2 * 2, "y": source // 2 % 4
        }
        axis = order[source % 2][level]
        spots[axis] = (spots[axis] + step) % 4
        column = spots["x"] % 2 * 2 + spots["x"] // 2
        target = ((spots["z"] * 4 + column) * 4 + spots["y"]) * 2 + source % 2
        pairs.append((source, target))
    return lax.ppermute(value, ("z", "xl", "xh", "y", "c"), pairs)


def swap(value):
    return lax.ppermute(value, "c", [(0, 1), (1, 0)])


def split_body(x_ref, cot_ref, out_ref, sems):
    copies = [
        pltpu.make_async_copy(value.at[frame], out_ref.at[:, which, frame], sems.at[which, frame])
        for which, value in enumerate((x_ref, cot_ref))
        for frame in range(4)
    ]
    for copy in copies:
        copy.start()
    for copy in copies:
        copy.wait()


def join_body(value_ref, after_ref, out_ref, token_ref, sems):
    copies = [
        pltpu.make_async_copy(value_ref.at[:, frame], out_ref.at[frame], sems.at[frame])
        for frame in range(4)
    ]
    for copy in copies:
        copy.start()
    token_ref[...] = after_ref[...]
    for copy in copies:
        copy.wait()


def on_device(activations, grad_out, norm_gain, qkv_weight, out_weight):
    anywhere = pl.BlockSpec(memory_space=pl.ANY)
    in_vmem = pl.BlockSpec(memory_space=pltpu.VMEM)
    params = pltpu.CompilerParams(vmem_limit_bytes=16 * 2**20)
    x_place = lax.axis_index("xh") * 2 + lax.axis_index("xl")
    place = jnp.stack([lax.axis_index("z"), x_place, lax.axis_index("y"), lax.axis_index("c")])
    place = place.astype(jnp.int32)
    group = place[3:]
    gain_row = norm_gain.reshape(1, D)
    both = pl.pallas_call(
        split_body, out_shape=pltpu.VMEM((8, 2, 4, 8, D), BF16), in_specs=[anywhere] * 2,
        out_specs=in_vmem, scratch_shapes=[pltpu.SemaphoreType.DMA((2, 4))],
        compiler_params=params,
    )(from_hbm(activations.reshape(4, 8, 8, D)), from_hbm(grad_out.reshape(4, 8, 8, D)))
    pick_a, pick_b, pick_att, token = pl.pallas_call(
        ready_body, out_shape=[pltpu.HBM((D, D), BF16)] * 3 + [shape(8, 128, F32)],
        in_specs=[pl.BlockSpec(memory_space=pltpu.SMEM)], out_specs=[in_vmem] * 4,
        compiler_params=params,
        cost_estimate=pl.CostEstimate(flops=10**9, bytes_accessed=2 * 10**7, transcendentals=0),
    )(place)
    both = lax.all_to_all(both, ("z", "xl"), split_axis=0, concat_axis=0, tiled=True)
    both = both.reshape(8, 64, D)
    (gained, qkv, cot_other, weight), token = call(
        forward_body,
        [shape(TOKENS, D), shape(TOKENS, 3 * D), shape(TOKENS, HALF), shape(D, 3 * D)],
        [place, both, gain_row, qkv_weight], scalars=1, flops=2 * TOKENS * D * 3 * D,
        scratch=[pltpu.SemaphoreType.DMA((6,))], hbm=(3,), after=[token],
    )
    their_gained, their_cot = swap(gained), swap(cot_other)

    def attention(which, after):
        return call(
            attention_body, [shape(TOKENS, HALF), shape(TOKENS, 3 * HALF)],
            [which, qkv, both, out_weight], scalars=1, flops=5 * 10**9,
            scratch=[pltpu.VMEM((TOKENS, HALF), BF16), pltpu.VMEM((TOKENS, TOKENS), F32)],
            after=after,
        )

    (att_other, stack_other), token = attention(1 - group, token)
    their_stack, their_other = swap(stack_other), swap(att_other)
    (att_mine, stack), token = attention(group, token)
    their_mine = swap(att_mine)
    (gained_a,), token = call(
        gained_body, [shape(D, 512)], [pick_a, gained, their_gained], flops=2 * D * D * 512,
        after=token,
    )
    work = {"a": 10**7, "b": 15 * 10**8, "b second": 8 * 10**9}
    base = {"a": [gained_a, stack, their_stack]}
    kinds = {"a": (term_a, 0, WIDTH_A, ORDER_A), "b": (term_b, 1, HALF, ORDER_B)}

    def run(which, body, outs, extra, after):
        term, scalars, _, _ = kinds[which]
        return call(
            functools.partial(body, term, len(base[which])), outs, base[which] + extra,
            scalars=scalars, flops=work[which], after=after,
        )

    def exchange(which, sent, level):
        order = kinds[which][3]
        return [send(sent[0], order, level, 1), send(sent[1], order, level, 3)]

    state = {}

    def early(which, after):
        sent, after = run(which, early_body, [shape(320, kinds[which][2])] * 2, [], after)
        state[which] = exchange(which, sent, 0)
        return after

    def relay(which, after):
        width, first = kinds[which][2], state[which]
        sent, after = run(which, relay_body, [shape(160, width)] * 2, first, after)
        state[which] = (first, exchange(which, sent, 0))
        return after

    def own_rows(which, after):
        first, second = state[which]
        outs = [shape(320, kinds[which][2], F32)]
        own, after = run(which, own_body, outs, first, after)
        state[which] = own + second
        return after

    gains = {"a": [], "b": []}

    def second_early(which, after):
        width = kinds[which][2] + (128 if gains[which] else 0)
        outs = [shape(rows, width, F32) for rows in (160, 80, 80)]
        (rest, *sent), after = call(
            second_early_body, outs, state[which] + gains[which], after=after,
            flops=work["b second" if which == "b" else "a"],
        )
        state[which] = [rest] + exchange(which, sent, 1)
        return after

    def second_relay(which, after):
        width = state[which][0].shape[1]
        outs = [shape(40, width, F32)] * 2 + [shape(80, width, F32)]
        (plus, minus, part), after = call(
            second_relay_body, outs, state[which], flops=work[which], after=after
        )
        state[which] = [part] + exchange(which, (plus, minus), 1)
        return after

    def third(which, after):
        outs = [shape(20, state[which][0].shape[1], F32)] * 4
        (own, *others), after = call(
            third_body, outs, state[which], flops=10**6, after=after
        )
        order = kinds[which][3]
        sent = [send(other, order, 2, step + 1) for step, other in enumerate(others)]
        state[which] = [own] + sent
        return after

    token = early("a", token)
    (att,), token = call(
        turn_body, [shape(D, 512)], [pick_att, att_mine, att_other, their_mine, their_other],
        after=token,
    )
    base["b"] = [place, both, their_cot, att]
    token = early("b", token)
    (grad_here, keep, give), token = call(
        input_grad_body, [shape(TOKENS, D)] + [shape(8, 384, F32)] * 2,
        [place, both, gain_row, weight, stack, stack_other, pick_b], scalars=1, after=token,
        scratch=[pltpu.VMEM((TOKENS, 3 * D), BF16)],
    )
    arrived = lax.ppermute(give, "xh", [(0, 1), (1, 0)])
    token = own_rows("a", relay("a", token))
    token = relay("b", token + [arrived])
    (own, give), token = call(gain_body, [shape(8, 384, F32)] * 2, [keep, arrived], after=token)
    gains["b"] = [own, lax.ppermute(give, "xl", [(0, 1), (1, 0)])]
    token = own_rows("b", token)
    token = second_early("b", second_early("a", token))
    grad_here, token = late(grad_here, token)
    back = lax.all_to_all(
        grad_here.reshape(8, 4, 8, D), ("z", "xl"), split_axis=0, concat_axis=0, tiled=True
    )
    token = second_relay("b", second_relay("a", token))
    token = third("b", third("a", token))
    grad_tokens, token = pl.pallas_call(
        join_body,
        out_shape=[jax.ShapeDtypeStruct((4, 8, 8, D), BF16), pltpu.VMEM((8, 128), F32)],
        in_specs=[anywhere, in_vmem], out_specs=[anywhere, in_vmem],
        scratch_shapes=[pltpu.SemaphoreType.DMA((4,))], compiler_params=params,
        cost_estimate=pl.CostEstimate(flops=10**7, bytes_accessed=1, transcendentals=0),
    )(back, pltpu.with_memory_space_constraint(token[0], pltpu.VMEM))
    (here, other), token = call(
        final_body, [shape(10, WIDTH_A + WIDTH_B, F32)] * 2, [place] + state["a"] + state["b"],
        scalars=1, after=[token],
    )
    theirs = swap(other)
    (qkv_grad, out_grad, gain_grad), _ = call(
        assemble_body, [shape(10, 3 * D, F32), shape(10, D, F32), shape(1, 10, F32)],
        [place, here, theirs], scalars=1, results=jax.ShapeDtypeStruct, last=True,
        after=token,
    )
    return (grad_tokens.reshape(1, 4, 64, D), qkv_grad, out_grad, gain_grad.reshape(10))


def solution(mesh):
    fine = Mesh(mesh.devices.reshape(4, 2, 2, 4, 2), ("z", "xl", "xh", "y", "c"))
    tm, space = ("z", "xl"), ("xh", "y", "c")
    tokens = P(None, tm, space, None)
    in_specs = (tokens, tokens, P(), P(), P())
    out_specs = (tokens, P(tm + space, None), P(tm + space, None), P(tm + space))
    return jax.shard_map(
        on_device, mesh=fine, in_specs=in_specs, out_specs=out_specs, check_vma=False
    )
```

time: 365 us -> 122 us (0.33)
  waiting for transfers between devices: 163 us -> 23.5 us
  blocking collectives: 72.1 us -> 0 us
  matrix products: 50.4 us -> 0 us
  Pallas kernels: 0 us -> 46.2 us
  local copies, waits for them, and re-layouts: 36.5 us -> 0.04 us
  starting transfers between devices: 15.4 us -> 51.2 us
  between operations: 14.2 us -> 0.91 us
  other arithmetic: 12.5 us -> 0.08 us
    unnamed x2 -> x0, waiting for transfers between devices: 152 us -> none
    unnamed x1 -> x0, blocking collectives: 72.1 us -> none
    pallas_call x0 -> x25, Pallas kernels: none -> 46.2 us  [the longest x21 36.3 us: call(): pl.pallas_call(run, out_shape=[results(o.shape, o.dtype) for o in outs] +...]
    dot_general x10 -> x0, matrix products: 45.6 us -> none  [the longest x5 17.1 us: contract(): return jnp.einsum(form, left, right, preferred_element_type=jnp.float32)]
    ppermute x0 -> x30, starting transfers between devices: none -> 40.8 us  [the longest x22 28.9 us: send(): return lax.ppermute(value, ('z', 'xl', 'xh', 'y', 'c'), pairs)]
    reshape x3 -> x1, local copies, waits for them, and re-layouts: 13.7 us -> 0.01 us  [on_device(): gain_row = norm_gain.reshape(1, D)]
    ppermute x0 -> x30, waiting for transfers between devices: none -> 12.4 us  [the longest x22 9.43 us: send(): return lax.ppermute(value, ('z', 'xl', 'xh', 'y', 'c'), pairs)]
    unnamed x36 -> x14, local copies, waits for them, and re-layouts: 8.3 us -> 0.03 us
  transfers between devices with their start and end apart: 4 -> 32, of which waited for: 3 -> 12; matrix products, arithmetic and copies ran while one was open for 5% -> 0% of each run, Pallas kernels for 0% -> 24%
where the time goes in v1:
time: 122 us
  starting transfers between devices  51.2 us (42%)
  Pallas kernels  46.2 us (38%)
  waiting for transfers between devices  23.5 us (19%)
    pallas_call x21, Pallas kernels, call(): pl.pallas_call(run, out_shape=[results(o.shape, o.dtype) for o in outs] +...  36.3 us
    ppermute x22, starting transfers between devices, send(): return lax.ppermute(value, ('z', 'xl', 'xh', 'y', 'c'), pairs)  28.9 us
    all_to_all x1, waiting for transfers between devices, on_device(): lax.all_to_all(both, ('z', 'xl'), split_axis=0, concat_axis=0, tiled=True)  11.1 us
    ppermute x6, starting transfers between devices, swap(): return lax.ppermute(value, 'c', [(0, 1), (1, 0)])  9.48 us
    ppermute x22, waiting for transfers between devices, send(): return lax.ppermute(value, ('z', 'xl', 'xh', 'y', 'c'), pairs)  9.43 us
    all_to_all x1, starting transfers between devices, on_device(): lax.all_to_all(both, ('z', 'xl'), split_axis=0, concat_axis=0, tiled=True)  6.8 us
    pallas_call x1, Pallas kernels, on_device(): pl.pallas_call(ready_body, out_shape=[pltpu.HBM((D, D), BF16)] * 3 + [sha...  6.42 us
    all_to_all x1, starting transfers between devices, on_device(): lax.all_to_all(grad_here.reshape(8, 4, 8, D), ('z', 'xl'), split_axis=0,...  3.54 us
  transfers between devices with their start and end apart: 32, of which 12 were waited for; matrix products, arithmetic and copies ran while one was open for 0% of the time, Pallas kernels for 24%

profile of v1, /device:TPU:1, one launch (start us, length us, event | category | flops | bytes accessed | tf_op | source)
XLA Modules:
  0.0 121.9 jit_solution(482188696273565646)
XLA Ops:
  0.6 2.5 %shard_map.84 = bf16[8,2,4,8,1280]{4,3,2,1,0:T(8,128)(2,1)} custom-call(bf16[4,8,8,1280]{3,2,1,0:T(8,128)(2,1)} %bitcast.17, bf16[4,8,8,1280]{3,2,1,0:T(8,128)(2,1)} %bitcast.18), custom_call_target="tpu_custom_call" | custom-call | tf_op jit(solution)/shard_map/pallas_call | solution.py:419
  3.2 6.8 %all-to-all-start = ((bf16[8,2,4,8,1280]{4,3,2,1,0:T(8,128)(2,1)}), bf16[8,2,4,8,1280]{4,3,2,1,0:T(8,128)(2,1)S(1)}, u32[]{:S(2)}, u32[]{:S(2)}) async-start(bf16[8,2,4,8,1280]{4,3,2,1,0:T(8,128)(2,1)} %shard_map.84), calls=%async_computation | async-start | bytes 2621440 | tf_op jit(solution)/shard_map/all_to_all | solution.py:430
  10.0 0.1 pad_add_fusion.place_ref.refs_0_
  10.1 6.4 %shard_map.85 = (bf16[1280,1280]{1,0:T(8,128)(2,1)}, bf16[1280,1280]{1,0:T(8,128)(2,1)}, bf16[1280,1280]{1,0:T(8,128)(2,1)}, f32[8,128]{1,0:T(8,128)S(1)}) custom-call(s32[4]{0:T(128)S(1)} %pad_add_fusion.place_ref.refs_0_), custom_call_target="tpu_custom_call" | custom-call | flops 1000000000 | bytes 20000000 | tf_op jit(solution)/shard_map/pallas_call | solution.py:424
  16.5 11.1 %all-to-all-done = bf16[8,2,4,8,1280]{4,3,2,1,0:T(8,128)(2,1)S(1)} async-done(((bf16[8,2,4,8,1280]{4,3,2,1,0:T(8,128)(2,1)}), bf16[8,2,4,8,1280]{4,3,2,1,0:T(8,128)(2,1)S(1)}, u32[]{:S(2)}, u32[]{:S(2)}) %all-to-all-start) | async-done | bytes 1310752 | tf_op jit(solution)/shard_map/all_to_all | solution.py:430
  27.6 6.8 %shard_map.86 = (bf16[256,1280]{1,0:T(8,128)(2,1)S(1)}, bf16[256,3840]{1,0:T(8,128)(2,1)S(1)}, bf16[256,640]{1,0:T(8,128)(2,1)S(1)}, bf16[1280,3840]{1,0:T(8,128)(2,1)S(1)}, f32[8,128]{1,0:T(8,128)S(1)}) custom-call(s32[4]{0:T(128)S(1)} %pad_add_fusion.place_ref.refs_0_, bf16[8,64,1280]{2,1,0:T(8,128)(2,1)S(1)} %bitcast.10, f32[1,1280]{1,0:T(1,128)S(1)} %reshape.32.refs_2_, ...), custom_call_target="tpu_custom_call" | custom-call | flops 2516582400 | bytes 5981444 | tf_op jit(solution)/shard_map/pallas_call | solution.py:54
  34.5 4.2 %shard_map.87 = (bf16[256,640]{1,0:T(8,128)(2,1)S(1)}, bf16[256,1920]{1,0:T(8,128)(2,1)S(1)}, f32[8,128]{1,0:T(8,128)S(1)}) custom-call(s32[1]{0:T(128)S(6)} %sub.3.refs_0_, bf16[256,3840]{1,0:T(8,128)(2,1)S(1)} %get-tuple-element.84.refs_1_, bf16[8,64,1280]{2,1,0:T(8,128)(2,1)S(1)} %bitcast.11, bf16[1280,1280]{1,0:T(8,128)(2,1)S(1)} %copy-done.2, ...), custom_call_target="tpu_custom_call" | custom-call | flops 5000000000 | bytes 1966081 | tf_op jit(solution)/shard_map/pallas_call | solution.py:54
  38.6 2.0 %collective-permute-start.4 = (bf16[256,1920]{1,0:T(8,128)(2,1)S(1)}, bf16[256,1920]{1,0:T(8,128)(2,1)S(1)}, u32[]{:S(2)}, u32[]{:S(2)}) collective-permute-start(bf16[256,1920]{1,0:T(8,128)(2,1)S(1)} %get-tuple-element.88.refs_5_), channel_id=1, source_target_pairs={{0,1},{1,0},{2,3},{3,2},{4,5},{5,4},{6,7},{7,6},{8,9},{9,8},{10,11... | collective-permute-start | bytes 2949128 | tf_op jit(solution)/shard_map/ppermute | solution.py:383
  40.6 0.3 collective-permute-start.3
  40.9 4.2 %shard_map.88 = (bf16[256,640]{1,0:T(8,128)(2,1)S(1)}, bf16[256,1920]{1,0:T(8,128)(2,1)S(1)}, f32[8,128]{1,0:T(8,128)S(1)}) custom-call(s32[1]{0:T(128)} %bitcast.3.refs_0_, bf16[256,3840]{1,0:T(8,128)(2,1)S(1)} %get-tuple-element.84.refs_1_, bf16[8,64,1280]{2,1,0:T(8,128)(2,1)S(1)} %bitcast.12, bf16[1280,1280]{1,0:T(8,128)(2,1)S(1)} %copy-done.2, ...), custom_call_target="tpu_custom_call" | custom-call | flops 5000000000 | bytes 1966081 | tf_op jit(solution)/shard_map/pallas_call | solution.py:54
  45.1 1.9 %shard_map.89 = (bf16[1280,512]{1,0:T(8,128)(2,1)S(1)}, f32[8,128]{1,0:T(8,128)S(1)}) custom-call(bf16[1280,1280]{1,0:T(8,128)(2,1)S(1)} %copy-done.3, bf16[256,1280]{1,0:T(8,128)(2,1)S(1)} %get-tuple-element.95.refs_1_, bf16[256,1280]{1,0:T(8,128)(2,1)S(1)} %collective-permute-done.3.refs_2_, f32[8,128]{1,0:T(8,128)S(1)} %get-tuple-element.96.refs_3_), custom_call_target="tpu_custom_call" | custom-call | flops 1677721600 | bytes 1474560 | tf_op jit(solution)/shard_map/pallas_call | solution.py:54
  47.0 1.5 %shard_map.90 = (bf16[320,1920]{1,0:T(8,128)(2,1)S(1)}, bf16[320,1920]{1,0:T(8,128)(2,1)S(1)}, f32[8,128]{1,0:T(8,128)S(1)}) custom-call(bf16[1280,512]{1,0:T(8,128)(2,1)S(1)} %get-tuple-element.97.refs_0_, bf16[256,1920]{1,0:T(8,128)(2,1)S(1)} %get-tuple-element.87.refs_1_.refs_4_, bf16[256,1920]{1,0:T(8,128)(2,1)S(1)} %collective-permute-done.4.refs_2_, ...), custom_call_target="tpu_custom_call" | custom-call | flops 10000000 | bytes 1433600 | tf_op jit(solution)/shard_map/pallas_call | solution.py:54
  48.5 1.4 %collective-permute-start.8 = (bf16[320,1920]{1,0:T(8,128)(2,1)S(1)}, bf16[320,1920]{1,0:T(8,128)(2,1)S(1)}, u32[]{:S(2)}, u32[]{:S(2)}) collective-permute-start(bf16[320,1920]{1,0:T(8,128)(2,1)S(1)} %get-tuple-element.108), channel_id=1, source_target_pairs={{0,32},{1,3},{2,34},{3,5},{4,36},{5,7},{6,38},{7,1},{8,40},{9,11},... | collective-permute-start | bytes 3686408 | tf_op jit(solution)/shard_map/ppermute | solution.py:379
  49.9 1.5 %collective-permute-start.9 = (bf16[320,1920]{1,0:T(8,128)(2,1)S(1)}, bf16[320,1920]{1,0:T(8,128)(2,1)S(1)}, u32[]{:S(2)}, u32[]{:S(2)}) collective-permute-start(bf16[320,1920]{1,0:T(8,128)(2,1)S(1)} %get-tuple-element.109), channel_id=1, source_target_pairs={{0,96},{1,7},{2,98},{3,1},{4,100},{5,3},{6,102},{7,5},{8,104},{9,1... | collective-permute-start | bytes 3686408 | tf_op jit(solution)/shard_map/ppermute | solution.py:379
  51.4 0.7 collective-permute-start.1
  52.1 0.5 collective-permute-start
  52.6 0.7 collective-permute-done.1.refs_3_
  53.3 0.5 collective-permute-done.2.refs_4_
  53.8 2.2 %shard_map.91 = (bf16[1280,512]{1,0:T(8,128)(2,1)S(1)}, f32[8,128]{1,0:T(8,128)S(1)}) custom-call(bf16[1280,1280]{1,0:T(8,128)(2,1)S(1)} %copy-done, bf16[256,640]{1,0:T(8,128)(2,1)S(1)} %get-tuple-element.92.refs_1_, bf16[256,640]{1,0:T(8,128)(2,1)S(1)} %get-tuple-element.93.refs_2_, bf16[256,640]{1,0:T(8,128)(2,1)S(1)} %collective-permute-done.1.refs_3_, ...), custom_call_target="tpu_custom_call" | custom-call | bytes 1 | tf_op jit(solution)/shard_map/pallas_call | solution.py:54
  56.1 1.2 %shard_map.92 = (bf16[320,640]{1,0:T(8,128)(2,1)S(1)}, bf16[320,640]{1,0:T(8,128)(2,1)S(1)}, f32[8,128]{1,0:T(8,128)S(1)}) custom-call(s32[4]{0:T(128)S(1)} %pad_add_fusion.place_ref.refs_0_, bf16[8,64,1280]{2,1,0:T(8,128)(2,1)S(1)} %bitcast.13, bf16[256,640]{1,0:T(8,128)(2,1)S(1)} %collective-permute-done.refs_2_, ...), custom_call_target="tpu_custom_call" | custom-call | flops 1500000000 | bytes 942084 | tf_op jit(solution)/shard_map/pallas_call | solution.py:54
  57.3 0.6 collective-permute-start.5
  57.9 2.1 %collective-permute-start.6 = (bf16[320,640]{1,0:T(8,128)(2,1)S(1)}, bf16[320,640]{1,0:T(8,128)(2,1)S(1)}, u32[]{:S(2)}, u32[]{:S(2)}) collective-permute-start(bf16[320,640]{1,0:T(8,128)(2,1)S(1)} %get-tuple-element.105), channel_id=1, source_target_pairs={{0,24},{1,25},{2,26},{3,27},{4,28},{5,29},{6,30},{7,31},{8,16},{9,... | collective-permute-start | bytes 1228808 | tf_op jit(solution)/shard_map/ppermute | solution.py:379
  60.1 5.2 %shard_map.93 = (bf16[256,1280]{1,0:T(8,128)(2,1)}, f32[8,384]{1,0:T(8,128)S(1)}, f32[8,384]{1,0:T(8,128)S(1)}, f32[8,128]{1,0:T(8,128)S(1)}) custom-call(s32[4]{0:T(128)S(1)} %pad_add_fusion.place_ref.refs_0_, bf16[8,64,1280]{2,1,0:T(8,128)(2,1)S(1)} %bitcast.14, f32[1,1280]{1,0:T(1,128)S(1)} %reshape.32.refs_2_, ...), custom_call_target="tpu_custom_call" | custom-call | bytes 1 | tf_op jit(solution)/shard_map/pallas_call | solution.py:54
  65.2 0.5 collective-permute-done.8.refs_3_
  65.8 0.9 shard_map.94
  66.6 1.4 %collective-permute-start.13 = (bf16[160,1920]{1,0:T(8,128)(2,1)S(1)}, bf16[160,1920]{1,0:T(8,128)(2,1)S(1)}, u32[]{:S(2)}, u32[]{:S(2)}) collective-permute-start(bf16[160,1920]{1,0:T(8,128)(2,1)S(1)} %get-tuple-element.121), channel_id=1, source_target_pairs={{0,32},{1,3},{2,34},{3,5},{4,36},{5,7},{6,38},{7,1},{8,40},{9,11},... | collective-permute-start | bytes 1843208 | tf_op jit(solution)/shard_map/ppermute | solution.py:379
  68.0 1.5 %collective-permute-start.14 = (bf16[160,1920]{1,0:T(8,128)(2,1)S(1)}, bf16[160,1920]{1,0:T(8,128)(2,1)S(1)}, u32[]{:S(2)}, u32[]{:S(2)}) collective-permute-start(bf16[160,1920]{1,0:T(8,128)(2,1)S(1)} %get-tuple-element.122), channel_id=1, source_target_pairs={{0,96},{1,7},{2,98},{3,1},{4,100},{5,3},{6,102},{7,5},{8,104},{9,1... | collective-permute-start | bytes 1843208 | tf_op jit(solution)/shard_map/ppermute | solution.py:379
  69.5 2.5 %collective-permute-start.7 = (f32[8,384]{1,0:T(8,128)S(1)}, f32[8,384]{1,0:T(8,128)S(1)}, u32[]{:S(2)}, u32[]{:S(2)}) collective-permute-start(f32[8,384]{1,0:T(8,128)S(1)} %get-tuple-element.107), channel_id=1, source_target_pairs={{0,8},{8,0},{1,9},{9,1},{2,10},{10,2},{3,11},{11,3},{4,12},{12,4},... | collective-permute-start | bytes 36872 | tf_op jit(solution)/shard_map/ppermute | solution.py:534
  72.0 0.9 shard_map.95
  72.8 0.7 collective-permute-done.7.refs_7_.refs_1_
  73.6 1.0 shard_map.96
  74.6 0.9 collective-permute-start.10
  75.5 1.8 %collective-permute-start.11 = (bf16[160,640]{1,0:T(8,128)(2,1)S(1)}, bf16[160,640]{1,0:T(8,128)(2,1)S(1)}, u32[]{:S(2)}, u32[]{:S(2)}) collective-permute-start(bf16[160,640]{1,0:T(8,128)(2,1)S(1)} %get-tuple-element.117), channel_id=1, source_target_pairs={{0,24},{1,25},{2,26},{3,27},{4,28},{5,29},{6,30},{7,31},{8,16},{9,... | collective-permute-start | bytes 614408 | tf_op jit(solution)/shard_map/ppermute | solution.py:379
  77.3 1.0 shard_map.98
  78.3 1.3 %shard_map.99 = (f32[160,1920]{1,0:T(8,128)S(1)}, f32[80,1920]{1,0:T(8,128)}, f32[80,1920]{1,0:T(8,128)}, f32[8,128]{1,0:T(8,128)S(1)}) custom-call(f32[320,1920]{1,0:T(8,128)S(1)} %get-tuple-element.120.refs_0_, bf16[160,1920]{1,0:T(8,128)(2,1)S(1)} %collective-permute-done.13.refs_1_, bf16[160,1920]{1,0:T(8,128)(2,1)S(1)} %collective-permute-done.14.refs_2_, ...), custom_call_target="tpu_custom_call" | custom-call | flops 10000000 | bytes 1536000 | tf_op jit(solution)/shard_map/pallas_call | solution.py:54
  79.6 1.5 %collective-permute-start.17 = (f32[80,1920]{1,0:T(8,128)}, f32[80,1920]{1,0:T(8,128)S(1)}, u32[]{:S(2)}, u32[]{:S(2)}) collective-permute-start(f32[80,1920]{1,0:T(8,128)} %get-tuple-element.131), channel_id=1, source_target_pairs={{0,2},{1,17},{2,4},{3,19},{4,6},{5,21},{6,0},{7,23},{8,10},{9,25},... | collective-permute-start | bytes 1843208 | tf_op jit(solution)/shard_map/ppermute | solution.py:379
  81.1 1.2 collective-permute-start.18
  82.3 0.8 shard_map.100
  83.1 2.7 %collective-permute-start.16 = (f32[80,768]{1,0:T(8,128)S(1)}, f32[80,768]{1,0:T(8,128)}, u32[]{:S(2)}, u32[]{:S(2)}) collective-permute-start(f32[80,768]{1,0:T(8,128)S(1)} %get-tuple-element.129), channel_id=1, source_target_pairs={{0,6},{1,7},{2,0},{3,1},{4,2},{5,3},{6,4},{7,5},{8,14},{9,15},{10,... | collective-permute-start | bytes 737288 | tf_op jit(solution)/shard_map/ppermute | solution.py:379
  85.8 3.5 %all-to-all-start.1 = ((bf16[8,4,8,1280]{3,2,1,0:T(8,128)(2,1)}), bf16[8,4,8,1280]{3,2,1,0:T(8,128)(2,1)S(1)}, u32[]{:S(2)}, u32[]{:S(2)}) async-start(bf16[8,4,8,1280]{3,2,1,0:T(8,128)(2,1)} %bitcast.7), calls=%async_computation.1 | async-start | bytes 1310720 | tf_op jit(solution)/shard_map/all_to_all | solution.py:542
  89.4 1.1 collective-permute-done.17.refs_1_
  90.4 0.1 collective-permute-done.18.refs_2_
  90.6 0.2 shard_map.102
  90.7 1.1 collective-permute-start.21
  91.9 1.8 %collective-permute-start.22 = (f32[40,1920]{1,0:T(8,128)S(1)}, f32[40,1920]{1,0:T(8,128)S(1)}, u32[]{:S(2)}, u32[]{:S(2)}) collective-permute-start(f32[40,1920]{1,0:T(8,128)S(1)} %get-tuple-element.140), channel_id=1, source_target_pairs={{0,6},{1,25},{2,0},{3,27},{4,2},{5,29},{6,4},{7,31},{8,14},{9,17},... | collective-permute-start | bytes 921608 | tf_op jit(solution)/shard_map/ppermute | solution.py:379
  93.7 1.1 shard_map.103
  94.9 1.1 collective-permute-start.19
  95.9 1.8 %collective-permute-start.20 = (f32[40,768]{1,0:T(8,128)S(1)}, f32[40,768]{1,0:T(8,128)S(1)}, u32[]{:S(2)}, u32[]{:S(2)}) collective-permute-start(f32[40,768]{1,0:T(8,128)S(1)} %get-tuple-element.137), channel_id=1, source_target_pairs={{0,6},{1,7},{2,0},{3,1},{4,2},{5,3},{6,4},{7,5},{8,14},{9,15},{10,... | collective-permute-start | bytes 368648 | tf_op jit(solution)/shard_map/ppermute | solution.py:379
  97.7 0.6 collective-permute-done.21.refs_1_
  98.3 1.4 %collective-permute-done.22.refs_2_ = f32[40,1920]{1,0:T(8,128)S(1)} collective-permute-done((f32[40,1920]{1,0:T(8,128)S(1)}, f32[40,1920]{1,0:T(8,128)S(1)}, u32[]{:S(2)}, u32[]{:S(2)}) %collective-permute-start.22) | collective-permute-done | bytes 307232 | tf_op jit(solution)/shard_map/ppermute | solution.py:379
  99.7 0.1 shard_map.104
  99.8 1.3 %collective-permute-start.23 = (f32[20,1920]{1,0:T(8,128)S(1)}, f32[20,1920]{1,0:T(8,128)S(1)}, u32[]{:S(2)}, u32[]{:S(2)}) collective-permute-start(f32[20,1920]{1,0:T(8,128)S(1)} %get-tuple-element.146), channel_id=1, source_target_pairs={{0,16},{1,33},{2,18},{3,35},{4,20},{5,37},{6,22},{7,39},{8,24},{9,... | collective-permute-start | bytes 460808 | tf_op jit(solution)/shard_map/ppermute | solution.py:379
  101.0 2.4 %collective-permute-start.24 = (f32[20,1920]{1,0:T(8,128)S(1)}, f32[20,1920]{1,0:T(8,128)S(1)}, u32[]{:S(2)}, u32[]{:S(2)}) collective-permute-start(f32[20,1920]{1,0:T(8,128)S(1)} %get-tuple-element.147), channel_id=1, source_target_pairs={{0,8},{1,65},{2,10},{3,67},{4,12},{5,69},{6,14},{7,71},{8,0},{9,73... | collective-permute-start | bytes 460808 | tf_op jit(solution)/shard_map/ppermute | solution.py:379
  103.5 1.2 collective-permute-start.25
  104.7 0.4 collective-permute-start.26
  105.0 0.9 collective-permute-start.27
  105.9 3.4 %collective-permute-done.26.refs_6_ = f32[20,768]{1,0:T(8,128)S(1)} collective-permute-done((f32[20,768]{1,0:T(8,128)S(1)}, f32[20,768]{1,0:T(8,128)S(1)}, u32[]{:S(2)}, u32[]{:S(2)}) %collective-permute-start.26) | collective-permute-done | bytes 61472 | tf_op jit(solution)/shard_map/ppermute | solution.py:379
  109.4 0.3 collective-permute-start.28
  109.6 0.9 shard_map.106
  110.5 2.3 %collective-permute-done.28.refs_8_ = f32[20,768]{1,0:T(8,128)S(1)} collective-permute-done((f32[20,768]{1,0:T(8,128)S(1)}, f32[20,768]{1,0:T(8,128)S(1)}, u32[]{:S(2)}, u32[]{:S(2)}) %collective-permute-start.28) | collective-permute-done | bytes 61472 | tf_op jit(solution)/shard_map/ppermute | solution.py:379
  112.9 0.6 shard_map.107
  113.5 6.1 %collective-permute-start.29 = (f32[10,2688]{1,0:T(8,128)S(1)}, f32[10,2688]{1,0:T(8,128)S(1)}, u32[]{:S(2)}, u32[]{:S(2)}) collective-permute-start(f32[10,2688]{1,0:T(8,128)S(1)} %get-tuple-element.155), channel_id=1, source_target_pairs={{0,1},{1,0},{2,3},{3,2},{4,5},{5,4},{6,7},{7,6},{8,9},{9,8},{10,11... | collective-permute-start | bytes 322568 | tf_op jit(solution)/shard_map/ppermute | solution.py:383
  119.6 1.0 collective-permute-done.29.refs_2_
  120.6 1.3 %shard_map.108 = (f32[10,3840]{1,0:T(8,128)}, f32[10,1280]{1,0:T(8,128)}, f32[1,10]{1,0:T(1,128)}) custom-call(s32[4]{0:T(128)S(1)} %pad_add_fusion.place_ref.refs_0_, f32[10,2688]{1,0:T(8,128)S(1)} %get-tuple-element.154.refs_1_, f32[10,2688]{1,0:T(8,128)S(1)} %collective-permute-done.29.refs_2_, f32[8,128]{1,0:T(8,128)S(1)} %get-tuple-element.156.refs_3_), custom_call_target="tpu_custom_call" | custom-call | bytes 1 | tf_op jit(solution)/shard_map/pallas_call | solution.py:54
  (41 shorter events, 0.2 us)
Async XLA Ops:
  3.2 6.8 %copy-start.6 = (f32[1280]{0:T(1024)S(1)}, f32[1280]{0:T(1024)}, u32[]{:S(2)}) copy-start(f32[1280]{0:T(1024)} %param.7) | copy-start | bytes 15364
  3.2 24.4 %all-to-all-start = ((bf16[8,2,4,8,1280]{4,3,2,1,0:T(8,128)(2,1)}), bf16[8,2,4,8,1280]{4,3,2,1,0:T(8,128)(2,1)S(1)}, u32[]{:S(2)}, u32[]{:S(2)}) async-start(bf16[8,2,4,8,1280]{4,3,2,1,0:T(8,128)(2,1)} %shard_map.84), calls=%async_computation | async-start | bytes 2621440 | tf_op jit(solution)/shard_map/all_to_all | solution.py:430
  27.6 6.8 %copy-start.2 = (bf16[1280,1280]{1,0:T(8,128)(2,1)S(1)}, bf16[1280,1280]{1,0:T(8,128)(2,1)}, u32[]{:S(2)}) copy-start(bf16[1280,1280]{1,0:T(8,128)(2,1)} %refs_3_.5) | copy-start | bytes 9830404
  38.6 8.3 %collective-permute-start.4 = (bf16[256,1920]{1,0:T(8,128)(2,1)S(1)}, bf16[256,1920]{1,0:T(8,128)(2,1)S(1)}, u32[]{:S(2)}, u32[]{:S(2)}) collective-permute-start(bf16[256,1920]{1,0:T(8,128)(2,1)S(1)} %get-tuple-element.88.refs_5_), channel_id=1, source_target_pairs={{0,1},{1,0},{2,3},{3,2},{4,5},{5,4},{6,7},{7,6},{8,9},{9,8},{10,11... | collective-permute-start | bytes 2949128 | tf_op jit(solution)/shard_map/ppermute | solution.py:383
  40.6 4.4 %collective-permute-start.3 = (bf16[256,1280]{1,0:T(8,128)(2,1)S(1)}, bf16[256,1280]{1,0:T(8,128)(2,1)S(1)}, u32[]{:S(2)}, u32[]{:S(2)}) collective-permute-start(bf16[256,1280]{1,0:T(8,128)(2,1)S(1)} %get-tuple-element.95.refs_1_), channel_id=1, source_target_pairs={{0,1},{1,0},{2,3},{3,2},{4,5},{5,4},{6,7},{7,6},{8,9},{9,8},{10,11... | collective-permute-start | bytes 1966088 | tf_op jit(solution)/shard_map/ppermute | solution.py:383
  40.9 4.2 %copy-start.3 = (bf16[1280,1280]{1,0:T(8,128)(2,1)S(1)}, bf16[1280,1280]{1,0:T(8,128)(2,1)}, u32[]{:S(2)}) copy-start(bf16[1280,1280]{1,0:T(8,128)(2,1)} %get-tuple-element.94.refs_0_) | copy-start | bytes 9830404
  47.0 6.8 %copy-start = (bf16[1280,1280]{1,0:T(8,128)(2,1)S(1)}, bf16[1280,1280]{1,0:T(8,128)(2,1)}, u32[]{:S(2)}) copy-start(bf16[1280,1280]{1,0:T(8,128)(2,1)} %get-tuple-element.91.refs_0_) | copy-start | bytes 9830404
  48.5 17.2 %collective-permute-start.8 = (bf16[320,1920]{1,0:T(8,128)(2,1)S(1)}, bf16[320,1920]{1,0:T(8,128)(2,1)S(1)}, u32[]{:S(2)}, u32[]{:S(2)}) collective-permute-start(bf16[320,1920]{1,0:T(8,128)(2,1)S(1)} %get-tuple-element.108), channel_id=1, source_target_pairs={{0,32},{1,3},{2,34},{3,5},{4,36},{5,7},{6,38},{7,1},{8,40},{9,11},... | collective-permute-start | bytes 3686408 | tf_op jit(solution)/shard_map/ppermute | solution.py:379
  49.9 15.9 %collective-permute-start.9 = (bf16[320,1920]{1,0:T(8,128)(2,1)S(1)}, bf16[320,1920]{1,0:T(8,128)(2,1)S(1)}, u32[]{:S(2)}, u32[]{:S(2)}) collective-permute-start(bf16[320,1920]{1,0:T(8,128)(2,1)S(1)} %get-tuple-element.109), channel_id=1, source_target_pairs={{0,96},{1,7},{2,98},{3,1},{4,100},{5,3},{6,102},{7,5},{8,104},{9,1... | collective-permute-start | bytes 3686408 | tf_op jit(solution)/shard_map/ppermute | solution.py:379
  51.4 1.9 %collective-permute-start.1 = (bf16[256,640]{1,0:T(8,128)(2,1)S(1)}, bf16[256,640]{1,0:T(8,128)(2,1)S(1)}, u32[]{:S(2)}, u32[]{:S(2)}) collective-permute-start(bf16[256,640]{1,0:T(8,128)(2,1)S(1)} %get-tuple-element.92.refs_1_), channel_id=1, source_target_pairs={{0,1},{1,0},{2,3},{3,2},{4,5},{5,4},{6,7},{7,6},{8,9},{9,8},{10,11... | collective-permute-start | bytes 983048 | tf_op jit(solution)/shard_map/ppermute | solution.py:383
  52.1 1.7 %collective-permute-start.2 = (bf16[256,640]{1,0:T(8,128)(2,1)S(1)}, bf16[256,640]{1,0:T(8,128)(2,1)S(1)}, u32[]{:S(2)}, u32[]{:S(2)}) collective-permute-start(bf16[256,640]{1,0:T(8,128)(2,1)S(1)} %get-tuple-element.93.refs_2_), channel_id=1, source_target_pairs={{0,1},{1,0},{2,3},{3,2},{4,5},{5,4},{6,7},{7,6},{8,9},{9,8},{10,11... | collective-permute-start | bytes 983048 | tf_op jit(solution)/shard_map/ppermute | solution.py:383
  52.1 4.0 %collective-permute-start = (bf16[256,640]{1,0:T(8,128)(2,1)S(1)}, bf16[256,640]{1,0:T(8,128)(2,1)S(1)}, u32[]{:S(2)}, u32[]{:S(2)}) collective-permute-start(bf16[256,640]{1,0:T(8,128)(2,1)S(1)} %get-tuple-element.90), channel_id=1, source_target_pairs={{0,1},{1,0},{2,3},{3,2},{4,5},{5,4},{6,7},{7,6},{8,9},{9,8},{10,11... | collective-permute-start | bytes 983048 | tf_op jit(solution)/shard_map/ppermute | solution.py:383
  56.1 4.0 %copy-start.1 = (bf16[1280,1280]{1,0:T(8,128)(2,1)S(1)}, bf16[1280,1280]{1,0:T(8,128)(2,1)}, u32[]{:S(2)}) copy-start(bf16[1280,1280]{1,0:T(8,128)(2,1)} %get-tuple-element.89.refs_6_) | copy-start | bytes 9830404
  57.3 16.3 %collective-permute-start.5 = (bf16[320,640]{1,0:T(8,128)(2,1)S(1)}, bf16[320,640]{1,0:T(8,128)(2,1)S(1)}, u32[]{:S(2)}, u32[]{:S(2)}) collective-permute-start(bf16[320,640]{1,0:T(8,128)(2,1)S(1)} %get-tuple-element.104), channel_id=1, source_target_pairs={{0,16},{1,17},{2,18},{3,19},{4,20},{5,21},{6,22},{7,23},{8,24},{9,... | collective-permute-start | bytes 1228808 | tf_op jit(solution)/shard_map/ppermute | solution.py:379
  57.9 15.7 %collective-permute-start.6 = (bf16[320,640]{1,0:T(8,128)(2,1)S(1)}, bf16[320,640]{1,0:T(8,128)(2,1)S(1)}, u32[]{:S(2)}, u32[]{:S(2)}) collective-permute-start(bf16[320,640]{1,0:T(8,128)(2,1)S(1)} %get-tuple-element.105), channel_id=1, source_target_pairs={{0,24},{1,25},{2,26},{3,27},{4,28},{5,29},{6,30},{7,31},{8,16},{9,... | collective-permute-start | bytes 1228808 | tf_op jit(solution)/shard_map/ppermute | solution.py:379
  66.6 11.6 %collective-permute-start.13 = (bf16[160,1920]{1,0:T(8,128)(2,1)S(1)}, bf16[160,1920]{1,0:T(8,128)(2,1)S(1)}, u32[]{:S(2)}, u32[]{:S(2)}) collective-permute-start(bf16[160,1920]{1,0:T(8,128)(2,1)S(1)} %get-tuple-element.121), channel_id=1, source_target_pairs={{0,32},{1,3},{2,34},{3,5},{4,36},{5,7},{6,38},{7,1},{8,40},{9,11},... | collective-permute-start | bytes 1843208 | tf_op jit(solution)/shard_map/ppermute | solution.py:379
  68.0 10.3 %collective-permute-start.14 = (bf16[160,1920]{1,0:T(8,128)(2,1)S(1)}, bf16[160,1920]{1,0:T(8,128)(2,1)S(1)}, u32[]{:S(2)}, u32[]{:S(2)}) collective-permute-start(bf16[160,1920]{1,0:T(8,128)(2,1)S(1)} %get-tuple-element.122), channel_id=1, source_target_pairs={{0,96},{1,7},{2,98},{3,1},{4,100},{5,3},{6,102},{7,5},{8,104},{9,1... | collective-permute-start | bytes 1843208 | tf_op jit(solution)/shard_map/ppermute | solution.py:379
  69.5 4.0 %collective-permute-start.7 = (f32[8,384]{1,0:T(8,128)S(1)}, f32[8,384]{1,0:T(8,128)S(1)}, u32[]{:S(2)}, u32[]{:S(2)}) collective-permute-start(f32[8,384]{1,0:T(8,128)S(1)} %get-tuple-element.107), channel_id=1, source_target_pairs={{0,8},{8,0},{1,9},{9,1},{2,10},{10,2},{3,11},{11,3},{4,12},{12,4},... | collective-permute-start | bytes 36872 | tf_op jit(solution)/shard_map/ppermute | solution.py:534
  74.6 7.7 %collective-permute-start.10 = (bf16[160,640]{1,0:T(8,128)(2,1)S(1)}, bf16[160,640]{1,0:T(8,128)(2,1)S(1)}, u32[]{:S(2)}, u32[]{:S(2)}) collective-permute-start(bf16[160,640]{1,0:T(8,128)(2,1)S(1)} %get-tuple-element.116), channel_id=1, source_target_pairs={{0,16},{1,17},{2,18},{3,19},{4,20},{5,21},{6,22},{7,23},{8,24},{9,... | collective-permute-start | bytes 614408 | tf_op jit(solution)/shard_map/ppermute | solution.py:379
  75.5 6.8 %collective-permute-start.11 = (bf16[160,640]{1,0:T(8,128)(2,1)S(1)}, bf16[160,640]{1,0:T(8,128)(2,1)S(1)}, u32[]{:S(2)}, u32[]{:S(2)}) collective-permute-start(bf16[160,640]{1,0:T(8,128)(2,1)S(1)} %get-tuple-element.117), channel_id=1, source_target_pairs={{0,24},{1,25},{2,26},{3,27},{4,28},{5,29},{6,30},{7,31},{8,16},{9,... | collective-permute-start | bytes 614408 | tf_op jit(solution)/shard_map/ppermute | solution.py:379
  77.3 5.0 %collective-permute-start.12 = (f32[8,384]{1,0:T(8,128)S(1)}, f32[8,384]{1,0:T(8,128)S(1)}, u32[]{:S(2)}, u32[]{:S(2)}) collective-permute-start(f32[8,384]{1,0:T(8,128)S(1)} %get-tuple-element.119), channel_id=1, source_target_pairs={{0,16},{16,0},{1,17},{17,1},{2,18},{18,2},{3,19},{19,3},{4,20},{20... | collective-permute-start | bytes 36872 | tf_op jit(solution)/shard_map/ppermute | solution.py:538
  79.6 10.8 %collective-permute-start.17 = (f32[80,1920]{1,0:T(8,128)}, f32[80,1920]{1,0:T(8,128)S(1)}, u32[]{:S(2)}, u32[]{:S(2)}) collective-permute-start(f32[80,1920]{1,0:T(8,128)} %get-tuple-element.131), channel_id=1, source_target_pairs={{0,2},{1,17},{2,4},{3,19},{4,6},{5,21},{6,0},{7,23},{8,10},{9,25},... | collective-permute-start | bytes 1843208 | tf_op jit(solution)/shard_map/ppermute | solution.py:379
  81.1 9.5 %collective-permute-start.18 = (f32[80,1920]{1,0:T(8,128)}, f32[80,1920]{1,0:T(8,128)S(1)}, u32[]{:S(2)}, u32[]{:S(2)}) collective-permute-start(f32[80,1920]{1,0:T(8,128)} %get-tuple-element.132), channel_id=1, source_target_pairs={{0,6},{1,25},{2,0},{3,27},{4,2},{5,29},{6,4},{7,31},{8,14},{9,17},... | collective-permute-start | bytes 1843208 | tf_op jit(solution)/shard_map/ppermute | solution.py:379
  83.1 2.7 %copy-start.4 = (f32[160,768]{1,0:T(8,128)}, f32[160,768]{1,0:T(8,128)S(1)}, u32[]{:S(2)}) copy-start(f32[160,768]{1,0:T(8,128)S(1)} %get-tuple-element.127.refs_0_) | copy-start | bytes 1474564
  83.1 10.6 %collective-permute-start.15 = (f32[80,768]{1,0:T(8,128)}, f32[80,768]{1,0:T(8,128)}, u32[]{:S(2)}, u32[]{:S(2)}) collective-permute-start(f32[80,768]{1,0:T(8,128)} %get-tuple-element.128), channel_id=1, source_target_pairs={{0,2},{1,3},{2,4},{3,5},{4,6},{5,7},{6,0},{7,1},{8,10},{9,11},{10,... | collective-permute-start | bytes 737288 | tf_op jit(solution)/shard_map/ppermute | solution.py:379
  83.1 10.6 %collective-permute-start.16 = (f32[80,768]{1,0:T(8,128)S(1)}, f32[80,768]{1,0:T(8,128)}, u32[]{:S(2)}, u32[]{:S(2)}) collective-permute-start(f32[80,768]{1,0:T(8,128)S(1)} %get-tuple-element.129), channel_id=1, source_target_pairs={{0,6},{1,7},{2,0},{3,1},{4,2},{5,3},{6,4},{7,5},{8,14},{9,15},{10,... | collective-permute-start | bytes 737288 | tf_op jit(solution)/shard_map/ppermute | solution.py:379
  85.8 23.8 %all-to-all-start.1 = ((bf16[8,4,8,1280]{3,2,1,0:T(8,128)(2,1)}), bf16[8,4,8,1280]{3,2,1,0:T(8,128)(2,1)S(1)}, u32[]{:S(2)}, u32[]{:S(2)}) async-start(bf16[8,4,8,1280]{3,2,1,0:T(8,128)(2,1)} %bitcast.7), calls=%async_computation.1 | async-start | bytes 1310720 | tf_op jit(solution)/shard_map/all_to_all | solution.py:542
  89.4 4.4 %copy-start.5 = (f32[160,768]{1,0:T(8,128)S(1)}, f32[160,768]{1,0:T(8,128)}, u32[]{:S(2)}) copy-start(f32[160,768]{1,0:T(8,128)} %copy-done.4) | copy-start | bytes 1474564
  90.7 7.6 %collective-permute-start.21 = (f32[40,1920]{1,0:T(8,128)S(1)}, f32[40,1920]{1,0:T(8,128)S(1)}, u32[]{:S(2)}, u32[]{:S(2)}) collective-permute-start(f32[40,1920]{1,0:T(8,128)S(1)} %get-tuple-element.139), channel_id=1, source_target_pairs={{0,2},{1,17},{2,4},{3,19},{4,6},{5,21},{6,0},{7,23},{8,10},{9,25},... | collective-permute-start | bytes 921608 | tf_op jit(solution)/shard_map/ppermute | solution.py:379
  91.9 7.8 %collective-permute-start.22 = (f32[40,1920]{1,0:T(8,128)S(1)}, f32[40,1920]{1,0:T(8,128)S(1)}, u32[]{:S(2)}, u32[]{:S(2)}) collective-permute-start(f32[40,1920]{1,0:T(8,128)S(1)} %get-tuple-element.140), channel_id=1, source_target_pairs={{0,6},{1,25},{2,0},{3,27},{4,2},{5,29},{6,4},{7,31},{8,14},{9,17},... | collective-permute-start | bytes 921608 | tf_op jit(solution)/shard_map/ppermute | solution.py:379
  94.9 9.8 %collective-permute-start.19 = (f32[40,768]{1,0:T(8,128)S(1)}, f32[40,768]{1,0:T(8,128)S(1)}, u32[]{:S(2)}, u32[]{:S(2)}) collective-permute-start(f32[40,768]{1,0:T(8,128)S(1)} %get-tuple-element.136), channel_id=1, source_target_pairs={{0,2},{1,3},{2,4},{3,5},{4,6},{5,7},{6,0},{7,1},{8,10},{9,11},{10,... | collective-permute-start | bytes 368648 | tf_op jit(solution)/shard_map/ppermute | solution.py:379
  95.9 8.7 %collective-permute-start.20 = (f32[40,768]{1,0:T(8,128)S(1)}, f32[40,768]{1,0:T(8,128)S(1)}, u32[]{:S(2)}, u32[]{:S(2)}) collective-permute-start(f32[40,768]{1,0:T(8,128)S(1)} %get-tuple-element.137), channel_id=1, source_target_pairs={{0,6},{1,7},{2,0},{3,1},{4,2},{5,3},{6,4},{7,5},{8,14},{9,15},{10,... | collective-permute-start | bytes 368648 | tf_op jit(solution)/shard_map/ppermute | solution.py:379
  99.8 13.1 %collective-permute-start.23 = (f32[20,1920]{1,0:T(8,128)S(1)}, f32[20,1920]{1,0:T(8,128)S(1)}, u32[]{:S(2)}, u32[]{:S(2)}) collective-permute-start(f32[20,1920]{1,0:T(8,128)S(1)} %get-tuple-element.146), channel_id=1, source_target_pairs={{0,16},{1,33},{2,18},{3,35},{4,20},{5,37},{6,22},{7,39},{8,24},{9,... | collective-permute-start | bytes 460808 | tf_op jit(solution)/shard_map/ppermute | solution.py:379
  101.0 11.8 %collective-permute-start.24 = (f32[20,1920]{1,0:T(8,128)S(1)}, f32[20,1920]{1,0:T(8,128)S(1)}, u32[]{:S(2)}, u32[]{:S(2)}) collective-permute-start(f32[20,1920]{1,0:T(8,128)S(1)} %get-tuple-element.147), channel_id=1, source_target_pairs={{0,8},{1,65},{2,10},{3,67},{4,12},{5,69},{6,14},{7,71},{8,0},{9,73... | collective-permute-start | bytes 460808 | tf_op jit(solution)/shard_map/ppermute | solution.py:379
  103.5 9.4 %collective-permute-start.25 = (f32[20,1920]{1,0:T(8,128)S(1)}, f32[20,1920]{1,0:T(8,128)S(1)}, u32[]{:S(2)}, u32[]{:S(2)}) collective-permute-start(f32[20,1920]{1,0:T(8,128)S(1)} %get-tuple-element.148), channel_id=1, source_target_pairs={{0,24},{1,97},{2,26},{3,99},{4,28},{5,101},{6,30},{7,103},{8,16},{... | collective-permute-start | bytes 460808 | tf_op jit(solution)/shard_map/ppermute | solution.py:379
  104.7 4.7 %collective-permute-start.26 = (f32[20,768]{1,0:T(8,128)S(1)}, f32[20,768]{1,0:T(8,128)S(1)}, u32[]{:S(2)}, u32[]{:S(2)}) collective-permute-start(f32[20,768]{1,0:T(8,128)S(1)} %get-tuple-element.150), channel_id=1, source_target_pairs={{0,32},{1,33},{2,34},{3,35},{4,36},{5,37},{6,38},{7,39},{8,40},{9,... | collective-permute-start | bytes 184328 | tf_op jit(solution)/shard_map/ppermute | solution.py:379
  105.0 5.5 %collective-permute-start.27 = (f32[20,768]{1,0:T(8,128)S(1)}, f32[20,768]{1,0:T(8,128)S(1)}, u32[]{:S(2)}, u32[]{:S(2)}) collective-permute-start(f32[20,768]{1,0:T(8,128)S(1)} %get-tuple-element.151), channel_id=1, source_target_pairs={{0,64},{1,65},{2,66},{3,67},{4,68},{5,69},{6,70},{7,71},{8,72},{9,... | collective-permute-start | bytes 184328 | tf_op jit(solution)/shard_map/ppermute | solution.py:379
  109.4 3.5 %collective-permute-start.28 = (f32[20,768]{1,0:T(8,128)S(1)}, f32[20,768]{1,0:T(8,128)S(1)}, u32[]{:S(2)}, u32[]{:S(2)}) collective-permute-start(f32[20,768]{1,0:T(8,128)S(1)} %get-tuple-element.152), channel_id=1, source_target_pairs={{0,96},{1,97},{2,98},{3,99},{4,100},{5,101},{6,102},{7,103},{8,104... | collective-permute-start | bytes 184328 | tf_op jit(solution)/shard_map/ppermute | solution.py:379
  113.5 7.1 %collective-permute-start.29 = (f32[10,2688]{1,0:T(8,128)S(1)}, f32[10,2688]{1,0:T(8,128)S(1)}, u32[]{:S(2)}, u32[]{:S(2)}) collective-permute-start(f32[10,2688]{1,0:T(8,128)S(1)} %get-tuple-element.155), channel_id=1, source_target_pairs={{0,1},{1,0},{2,3},{3,2},{4,5},{5,4},{6,7},{7,6},{8,9},{9,8},{10,11... | collective-permute-start | bytes 322568 | tf_op jit(solution)/shard_map/ppermute | solution.py:383

commit v2 on v1

--- a/solution.py
+++ b/solution.py
@@ -109,7 +109,7 @@
 
 
 def forward_body(place_ref, both_ref, gain_ref, weight_ref, gained_ref, qkv_ref, cot_ref,
-                 held_ref, sems):
+                 held_ref, hat_ref, inv_ref, sems):
     pieces = [slice(step * HALF, (step + 1) * HALF) for step in range(6)]
     copies = [
         pltpu.make_async_copy(weight_ref.at[:, piece], held_ref.at[:, piece], sems.at[step])
@@ -117,7 +117,9 @@
     ]
     for copy in copies[:2]:
         copy.start()
-    normalized, _ = normalize(both_ref)
+    normalized, inv_std = normalize(both_ref)
+    hat_ref[...] = normalized
+    inv_ref[...] = jnp.broadcast_to(inv_std, (TOKENS, 128))
     gained = (normalized * gain_ref[...]).astype(BF16)
     gained_ref[...] = gained
     cot_ref[...] = side(both_ref, 1, half(place_ref, False))
@@ -173,15 +175,24 @@
                 stack_ref[:, at:at + 128] = total
 
 
-def input_grad_body(place_ref, both_ref, gain_ref, weight_ref, mine_ref, other_ref, pick_ref,
+def joint_attention_body(group_ref, qkv_ref, both_ref, weight_ref, out_ref, *scratch):
+    attention_body(
+        group_ref, qkv_ref, both_ref, weight_ref, out_ref.at[:, :HALF], out_ref.at[:, HALF:],
+        *scratch
+    )
+
+
+def input_grad_body(place_ref, both_ref, hat_ref, inv_ref, gain_ref, weight_ref, mine_ref,
+                    other_ref, pick_ref,
                     grad_ref, keep, give, joined_ref):
     for own, stack_ref in ((True, mine_ref), (False, other_ref)):
         group = place_ref[3] if own else 1 - place_ref[3]
         for part in range(3):
             columns = pl.ds(pl.multiple_of(group * HALF + part * D, 128), HALF)
-            joined_ref[:, columns] = stack_ref[:, part * HALF:(part + 1) * HALF]
+            start = part * HALF if own else (part + 1) * HALF
+            joined_ref[:, columns] = stack_ref[:, start:start + HALF]
     normed_grad = dot(joined_ref[...], weight_ref[...], NT)
-    normalized, inv_std = normalize(both_ref)
+    normalized, inv_std = hat_ref[...], inv_ref[:, 0:1]
     scaled = normed_grad * gain_ref[...]
     inner = scaled - jnp.mean(scaled, axis=-1, keepdims=True)
     inner -= normalized * jnp.mean(scaled * normalized, axis=-1, keepdims=True)
@@ -259,18 +270,18 @@
         out[rows, TOKENS:] = dot(pick_ref[rows, :], partner_ref[...], NT).astype(BF16)
 
 
-def turn_body(pick_att, mine, other, their_mine, their_other, att_out):
-    sides = ((mine, other), (their_other, their_mine))
+def turn_body(pick_att, mine, other, their_mine, theirs, att_out):
+    sides = ((mine, other), (theirs, their_mine))
     for step in range(4):
         rows = slice(step * 320, (step + 1) * 320)
         for which, (first, second) in enumerate(sides):
-            turned = dot(pick_att[rows, :HALF], first[...], NT)
-            turned += dot(pick_att[rows, HALF:], second[...], NT)
+            turned = dot(pick_att[rows, :HALF], first[:, :HALF], NT)
+            turned += dot(pick_att[rows, HALF:], second[:, :HALF], NT)
             att_out[rows, which * TOKENS:(which + 1) * TOKENS] = turned.astype(BF16)
 
 
-def term_a(rows, gained, stack, their_stack):
-    return dot(gained[rows, :TOKENS], stack[...]) + dot(gained[rows, TOKENS:], their_stack[...])
+def term_a(rows, gained, stack, theirs):
+    return dot(gained[rows, :TOKENS], stack[...]) + dot(gained[rows, TOKENS:], theirs[:, HALF:])
 
 
 def term_b(rows, place_ref, both, their_cot, att):
@@ -337,16 +348,17 @@
     three[...] = lower[20:40]
 
 
-def final_body(place_ref, *refs):
+def add_body(own, one, two, three, out):
+    out[...] = (own[...] + one[...]) + (two[...] + three[...])
+
+
+def final_body(place_ref, total_a, own, one, two, three, here, other):
     on_first = place_ref[3] == 0
-    blocks, outs = refs[:8], refs[8:]
-    for first, columns in ((0, slice(0, WIDTH_A)), (4, slice(WIDTH_A, WIDTH_A + WIDTH_B))):
-        total = blocks[first][...]
-        for other in range(1, 4):
-            total += blocks[first + other][...]
-        low, high = total[0:10], total[10:20]
-        outs[0][:, columns] = jnp.where(on_first, low, high)
-        outs[1][:, columns] = jnp.where(on_first, high, low)
+    total_b = (own[...] + one[...]) + (two[...] + three[...])
+    total = jnp.concatenate([total_a[...], total_b], axis=1)
+    low, high = total[0:10], total[10:20]
+    here[...] = jnp.where(on_first, low, high)
+    other[...] = jnp.where(on_first, high, low)
 
 
 def assemble_body(place_ref, here, theirs, qkv_ref, out_ref, gain_ref):
@@ -429,32 +441,35 @@
     )(place)
     both = lax.all_to_all(both, ("z", "xl"), split_axis=0, concat_axis=0, tiled=True)
     both = both.reshape(8, 64, D)
-    (gained, qkv, cot_other, weight), token = call(
+    (gained, qkv, cot_other, weight, hat, inv_std), token = call(
         forward_body,
-        [shape(TOKENS, D), shape(TOKENS, 3 * D), shape(TOKENS, HALF), shape(D, 3 * D)],
+        [shape(TOKENS, D), shape(TOKENS, 3 * D), shape(TOKENS, HALF), shape(D, 3 * D),
+         shape(TOKENS, D, F32), shape(TOKENS, 128, F32)],
         [place, both, gain_row, qkv_weight], scalars=1, flops=2 * TOKENS * D * 3 * D,
         scratch=[pltpu.SemaphoreType.DMA((6,))], hbm=(3,), after=[token],
     )
     their_gained, their_cot = swap(gained), swap(cot_other)
 
-    def attention(which, after):
+    def attention(which, after, outs):
         return call(
-            attention_body, [shape(TOKENS, HALF), shape(TOKENS, 3 * HALF)],
+            attention_body if len(outs) == 2 else joint_attention_body, outs,
             [which, qkv, both, out_weight], scalars=1, flops=5 * 10**9,
             scratch=[pltpu.VMEM((TOKENS, HALF), BF16), pltpu.VMEM((TOKENS, TOKENS), F32)],
             after=after,
         )
 
-    (att_other, stack_other), token = attention(1 - group, token)
-    their_stack, their_other = swap(stack_other), swap(att_other)
-    (att_mine, stack), token = attention(group, token)
+    (other_half,), token = attention(1 - group, token, [shape(TOKENS, 4 * HALF)])
+    their_half = swap(other_half)
+    (att_mine, stack), token = attention(
+        group, token, [shape(TOKENS, HALF), shape(TOKENS, 3 * HALF)]
+    )
     their_mine = swap(att_mine)
     (gained_a,), token = call(
         gained_body, [shape(D, 512)], [pick_a, gained, their_gained], flops=2 * D * D * 512,
         after=token,
     )
     work = {"a": 10**7, "b": 15 * 10**8, "b second": 8 * 10**9}
-    base = {"a": [gained_a, stack, their_stack]}
+    base = {"a": [gained_a, stack, their_half]}
     kinds = {"a": (term_a, 0, WIDTH_A, ORDER_A), "b": (term_b, 1, HALF, ORDER_B)}
 
     def run(which, body, outs, extra, after):
@@ -512,31 +527,31 @@
     def third(which, after):
         outs = [shape(20, state[which][0].shape[1], F32)] * 4
         (own, *others), after = call(
-            third_body, outs, state[which], flops=10**6, after=after
+            third_body, outs, state[which], flops=work[which], after=after
         )
         order = kinds[which][3]
         sent = [send(other, order, 2, step + 1) for step, other in enumerate(others)]
         state[which] = [own] + sent
         return after
 
-    token = early("a", token)
+    token = early("a", token + [their_mine])
     (att,), token = call(
-        turn_body, [shape(D, 512)], [pick_att, att_mine, att_other, their_mine, their_other],
+        turn_body, [shape(D, 512)], [pick_att, att_mine, other_half, their_mine, their_half],
         after=token,
     )
     base["b"] = [place, both, their_cot, att]
     token = early("b", token)
     (grad_here, keep, give), token = call(
         input_grad_body, [shape(TOKENS, D)] + [shape(8, 384, F32)] * 2,
-        [place, both, gain_row, weight, stack, stack_other, pick_b], scalars=1, after=token,
+        [place, both, hat, inv_std, gain_row, weight, stack, other_half, pick_b], scalars=1,
+        after=token,
         scratch=[pltpu.VMEM((TOKENS, 3 * D), BF16)],
     )
     arrived = lax.ppermute(give, "xh", [(0, 1), (1, 0)])
-    token = own_rows("a", relay("a", token))
-    token = relay("b", token + [arrived])
+    token = relay("b", relay("a", token))
+    token = own_rows("b", own_rows("a", token))
     (own, give), token = call(gain_body, [shape(8, 384, F32)] * 2, [keep, arrived], after=token)
     gains["b"] = [own, lax.ppermute(give, "xl", [(0, 1), (1, 0)])]
-    token = own_rows("b", token)
     token = second_early("b", second_early("a", token))
     grad_here, token = late(grad_here, token)
     back = lax.all_to_all(
@@ -544,6 +559,7 @@
     )
     token = second_relay("b", second_relay("a", token))
     token = third("b", third("a", token))
+    (total_a,), token = call(add_body, [shape(20, WIDTH_A, F32)], state["a"], after=token)
     grad_tokens, token = pl.pallas_call(
         join_body,
         out_shape=[jax.ShapeDtypeStruct((4, 8, 8, D), BF16), pltpu.VMEM((8, 128), F32)],
@@ -552,7 +568,7 @@
         cost_estimate=pl.CostEstimate(flops=10**7, bytes_accessed=1, transcendentals=0),
     )(back, pltpu.with_memory_space_constraint(token[0], pltpu.VMEM))
     (here, other), token = call(
-        final_body, [shape(10, WIDTH_A + WIDTH_B, F32)] * 2, [place] + state["a"] + state["b"],
+        final_body, [shape(10, WIDTH_A + WIDTH_B, F32)] * 2, [place, total_a] + state["b"],
         scalars=1, after=[token],
     )
     theirs = swap(other)

time: 122 us -> 122 us (level)
  waiting for transfers between devices: 23.5 us -> 22 us
    ppermute x6 -> x5, starting transfers between devices: 9.48 us -> 10.3 us  [swap(): return lax.ppermute(value, 'c', [(0, 1), (1, 0)])]
    pallas_call x21 -> x22, Pallas kernels: 36.3 us -> 36.3 us  [call(): pl.pallas_call(run, out_shape=[results(o.shape, o.dtype) for o in outs] +...]
  transfers between devices with their start and end apart: 32 -> 31, of which waited for: 12 -> 12; matrix products, arithmetic and copies ran while one was open for 0% -> 0% of each run, Pallas kernels for 24% -> 24%
where the time goes in v2:
time: 122 us; the launch traced here: 121 us
  starting transfers between devices  52.2 us (43%)
  Pallas kernels  46.1 us (38%)
  waiting for transfers between devices  22 us (18%)
    pallas_call x22, Pallas kernels, call(): pl.pallas_call(run, out_shape=[results(o.shape, o.dtype) for o in outs] +...  36.3 us
    ppermute x22, starting transfers between devices, send(): return lax.ppermute(value, ('z', 'xl', 'xh', 'y', 'c'), pairs)  29.8 us
    all_to_all x1, waiting for transfers between devices, on_device(): lax.all_to_all(both, ('z', 'xl'), split_axis=0, concat_axis=0, tiled=True)  11.1 us
    ppermute x5, starting transfers between devices, swap(): return lax.ppermute(value, 'c', [(0, 1), (1, 0)])  10.3 us
    ppermute x22, waiting for transfers between devices, send(): return lax.ppermute(value, ('z', 'xl', 'xh', 'y', 'c'), pairs)  8.74 us
    all_to_all x1, starting transfers between devices, on_device(): lax.all_to_all(both, ('z', 'xl'), split_axis=0, concat_axis=0, tiled=True)  6.8 us
    pallas_call x1, Pallas kernels, on_device(): pl.pallas_call(ready_body, out_shape=[pltpu.HBM((D, D), BF16)] * 3 + [sha...  6.42 us
    all_to_all x1, starting transfers between devices, on_device(): lax.all_to_all(grad_here.reshape(8, 4, 8, D), ('z', 'xl'), split_axis=0,...  3.54 us
  transfers between devices with their start and end apart: 31, of which 12 were waited for; matrix products, arithmetic and copies ran while one was open for 0% of the time, Pallas kernels for 24%

profile of v2, /device:TPU:1, one launch (start us, length us, event | category | flops | bytes accessed | tf_op | source)
XLA Modules:
  0.0 121.4 jit_solution(3740957146559657906)
XLA Ops:
  0.6 2.5 %shard_map.84 = bf16[8,2,4,8,1280]{4,3,2,1,0:T(8,128)(2,1)} custom-call(bf16[4,8,8,1280]{3,2,1,0:T(8,128)(2,1)} %bitcast.17, bf16[4,8,8,1280]{3,2,1,0:T(8,128)(2,1)} %bitcast.18), custom_call_target="tpu_custom_call" | custom-call | tf_op jit(solution)/shard_map/pallas_call | solution.py:431
  3.2 6.8 %all-to-all-start = ((bf16[8,2,4,8,1280]{4,3,2,1,0:T(8,128)(2,1)}), bf16[8,2,4,8,1280]{4,3,2,1,0:T(8,128)(2,1)S(1)}, u32[]{:S(2)}, u32[]{:S(2)}) async-start(bf16[8,2,4,8,1280]{4,3,2,1,0:T(8,128)(2,1)} %shard_map.84), calls=%async_computation | async-start | bytes 2621440 | tf_op jit(solution)/shard_map/all_to_all | solution.py:442
  10.1 6.4 %shard_map.85 = (bf16[1280,1280]{1,0:T(8,128)(2,1)}, bf16[1280,1280]{1,0:T(8,128)(2,1)}, bf16[1280,1280]{1,0:T(8,128)(2,1)}, f32[8,128]{1,0:T(8,128)S(1)}) custom-call(s32[4]{0:T(128)S(1)} %pad_add_fusion.place_ref.refs_0_), custom_call_target="tpu_custom_call" | custom-call | flops 1000000000 | bytes 20000000 | tf_op jit(solution)/shard_map/pallas_call | solution.py:436
  16.5 11.1 %all-to-all-done = bf16[8,2,4,8,1280]{4,3,2,1,0:T(8,128)(2,1)S(1)} async-done(((bf16[8,2,4,8,1280]{4,3,2,1,0:T(8,128)(2,1)}), bf16[8,2,4,8,1280]{4,3,2,1,0:T(8,128)(2,1)S(1)}, u32[]{:S(2)}, u32[]{:S(2)}) %all-to-all-start) | async-done | bytes 1310752 | tf_op jit(solution)/shard_map/all_to_all | solution.py:442
  27.6 6.8 %shard_map.86 = (bf16[256,1280]{1,0:T(8,128)(2,1)S(1)}, bf16[256,3840]{1,0:T(8,128)(2,1)S(1)}, bf16[256,640]{1,0:T(8,128)(2,1)S(1)}, bf16[1280,3840]{1,0:T(8,128...) custom-call(s32[4]{0:T(128)S(1)} %pad_add_fusion.place_ref.refs_0_, ...), custom_call_target="tpu_custom_call" | custom-call | flops 2516582400 | bytes 6341892 | tf_op jit(solution)/shard_map/pallas_call | solution.py:54
  34.5 4.2 %shard_map.87 = (bf16[256,2560]{1,0:T(8,128)(2,1)S(1)}, f32[8,128]{1,0:T(8,128)S(1)}) custom-call(s32[1]{0:T(128)S(6)} %sub.3.refs_0_, bf16[256,3840]{1,0:T(8,128)(2,1)S(1)} %get-tuple-element.89.refs_1_, bf16[8,64,1280]{2,1,0:T(8,128)(2,1)S(1)} %bitcast.11, bf16[1280,1280]{1,0:T(8,128)(2,1)S(1)} %copy-done.2, f32[8,128]{1,0:T(8,128)S(1)} %get-tuple-element.90.refs_4_), custom_call_target="tpu_custom_call" | custom-call | flops 5000000000 | bytes 1966081 | tf_op jit(solution)/shard_map/pallas_call | solution.py:54
  38.7 1.9 %collective-permute-start.2 = (bf16[256,2560]{1,0:T(8,128)(2,1)S(1)}, bf16[256,2560]{1,0:T(8,128)(2,1)S(1)}, u32[]{:S(2)}, u32[]{:S(2)}) collective-permute-start(bf16[256,2560]{1,0:T(8,128)(2,1)S(1)} %get-tuple-element.93.refs_2_.refs_7_), channel_id=1, source_target_pairs={{0,1},{1,0},{2,3},{3,2},{4,5},{5,4},{6,7},{7,6},{8,9},{9,8},{10,11... | collective-permute-start | bytes 3932168 | tf_op jit(solution)/shard_map/ppermute | solution.py:395
  40.6 0.3 collective-permute-start.3
  40.9 4.2 %shard_map.88 = (bf16[256,640]{1,0:T(8,128)(2,1)S(1)}, bf16[256,1920]{1,0:T(8,128)(2,1)S(1)}, f32[8,128]{1,0:T(8,128)S(1)}) custom-call(s32[1]{0:T(128)} %bitcast.3.refs_0_, bf16[256,3840]{1,0:T(8,128)(2,1)S(1)} %get-tuple-element.89.refs_1_, bf16[8,64,1280]{2,1,0:T(8,128)(2,1)S(1)} %bitcast.12, bf16[1280,1280]{1,0:T(8,128)(2,1)S(1)} %copy-done.2, ...), custom_call_target="tpu_custom_call" | custom-call | flops 5000000000 | bytes 1966081 | tf_op jit(solution)/shard_map/pallas_call | solution.py:54
  45.0 0.3 collective-permute-start.1
  45.4 1.9 %shard_map.89 = (bf16[1280,512]{1,0:T(8,128)(2,1)S(1)}, f32[8,128]{1,0:T(8,128)S(1)}) custom-call(bf16[1280,1280]{1,0:T(8,128)(2,1)S(1)} %copy-done.3, bf16[256,1280]{1,0:T(8,128)(2,1)S(1)} %get-tuple-element.99.refs_1_, bf16[256,1280]{1,0:T(8,128)(2,1)S(1)} %collective-permute-done.3.refs_2_, f32[8,128]{1,0:T(8,128)S(1)} %get-tuple-element.100.refs_3_), custom_call_target="tpu_custom_call" | custom-call | flops 1677721600 | bytes 1474560 | tf_op jit(solution)/shard_map/pallas_call | solution.py:54
  47.3 1.5 %shard_map.90 = (bf16[320,1920]{1,0:T(8,128)(2,1)S(1)}, bf16[320,1920]{1,0:T(8,128)(2,1)S(1)}, f32[8,128]{1,0:T(8,128)S(1)}) custom-call(bf16[1280,512]{1,0:T(8,128)(2,1)S(1)} %get-tuple-element.101.refs_0_, bf16[256,1920]{1,0:T(8,128)(2,1)S(1)} %get-tuple-element.92.refs_1_.refs_6_, bf16[256,2560]{1,0:T(8,128)(2,1)S(1)} %collective-permute-done.2.refs_2_.refs_4_, ...), custom_call_target="tpu_custom_call" | custom-call | flops 10000000 | bytes 1515520 | tf_op jit(solution)/shard_map/pallas_call | solution.py:54
  48.8 1.4 %collective-permute-start.6 = (bf16[320,1920]{1,0:T(8,128)(2,1)S(1)}, bf16[320,1920]{1,0:T(8,128)(2,1)S(1)}, u32[]{:S(2)}, u32[]{:S(2)}) collective-permute-start(bf16[320,1920]{1,0:T(8,128)(2,1)S(1)} %get-tuple-element.110), channel_id=1, source_target_pairs={{0,32},{1,3},{2,34},{3,5},{4,36},{5,7},{6,38},{7,1},{8,40},{9,11},... | collective-permute-start | bytes 3686408 | tf_op jit(solution)/shard_map/ppermute | solution.py:391
  50.2 1.5 %collective-permute-start.7 = (bf16[320,1920]{1,0:T(8,128)(2,1)S(1)}, bf16[320,1920]{1,0:T(8,128)(2,1)S(1)}, u32[]{:S(2)}, u32[]{:S(2)}) collective-permute-start(bf16[320,1920]{1,0:T(8,128)(2,1)S(1)} %get-tuple-element.111), channel_id=1, source_target_pairs={{0,96},{1,7},{2,98},{3,1},{4,100},{5,3},{6,102},{7,5},{8,104},{9,1... | collective-permute-start | bytes 3686408 | tf_op jit(solution)/shard_map/ppermute | solution.py:391
  51.7 0.7 collective-permute-start
  52.4 2.2 %shard_map.91 = (bf16[1280,512]{1,0:T(8,128)(2,1)S(1)}, f32[8,128]{1,0:T(8,128)S(1)}) custom-call(bf16[1280,1280]{1,0:T(8,128)(2,1)S(1)} %copy-done.1, bf16[256,640]{1,0:T(8,128)(2,1)S(1)} %get-tuple-element.97.refs_1_, bf16[256,2560]{1,0:T(8,128)(2,1)S(1)} %get-tuple-element.93.refs_2_.refs_7_, bf16[256,640]{1,0:T(8,128)(2,1)S(1)} %collective-permute-done.1.refs_4_.refs_3_, ...), custom_call_target="tpu_custom_call" | custom-call | bytes 1 | tf_op jit(solution)/shard_map/pallas_call | solution.py:54
  54.7 1.2 %shard_map.92 = (bf16[320,640]{1,0:T(8,128)(2,1)S(1)}, bf16[320,640]{1,0:T(8,128)(2,1)S(1)}, f32[8,128]{1,0:T(8,128)S(1)}) custom-call(s32[4]{0:T(128)S(1)} %pad_add_fusion.place_ref.refs_0_, bf16[8,64,1280]{2,1,0:T(8,128)(2,1)S(1)} %bitcast.13, bf16[256,640]{1,0:T(8,128)(2,1)S(1)} %collective-permute-done.refs_2_, ...), custom_call_target="tpu_custom_call" | custom-call | flops 1500000000 | bytes 942084 | tf_op jit(solution)/shard_map/pallas_call | solution.py:54
  55.9 0.6 collective-permute-start.4
  56.5 2.1 %collective-permute-start.5 = (bf16[320,640]{1,0:T(8,128)(2,1)S(1)}, bf16[320,640]{1,0:T(8,128)(2,1)S(1)}, u32[]{:S(2)}, u32[]{:S(2)}) collective-permute-start(bf16[320,640]{1,0:T(8,128)(2,1)S(1)} %get-tuple-element.109), channel_id=1, source_target_pairs={{0,24},{1,25},{2,26},{3,27},{4,28},{5,29},{6,30},{7,31},{8,16},{9,... | collective-permute-start | bytes 1228808 | tf_op jit(solution)/shard_map/ppermute | solution.py:391
  58.7 5.1 %shard_map.93 = (bf16[256,1280]{1,0:T(8,128)(2,1)}, f32[8,384]{1,0:T(8,128)S(1)}, f32[8,384]{1,0:T(8,128)S(1)}, f32[8,128]{1,0:T(8,128)S(1)}) custom-call(s32[4]{0:T(128)S(1)} %pad_add_fusion.place_ref.refs_0_, bf16[8,64,1280]{2,1,0:T(8,128)(2,1)S(1)} %bitcast.14, f32[256,1280]{1,0:T(8,128)S(1)} %get-tuple-element.86.refs_2_, ...), custom_call_target="tpu_custom_call" | custom-call | bytes 1 | tf_op jit(solution)/shard_map/pallas_call | solution.py:54
  63.8 2.3 %collective-permute-done.6.refs_3_ = bf16[320,1920]{1,0:T(8,128)(2,1)S(1)} collective-permute-done((bf16[320,1920]{1,0:T(8,128)(2,1)S(1)}, bf16[320,1920]{1,0:T(8,128)(2,1)S(1)}, u32[]{:S(2)}, u32[]{:S(2)}) %collective-permute-start.6) | collective-permute-done | bytes 1228832 | tf_op jit(solution)/shard_map/ppermute | solution.py:391
  66.1 0.9 shard_map.94
  66.9 1.4 %collective-permute-start.12 = (bf16[160,1920]{1,0:T(8,128)(2,1)S(1)}, bf16[160,1920]{1,0:T(8,128)(2,1)S(1)}, u32[]{:S(2)}, u32[]{:S(2)}) collective-permute-start(bf16[160,1920]{1,0:T(8,128)(2,1)S(1)} %get-tuple-element.125), channel_id=1, source_target_pairs={{0,32},{1,3},{2,34},{3,5},{4,36},{5,7},{6,38},{7,1},{8,40},{9,11},... | collective-permute-start | bytes 1843208 | tf_op jit(solution)/shard_map/ppermute | solution.py:391
  68.3 1.5 %collective-permute-start.13 = (bf16[160,1920]{1,0:T(8,128)(2,1)S(1)}, bf16[160,1920]{1,0:T(8,128)(2,1)S(1)}, u32[]{:S(2)}, u32[]{:S(2)}) collective-permute-start(bf16[160,1920]{1,0:T(8,128)(2,1)S(1)} %get-tuple-element.126), channel_id=1, source_target_pairs={{0,96},{1,7},{2,98},{3,1},{4,100},{5,3},{6,102},{7,5},{8,104},{9,1... | collective-permute-start | bytes 1843208 | tf_op jit(solution)/shard_map/ppermute | solution.py:391
  69.8 1.0 shard_map.95
  70.8 0.6 collective-permute-start.8
  71.4 2.1 %collective-permute-start.9 = (bf16[160,640]{1,0:T(8,128)(2,1)S(1)}, bf16[160,640]{1,0:T(8,128)(2,1)S(1)}, u32[]{:S(2)}, u32[]{:S(2)}) collective-permute-start(bf16[160,640]{1,0:T(8,128)(2,1)S(1)} %get-tuple-element.118), channel_id=1, source_target_pairs={{0,24},{1,25},{2,26},{3,27},{4,28},{5,29},{6,30},{7,31},{8,16},{9,... | collective-permute-start | bytes 614408 | tf_op jit(solution)/shard_map/ppermute | solution.py:391
  73.5 1.2 %collective-permute-start.10 = (f32[8,384]{1,0:T(8,128)S(1)}, f32[8,384]{1,0:T(8,128)S(1)}, u32[]{:S(2)}, u32[]{:S(2)}) collective-permute-start(f32[8,384]{1,0:T(8,128)S(1)} %get-tuple-element.120), channel_id=1, source_target_pairs={{0,8},{8,0},{1,9},{9,1},{2,10},{10,2},{3,11},{11,3},{4,12},{12,4},... | collective-permute-start | bytes 36872 | tf_op jit(solution)/shard_map/ppermute | solution.py:550
  74.8 0.8 shard_map.96
  75.6 1.0 shard_map.97
  76.6 1.1 collective-permute-done.10.refs_1_
  77.7 0.6 collective-permute-start.11
  78.3 1.3 %shard_map.99 = (f32[160,1920]{1,0:T(8,128)S(1)}, f32[80,1920]{1,0:T(8,128)}, f32[80,1920]{1,0:T(8,128)}, f32[8,128]{1,0:T(8,128)S(1)}) custom-call(f32[320,1920]{1,0:T(8,128)S(1)} %get-tuple-element.124.refs_0_, bf16[160,1920]{1,0:T(8,128)(2,1)S(1)} %collective-permute-done.12.refs_1_, bf16[160,1920]{1,0:T(8,128)(2,1)S(1)} %collective-permute-done.13.refs_2_, ...), custom_call_target="tpu_custom_call" | custom-call | flops 10000000 | bytes 1536000 | tf_op jit(solution)/shard_map/pallas_call | solution.py:54
  79.6 0.9 collective-permute-start.14
  80.5 1.8 %collective-permute-start.15 = (f32[80,1920]{1,0:T(8,128)}, f32[80,1920]{1,0:T(8,128)S(1)}, u32[]{:S(2)}, u32[]{:S(2)}) collective-permute-start(f32[80,1920]{1,0:T(8,128)} %get-tuple-element.133), channel_id=1, source_target_pairs={{0,6},{1,25},{2,0},{3,27},{4,2},{5,29},{6,4},{7,31},{8,14},{9,17},... | collective-permute-start | bytes 1843208 | tf_op jit(solution)/shard_map/ppermute | solution.py:391
  82.3 0.8 shard_map.100
  83.1 0.3 collective-permute-start.18
  83.5 2.3 %collective-permute-start.19 = (f32[80,768]{1,0:T(8,128)S(1)}, f32[80,768]{1,0:T(8,128)}, u32[]{:S(2)}, u32[]{:S(2)}) collective-permute-start(f32[80,768]{1,0:T(8,128)S(1)} %get-tuple-element.140), channel_id=1, source_target_pairs={{0,6},{1,7},{2,0},{3,1},{4,2},{5,3},{6,4},{7,5},{8,14},{9,15},{10,... | collective-permute-start | bytes 737288 | tf_op jit(solution)/shard_map/ppermute | solution.py:391
  85.8 3.5 %all-to-all-start.1 = ((bf16[8,4,8,1280]{3,2,1,0:T(8,128)(2,1)}), bf16[8,4,8,1280]{3,2,1,0:T(8,128)(2,1)S(1)}, u32[]{:S(2)}, u32[]{:S(2)}) async-start(bf16[8,4,8,1280]{3,2,1,0:T(8,128)(2,1)} %bitcast.7), calls=%async_computation.1 | async-start | bytes 1310720 | tf_op jit(solution)/shard_map/all_to_all | solution.py:557
  89.4 1.0 collective-permute-done.14.refs_1_
  90.3 0.2 shard_map.102
  90.5 0.5 collective-permute-start.16
  91.0 2.3 %collective-permute-start.17 = (f32[40,1920]{1,0:T(8,128)S(1)}, f32[40,1920]{1,0:T(8,128)S(1)}, u32[]{:S(2)}, u32[]{:S(2)}) collective-permute-start(f32[40,1920]{1,0:T(8,128)S(1)} %get-tuple-element.137), channel_id=1, source_target_pairs={{0,6},{1,25},{2,0},{3,27},{4,2},{5,29},{6,4},{7,31},{8,14},{9,17},... | collective-permute-start | bytes 921608 | tf_op jit(solution)/shard_map/ppermute | solution.py:391
  93.4 1.1 shard_map.103
  94.5 0.1 collective-permute-start.23
  94.6 2.6 %collective-permute-start.24 = (f32[40,768]{1,0:T(8,128)S(1)}, f32[40,768]{1,0:T(8,128)S(1)}, u32[]{:S(2)}, u32[]{:S(2)}) collective-permute-start(f32[40,768]{1,0:T(8,128)S(1)} %get-tuple-element.149), channel_id=1, source_target_pairs={{0,6},{1,7},{2,0},{3,1},{4,2},{5,3},{6,4},{7,5},{8,14},{9,15},{10,... | collective-permute-start | bytes 368648 | tf_op jit(solution)/shard_map/ppermute | solution.py:391
  97.2 1.3 %collective-permute-done.16.refs_1_ = f32[40,1920]{1,0:T(8,128)S(1)} collective-permute-done((f32[40,1920]{1,0:T(8,128)S(1)}, f32[40,1920]{1,0:T(8,128)S(1)}, u32[]{:S(2)}, u32[]{:S(2)}) %collective-permute-start.16) | collective-permute-done | bytes 307232 | tf_op jit(solution)/shard_map/ppermute | solution.py:391
  98.5 1.7 %collective-permute-done.17.refs_2_ = f32[40,1920]{1,0:T(8,128)S(1)} collective-permute-done((f32[40,1920]{1,0:T(8,128)S(1)}, f32[40,1920]{1,0:T(8,128)S(1)}, u32[]{:S(2)}, u32[]{:S(2)}) %collective-permute-start.17) | collective-permute-done | bytes 307232 | tf_op jit(solution)/shard_map/ppermute | solution.py:391
  100.3 1.4 %collective-permute-start.20 = (f32[20,1920]{1,0:T(8,128)S(1)}, f32[20,1920]{1,0:T(8,128)S(1)}, u32[]{:S(2)}, u32[]{:S(2)}) collective-permute-start(f32[20,1920]{1,0:T(8,128)S(1)} %get-tuple-element.144), channel_id=1, source_target_pairs={{0,16},{1,33},{2,18},{3,35},{4,20},{5,37},{6,22},{7,39},{8,24},{9,... | collective-permute-start | bytes 460808 | tf_op jit(solution)/shard_map/ppermute | solution.py:391
  101.7 2.4 %collective-permute-start.21 = (f32[20,1920]{1,0:T(8,128)S(1)}, f32[20,1920]{1,0:T(8,128)S(1)}, u32[]{:S(2)}, u32[]{:S(2)}) collective-permute-start(f32[20,1920]{1,0:T(8,128)S(1)} %get-tuple-element.145), channel_id=1, source_target_pairs={{0,8},{1,65},{2,10},{3,67},{4,12},{5,69},{6,14},{7,71},{8,0},{9,73... | collective-permute-start | bytes 460808 | tf_op jit(solution)/shard_map/ppermute | solution.py:391
  104.1 1.2 collective-permute-start.22
  105.3 0.4 collective-permute-start.25
  105.6 0.9 collective-permute-start.26
  106.5 0.1 collective-permute-done.20.refs_1_
  106.6 1.5 %collective-permute-start.27 = (f32[20,768]{1,0:T(8,128)S(1)}, f32[20,768]{1,0:T(8,128)S(1)}, u32[]{:S(2)}, u32[]{:S(2)}) collective-permute-start(f32[20,768]{1,0:T(8,128)S(1)} %get-tuple-element.158), channel_id=1, source_target_pairs={{0,96},{1,97},{2,98},{3,99},{4,100},{5,101},{6,102},{7,103},{8,104... | collective-permute-start | bytes 184328 | tf_op jit(solution)/shard_map/ppermute | solution.py:391
  108.1 0.8 collective-permute-done.21.refs_2_
  109.0 0.9 shard_map.107
  109.9 0.1 collective-permute-done.25.refs_3_
  110.0 0.8 collective-permute-done.26.refs_4_
  110.8 0.6 collective-permute-done.27.refs_5_
  111.4 0.6 shard_map.108
  112.0 7.1 %collective-permute-start.28 = (f32[10,2688]{1,0:T(8,128)S(1)}, f32[10,2688]{1,0:T(8,128)S(1)}, u32[]{:S(2)}, u32[]{:S(2)}) collective-permute-start(f32[10,2688]{1,0:T(8,128)S(1)} %get-tuple-element.161), channel_id=1, source_target_pairs={{0,1},{1,0},{2,3},{3,2},{4,5},{5,4},{6,7},{7,6},{8,9},{9,8},{10,11... | collective-permute-start | bytes 322568 | tf_op jit(solution)/shard_map/ppermute | solution.py:395
  119.1 1.0 collective-permute-done.28.refs_2_
  120.1 1.3 %shard_map.109 = (f32[10,3840]{1,0:T(8,128)}, f32[10,1280]{1,0:T(8,128)}, f32[1,10]{1,0:T(1,128)}) custom-call(s32[4]{0:T(128)S(1)} %pad_add_fusion.place_ref.refs_0_, f32[10,2688]{1,0:T(8,128)S(1)} %get-tuple-element.160.refs_1_, f32[10,2688]{1,0:T(8,128)S(1)} %collective-permute-done.28.refs_2_, f32[8,128]{1,0:T(8,128)S(1)} %get-tuple-element.162.refs_3_), custom_call_target="tpu_custom_call" | custom-call | bytes 1 | tf_op jit(solution)/shard_map/pallas_call | solution.py:54
  (40 shorter events, 0.4 us)
Async XLA Ops:
  3.2 6.8 %copy-start.6 = (f32[1280]{0:T(1024)S(1)}, f32[1280]{0:T(1024)}, u32[]{:S(2)}) copy-start(f32[1280]{0:T(1024)} %param.7) | copy-start | bytes 15364
  3.2 24.4 %all-to-all-start = ((bf16[8,2,4,8,1280]{4,3,2,1,0:T(8,128)(2,1)}), bf16[8,2,4,8,1280]{4,3,2,1,0:T(8,128)(2,1)S(1)}, u32[]{:S(2)}, u32[]{:S(2)}) async-start(bf16[8,2,4,8,1280]{4,3,2,1,0:T(8,128)(2,1)} %shard_map.84), calls=%async_computation | async-start | bytes 2621440 | tf_op jit(solution)/shard_map/all_to_all | solution.py:442
  27.6 6.9 %copy-start.2 = (bf16[1280,1280]{1,0:T(8,128)(2,1)S(1)}, bf16[1280,1280]{1,0:T(8,128)(2,1)}, u32[]{:S(2)}) copy-start(bf16[1280,1280]{1,0:T(8,128)(2,1)} %refs_3_.5) | copy-start | bytes 9830404
  38.7 8.6 %collective-permute-start.2 = (bf16[256,2560]{1,0:T(8,128)(2,1)S(1)}, bf16[256,2560]{1,0:T(8,128)(2,1)S(1)}, u32[]{:S(2)}, u32[]{:S(2)}) collective-permute-start(bf16[256,2560]{1,0:T(8,128)(2,1)S(1)} %get-tuple-element.93.refs_2_.refs_7_), channel_id=1, source_target_pairs={{0,1},{1,0},{2,3},{3,2},{4,5},{5,4},{6,7},{7,6},{8,9},{9,8},{10,11... | collective-permute-start | bytes 3932168 | tf_op jit(solution)/shard_map/ppermute | solution.py:395
  40.6 4.8 %collective-permute-start.3 = (bf16[256,1280]{1,0:T(8,128)(2,1)S(1)}, bf16[256,1280]{1,0:T(8,128)(2,1)S(1)}, u32[]{:S(2)}, u32[]{:S(2)}) collective-permute-start(bf16[256,1280]{1,0:T(8,128)(2,1)S(1)} %get-tuple-element.99.refs_1_), channel_id=1, source_target_pairs={{0,1},{1,0},{2,3},{3,2},{4,5},{5,4},{6,7},{7,6},{8,9},{9,8},{10,11... | collective-permute-start | bytes 1966088 | tf_op jit(solution)/shard_map/ppermute | solution.py:395
  40.9 4.5 %copy-start.3 = (bf16[1280,1280]{1,0:T(8,128)(2,1)S(1)}, bf16[1280,1280]{1,0:T(8,128)(2,1)}, u32[]{:S(2)}) copy-start(bf16[1280,1280]{1,0:T(8,128)(2,1)} %get-tuple-element.98.refs_0_) | copy-start | bytes 9830404
  45.0 2.2 %collective-permute-start.1 = (bf16[256,640]{1,0:T(8,128)(2,1)S(1)}, bf16[256,640]{1,0:T(8,128)(2,1)S(1)}, u32[]{:S(2)}, u32[]{:S(2)}) collective-permute-start(bf16[256,640]{1,0:T(8,128)(2,1)S(1)} %get-tuple-element.97.refs_1_), channel_id=1, source_target_pairs={{0,1},{1,0},{2,3},{3,2},{4,5},{5,4},{6,7},{7,6},{8,9},{9,8},{10,11... | collective-permute-start | bytes 983048 | tf_op jit(solution)/shard_map/ppermute | solution.py:395
  47.3 5.1 %copy-start.1 = (bf16[1280,1280]{1,0:T(8,128)(2,1)S(1)}, bf16[1280,1280]{1,0:T(8,128)(2,1)}, u32[]{:S(2)}) copy-start(bf16[1280,1280]{1,0:T(8,128)(2,1)} %get-tuple-element.96.refs_0_) | copy-start | bytes 9830404
  48.8 17.2 %collective-permute-start.6 = (bf16[320,1920]{1,0:T(8,128)(2,1)S(1)}, bf16[320,1920]{1,0:T(8,128)(2,1)S(1)}, u32[]{:S(2)}, u32[]{:S(2)}) collective-permute-start(bf16[320,1920]{1,0:T(8,128)(2,1)S(1)} %get-tuple-element.110), channel_id=1, source_target_pairs={{0,32},{1,3},{2,34},{3,5},{4,36},{5,7},{6,38},{7,1},{8,40},{9,11},... | collective-permute-start | bytes 3686408 | tf_op jit(solution)/shard_map/ppermute | solution.py:391
  50.2 15.9 %collective-permute-start.7 = (bf16[320,1920]{1,0:T(8,128)(2,1)S(1)}, bf16[320,1920]{1,0:T(8,128)(2,1)S(1)}, u32[]{:S(2)}, u32[]{:S(2)}) collective-permute-start(bf16[320,1920]{1,0:T(8,128)(2,1)S(1)} %get-tuple-element.111), channel_id=1, source_target_pairs={{0,96},{1,7},{2,98},{3,1},{4,100},{5,3},{6,102},{7,5},{8,104},{9,1... | collective-permute-start | bytes 3686408 | tf_op jit(solution)/shard_map/ppermute | solution.py:391
  51.7 2.9 %collective-permute-start = (bf16[256,640]{1,0:T(8,128)(2,1)S(1)}, bf16[256,640]{1,0:T(8,128)(2,1)S(1)}, u32[]{:S(2)}, u32[]{:S(2)}) collective-permute-start(bf16[256,640]{1,0:T(8,128)(2,1)S(1)} %get-tuple-element.95), channel_id=1, source_target_pairs={{0,1},{1,0},{2,3},{3,2},{4,5},{5,4},{6,7},{7,6},{8,9},{9,8},{10,11... | collective-permute-start | bytes 983048 | tf_op jit(solution)/shard_map/ppermute | solution.py:395
  54.7 4.0 %copy-start = (bf16[1280,1280]{1,0:T(8,128)(2,1)S(1)}, bf16[1280,1280]{1,0:T(8,128)(2,1)}, u32[]{:S(2)}) copy-start(bf16[1280,1280]{1,0:T(8,128)(2,1)} %get-tuple-element.94.refs_8_) | copy-start | bytes 9830404
  55.9 13.9 %collective-permute-start.4 = (bf16[320,640]{1,0:T(8,128)(2,1)S(1)}, bf16[320,640]{1,0:T(8,128)(2,1)S(1)}, u32[]{:S(2)}, u32[]{:S(2)}) collective-permute-start(bf16[320,640]{1,0:T(8,128)(2,1)S(1)} %get-tuple-element.108), channel_id=1, source_target_pairs={{0,16},{1,17},{2,18},{3,19},{4,20},{5,21},{6,22},{7,23},{8,24},{9,... | collective-permute-start | bytes 1228808 | tf_op jit(solution)/shard_map/ppermute | solution.py:391
  56.5 13.3 %collective-permute-start.5 = (bf16[320,640]{1,0:T(8,128)(2,1)S(1)}, bf16[320,640]{1,0:T(8,128)(2,1)S(1)}, u32[]{:S(2)}, u32[]{:S(2)}) collective-permute-start(bf16[320,640]{1,0:T(8,128)(2,1)S(1)} %get-tuple-element.109), channel_id=1, source_target_pairs={{0,24},{1,25},{2,26},{3,27},{4,28},{5,29},{6,30},{7,31},{8,16},{9,... | collective-permute-start | bytes 1228808 | tf_op jit(solution)/shard_map/ppermute | solution.py:391
  66.9 11.4 %collective-permute-start.12 = (bf16[160,1920]{1,0:T(8,128)(2,1)S(1)}, bf16[160,1920]{1,0:T(8,128)(2,1)S(1)}, u32[]{:S(2)}, u32[]{:S(2)}) collective-permute-start(bf16[160,1920]{1,0:T(8,128)(2,1)S(1)} %get-tuple-element.125), channel_id=1, source_target_pairs={{0,32},{1,3},{2,34},{3,5},{4,36},{5,7},{6,38},{7,1},{8,40},{9,11},... | collective-permute-start | bytes 1843208 | tf_op jit(solution)/shard_map/ppermute | solution.py:391
  68.3 10.0 %collective-permute-start.13 = (bf16[160,1920]{1,0:T(8,128)(2,1)S(1)}, bf16[160,1920]{1,0:T(8,128)(2,1)S(1)}, u32[]{:S(2)}, u32[]{:S(2)}) collective-permute-start(bf16[160,1920]{1,0:T(8,128)(2,1)S(1)} %get-tuple-element.126), channel_id=1, source_target_pairs={{0,96},{1,7},{2,98},{3,1},{4,100},{5,3},{6,102},{7,5},{8,104},{9,1... | collective-permute-start | bytes 1843208 | tf_op jit(solution)/shard_map/ppermute | solution.py:391
  70.8 11.5 %collective-permute-start.8 = (bf16[160,640]{1,0:T(8,128)(2,1)S(1)}, bf16[160,640]{1,0:T(8,128)(2,1)S(1)}, u32[]{:S(2)}, u32[]{:S(2)}) collective-permute-start(bf16[160,640]{1,0:T(8,128)(2,1)S(1)} %get-tuple-element.117), channel_id=1, source_target_pairs={{0,16},{1,17},{2,18},{3,19},{4,20},{5,21},{6,22},{7,23},{8,24},{9,... | collective-permute-start | bytes 614408 | tf_op jit(solution)/shard_map/ppermute | solution.py:391
  71.4 10.9 %collective-permute-start.9 = (bf16[160,640]{1,0:T(8,128)(2,1)S(1)}, bf16[160,640]{1,0:T(8,128)(2,1)S(1)}, u32[]{:S(2)}, u32[]{:S(2)}) collective-permute-start(bf16[160,640]{1,0:T(8,128)(2,1)S(1)} %get-tuple-element.118), channel_id=1, source_target_pairs={{0,24},{1,25},{2,26},{3,27},{4,28},{5,29},{6,30},{7,31},{8,16},{9,... | collective-permute-start | bytes 614408 | tf_op jit(solution)/shard_map/ppermute | solution.py:391
  73.5 4.2 %collective-permute-start.10 = (f32[8,384]{1,0:T(8,128)S(1)}, f32[8,384]{1,0:T(8,128)S(1)}, u32[]{:S(2)}, u32[]{:S(2)}) collective-permute-start(f32[8,384]{1,0:T(8,128)S(1)} %get-tuple-element.120), channel_id=1, source_target_pairs={{0,8},{8,0},{1,9},{9,1},{2,10},{10,2},{3,11},{11,3},{4,12},{12,4},... | collective-permute-start | bytes 36872 | tf_op jit(solution)/shard_map/ppermute | solution.py:550
  77.7 4.6 %collective-permute-start.11 = (f32[8,384]{1,0:T(8,128)S(1)}, f32[8,384]{1,0:T(8,128)S(1)}, u32[]{:S(2)}, u32[]{:S(2)}) collective-permute-start(f32[8,384]{1,0:T(8,128)S(1)} %get-tuple-element.123), channel_id=1, source_target_pairs={{0,16},{16,0},{1,17},{17,1},{2,18},{18,2},{3,19},{19,3},{4,20},{20... | collective-permute-start | bytes 36872 | tf_op jit(solution)/shard_map/ppermute | solution.py:554
  79.6 10.7 %collective-permute-start.14 = (f32[80,1920]{1,0:T(8,128)}, f32[80,1920]{1,0:T(8,128)S(1)}, u32[]{:S(2)}, u32[]{:S(2)}) collective-permute-start(f32[80,1920]{1,0:T(8,128)} %get-tuple-element.132), channel_id=1, source_target_pairs={{0,2},{1,17},{2,4},{3,19},{4,6},{5,21},{6,0},{7,23},{8,10},{9,25},... | collective-permute-start | bytes 1843208 | tf_op jit(solution)/shard_map/ppermute | solution.py:391
  80.5 9.8 %collective-permute-start.15 = (f32[80,1920]{1,0:T(8,128)}, f32[80,1920]{1,0:T(8,128)S(1)}, u32[]{:S(2)}, u32[]{:S(2)}) collective-permute-start(f32[80,1920]{1,0:T(8,128)} %get-tuple-element.133), channel_id=1, source_target_pairs={{0,6},{1,25},{2,0},{3,27},{4,2},{5,29},{6,4},{7,31},{8,14},{9,17},... | collective-permute-start | bytes 1843208 | tf_op jit(solution)/shard_map/ppermute | solution.py:391
  83.1 2.7 %copy-start.4 = (f32[160,768]{1,0:T(8,128)}, f32[160,768]{1,0:T(8,128)S(1)}, u32[]{:S(2)}) copy-start(f32[160,768]{1,0:T(8,128)S(1)} %get-tuple-element.138.refs_0_) | copy-start | bytes 1474564
  83.1 10.2 %collective-permute-start.18 = (f32[80,768]{1,0:T(8,128)}, f32[80,768]{1,0:T(8,128)}, u32[]{:S(2)}, u32[]{:S(2)}) collective-permute-start(f32[80,768]{1,0:T(8,128)} %get-tuple-element.139), channel_id=1, source_target_pairs={{0,2},{1,3},{2,4},{3,5},{4,6},{5,7},{6,0},{7,1},{8,10},{9,11},{10,... | collective-permute-start | bytes 737288 | tf_op jit(solution)/shard_map/ppermute | solution.py:391
  83.5 9.9 %collective-permute-start.19 = (f32[80,768]{1,0:T(8,128)S(1)}, f32[80,768]{1,0:T(8,128)}, u32[]{:S(2)}, u32[]{:S(2)}) collective-permute-start(f32[80,768]{1,0:T(8,128)S(1)} %get-tuple-element.140), channel_id=1, source_target_pairs={{0,6},{1,7},{2,0},{3,1},{4,2},{5,3},{6,4},{7,5},{8,14},{9,15},{10,... | collective-permute-start | bytes 737288 | tf_op jit(solution)/shard_map/ppermute | solution.py:391
  85.8 23.2 %all-to-all-start.1 = ((bf16[8,4,8,1280]{3,2,1,0:T(8,128)(2,1)}), bf16[8,4,8,1280]{3,2,1,0:T(8,128)(2,1)S(1)}, u32[]{:S(2)}, u32[]{:S(2)}) async-start(bf16[8,4,8,1280]{3,2,1,0:T(8,128)(2,1)} %bitcast.7), calls=%async_computation.1 | async-start | bytes 1310720 | tf_op jit(solution)/shard_map/all_to_all | solution.py:557
  89.4 4.0 %copy-start.5 = (f32[160,768]{1,0:T(8,128)S(1)}, f32[160,768]{1,0:T(8,128)}, u32[]{:S(2)}) copy-start(f32[160,768]{1,0:T(8,128)} %copy-done.4) | copy-start | bytes 1474564
  90.5 8.0 %collective-permute-start.16 = (f32[40,1920]{1,0:T(8,128)S(1)}, f32[40,1920]{1,0:T(8,128)S(1)}, u32[]{:S(2)}, u32[]{:S(2)}) collective-permute-start(f32[40,1920]{1,0:T(8,128)S(1)} %get-tuple-element.136), channel_id=1, source_target_pairs={{0,2},{1,17},{2,4},{3,19},{4,6},{5,21},{6,0},{7,23},{8,10},{9,25},... | collective-permute-start | bytes 921608 | tf_op jit(solution)/shard_map/ppermute | solution.py:391
  91.0 9.2 %collective-permute-start.17 = (f32[40,1920]{1,0:T(8,128)S(1)}, f32[40,1920]{1,0:T(8,128)S(1)}, u32[]{:S(2)}, u32[]{:S(2)}) collective-permute-start(f32[40,1920]{1,0:T(8,128)S(1)} %get-tuple-element.137), channel_id=1, source_target_pairs={{0,6},{1,25},{2,0},{3,27},{4,2},{5,29},{6,4},{7,31},{8,14},{9,17},... | collective-permute-start | bytes 921608 | tf_op jit(solution)/shard_map/ppermute | solution.py:391
  94.5 10.7 %collective-permute-start.23 = (f32[40,768]{1,0:T(8,128)S(1)}, f32[40,768]{1,0:T(8,128)S(1)}, u32[]{:S(2)}, u32[]{:S(2)}) collective-permute-start(f32[40,768]{1,0:T(8,128)S(1)} %get-tuple-element.148), channel_id=1, source_target_pairs={{0,2},{1,3},{2,4},{3,5},{4,6},{5,7},{6,0},{7,1},{8,10},{9,11},{10,... | collective-permute-start | bytes 368648 | tf_op jit(solution)/shard_map/ppermute | solution.py:391
  94.6 10.6 %collective-permute-start.24 = (f32[40,768]{1,0:T(8,128)S(1)}, f32[40,768]{1,0:T(8,128)S(1)}, u32[]{:S(2)}, u32[]{:S(2)}) collective-permute-start(f32[40,768]{1,0:T(8,128)S(1)} %get-tuple-element.149), channel_id=1, source_target_pairs={{0,6},{1,7},{2,0},{3,1},{4,2},{5,3},{6,4},{7,5},{8,14},{9,15},{10,... | collective-permute-start | bytes 368648 | tf_op jit(solution)/shard_map/ppermute | solution.py:391
  100.3 6.3 %collective-permute-start.20 = (f32[20,1920]{1,0:T(8,128)S(1)}, f32[20,1920]{1,0:T(8,128)S(1)}, u32[]{:S(2)}, u32[]{:S(2)}) collective-permute-start(f32[20,1920]{1,0:T(8,128)S(1)} %get-tuple-element.144), channel_id=1, source_target_pairs={{0,16},{1,33},{2,18},{3,35},{4,20},{5,37},{6,22},{7,39},{8,24},{9,... | collective-permute-start | bytes 460808 | tf_op jit(solution)/shard_map/ppermute | solution.py:391
  101.7 7.3 %collective-permute-start.21 = (f32[20,1920]{1,0:T(8,128)S(1)}, f32[20,1920]{1,0:T(8,128)S(1)}, u32[]{:S(2)}, u32[]{:S(2)}) collective-permute-start(f32[20,1920]{1,0:T(8,128)S(1)} %get-tuple-element.145), channel_id=1, source_target_pairs={{0,8},{1,65},{2,10},{3,67},{4,12},{5,69},{6,14},{7,71},{8,0},{9,73... | collective-permute-start | bytes 460808 | tf_op jit(solution)/shard_map/ppermute | solution.py:391
  104.1 4.9 %collective-permute-start.22 = (f32[20,1920]{1,0:T(8,128)S(1)}, f32[20,1920]{1,0:T(8,128)S(1)}, u32[]{:S(2)}, u32[]{:S(2)}) collective-permute-start(f32[20,1920]{1,0:T(8,128)S(1)} %get-tuple-element.146), channel_id=1, source_target_pairs={{0,24},{1,97},{2,26},{3,99},{4,28},{5,101},{6,30},{7,103},{8,16},{... | collective-permute-start | bytes 460808 | tf_op jit(solution)/shard_map/ppermute | solution.py:391
  105.3 4.8 %collective-permute-start.25 = (f32[20,768]{1,0:T(8,128)S(1)}, f32[20,768]{1,0:T(8,128)S(1)}, u32[]{:S(2)}, u32[]{:S(2)}) collective-permute-start(f32[20,768]{1,0:T(8,128)S(1)} %get-tuple-element.156), channel_id=1, source_target_pairs={{0,32},{1,33},{2,34},{3,35},{4,36},{5,37},{6,38},{7,39},{8,40},{9,... | collective-permute-start | bytes 184328 | tf_op jit(solution)/shard_map/ppermute | solution.py:391
  105.6 5.2 %collective-permute-start.26 = (f32[20,768]{1,0:T(8,128)S(1)}, f32[20,768]{1,0:T(8,128)S(1)}, u32[]{:S(2)}, u32[]{:S(2)}) collective-permute-start(f32[20,768]{1,0:T(8,128)S(1)} %get-tuple-element.157), channel_id=1, source_target_pairs={{0,64},{1,65},{2,66},{3,67},{4,68},{5,69},{6,70},{7,71},{8,72},{9,... | collective-permute-start | bytes 184328 | tf_op jit(solution)/shard_map/ppermute | solution.py:391
  106.6 4.8 %collective-permute-start.27 = (f32[20,768]{1,0:T(8,128)S(1)}, f32[20,768]{1,0:T(8,128)S(1)}, u32[]{:S(2)}, u32[]{:S(2)}) collective-permute-start(f32[20,768]{1,0:T(8,128)S(1)} %get-tuple-element.158), channel_id=1, source_target_pairs={{0,96},{1,97},{2,98},{3,99},{4,100},{5,101},{6,102},{7,103},{8,104... | collective-permute-start | bytes 184328 | tf_op jit(solution)/shard_map/ppermute | solution.py:391
  112.0 8.1 %collective-permute-start.28 = (f32[10,2688]{1,0:T(8,128)S(1)}, f32[10,2688]{1,0:T(8,128)S(1)}, u32[]{:S(2)}, u32[]{:S(2)}) collective-permute-start(f32[10,2688]{1,0:T(8,128)S(1)} %get-tuple-element.161), channel_id=1, source_target_pairs={{0,1},{1,0},{2,3},{3,2},{4,5},{5,4},{6,7},{7,6},{8,9},{9,8},{10,11... | collective-permute-start | bytes 322568 | tf_op jit(solution)/shard_map/ppermute | solution.py:395

commit v3 on v2

--- a/solution.py
+++ b/solution.py
@@ -108,14 +108,15 @@
     return pl.ds(pl.multiple_of(core * HALF, 128), HALF)
 
 
-def forward_body(place_ref, both_ref, gain_ref, weight_ref, gained_ref, qkv_ref, cot_ref,
-                 held_ref, hat_ref, inv_ref, sems):
+def forward_body(place_ref, both_ref, gain_ref, weight_ref, out_weight_ref, gained_ref, qkv_ref, cot_ref,
+                 held_ref, hat_ref, inv_ref, out_held_ref, sems):
     pieces = [slice(step * HALF, (step + 1) * HALF) for step in range(6)]
     copies = [
         pltpu.make_async_copy(weight_ref.at[:, piece], held_ref.at[:, piece], sems.at[step])
         for step, piece in enumerate(pieces)
     ]
-    for copy in copies[:2]:
+    copies.append(pltpu.make_async_copy(out_weight_ref, out_held_ref, sems.at[6]))
+    for copy in copies[:3]:
         copy.start()
     normalized, inv_std = normalize(both_ref)
     hat_ref[...] = normalized
@@ -125,9 +126,10 @@
     cot_ref[...] = side(both_ref, 1, half(place_ref, False))
     for step, (copy, piece) in enumerate(zip(copies, pieces)):
         copy.wait()
-        if step + 2 < len(copies):
-            copies[step + 2].start()
+        if step + 3 < len(copies):
+            copies[step + 3].start()
         qkv_ref[:, piece] = dot(gained, held_ref[:, piece]).astype(BF16)
+    copies[6].wait()
 
 
 def attention_body(group_ref, qkv_ref, both_ref, weight_ref, att_ref, stack_ref, ag_ref,
@@ -441,19 +443,19 @@
     )(place)
     both = lax.all_to_all(both, ("z", "xl"), split_axis=0, concat_axis=0, tiled=True)
     both = both.reshape(8, 64, D)
-    (gained, qkv, cot_other, weight, hat, inv_std), token = call(
+    (gained, qkv, cot_other, weight, hat, inv_std, held_out), token = call(
         forward_body,
         [shape(TOKENS, D), shape(TOKENS, 3 * D), shape(TOKENS, HALF), shape(D, 3 * D),
-         shape(TOKENS, D, F32), shape(TOKENS, 128, F32)],
-        [place, both, gain_row, qkv_weight], scalars=1, flops=2 * TOKENS * D * 3 * D,
-        scratch=[pltpu.SemaphoreType.DMA((6,))], hbm=(3,), after=[token],
+         shape(TOKENS, D, F32), shape(TOKENS, 128, F32), shape(D, D)],
+        [place, both, gain_row, qkv_weight, out_weight], scalars=1, flops=2 * TOKENS * D * 3 * D,
+        scratch=[pltpu.SemaphoreType.DMA((7,))], hbm=(3, 4), after=[token],
     )
     their_gained, their_cot = swap(gained), swap(cot_other)
 
     def attention(which, after, outs):
         return call(
             attention_body if len(outs) == 2 else joint_attention_body, outs,
-            [which, qkv, both, out_weight], scalars=1, flops=5 * 10**9,
+            [which, qkv, both, held_out], scalars=1, flops=5 * 10**9,
             scratch=[pltpu.VMEM((TOKENS, HALF), BF16), pltpu.VMEM((TOKENS, TOKENS), F32)],
             after=after,
         )

time: 122 us -> 121 us (level)
  no operation moved by 1% of the time
where the time goes in v3:
time: 121 us
  starting transfers between devices  52.3 us (43%)
  Pallas kernels  45.7 us (38%)
  waiting for transfers between devices  22 us (18%)
    pallas_call x22, Pallas kernels, call(): pl.pallas_call(run, out_shape=[results(o.shape, o.dtype) for o in outs] +...  35.9 us
    ppermute x22, starting transfers between devices, send(): return lax.ppermute(value, ('z', 'xl', 'xh', 'y', 'c'), pairs)  29.8 us
    all_to_all x1, waiting for transfers between devices, on_device(): lax.all_to_all(both, ('z', 'xl'), split_axis=0, concat_axis=0, tiled=True)  11.1 us
    ppermute x5, starting transfers between devices, swap(): return lax.ppermute(value, 'c', [(0, 1), (1, 0)])  10.3 us
    ppermute x22, waiting for transfers between devices, send(): return lax.ppermute(value, ('z', 'xl', 'xh', 'y', 'c'), pairs)  8.73 us
    all_to_all x1, starting transfers between devices, on_device(): lax.all_to_all(both, ('z', 'xl'), split_axis=0, concat_axis=0, tiled=True)  6.8 us
    pallas_call x1, Pallas kernels, on_device(): pl.pallas_call(ready_body, out_shape=[pltpu.HBM((D, D), BF16)] * 3 + [sha...  6.42 us
    all_to_all x1, starting transfers between devices, on_device(): lax.all_to_all(grad_here.reshape(8, 4, 8, D), ('z', 'xl'), split_axis=0,...  3.54 us
  transfers between devices with their start and end apart: 31, of which 12 were waited for; matrix products, arithmetic and copies ran while one was open for 0% of the time, Pallas kernels for 24%

profile of v3, /device:TPU:1, one launch (start us, length us, event | category | flops | bytes accessed | tf_op | source)
XLA Modules:
  0.0 120.9 jit_solution(15539158727439219456)
XLA Ops:
  0.6 2.5 %shard_map.84 = bf16[8,2,4,8,1280]{4,3,2,1,0:T(8,128)(2,1)} custom-call(bf16[4,8,8,1280]{3,2,1,0:T(8,128)(2,1)} %bitcast.17, bf16[4,8,8,1280]{3,2,1,0:T(8,128)(2,1)} %bitcast.18), custom_call_target="tpu_custom_call" | custom-call | tf_op jit(solution)/shard_map/pallas_call | solution.py:433
  3.2 6.8 %all-to-all-start = ((bf16[8,2,4,8,1280]{4,3,2,1,0:T(8,128)(2,1)}), bf16[8,2,4,8,1280]{4,3,2,1,0:T(8,128)(2,1)S(1)}, u32[]{:S(2)}, u32[]{:S(2)}) async-start(bf16[8,2,4,8,1280]{4,3,2,1,0:T(8,128)(2,1)} %shard_map.84), calls=%async_computation | async-start | bytes 2621440 | tf_op jit(solution)/shard_map/all_to_all | solution.py:444
  10.1 6.4 %shard_map.85 = (bf16[1280,1280]{1,0:T(8,128)(2,1)}, bf16[1280,1280]{1,0:T(8,128)(2,1)}, bf16[1280,1280]{1,0:T(8,128)(2,1)}, f32[8,128]{1,0:T(8,128)S(1)}) custom-call(s32[4]{0:T(128)S(1)} %pad_add_fusion.place_ref.refs_0_), custom_call_target="tpu_custom_call" | custom-call | flops 1000000000 | bytes 20000000 | tf_op jit(solution)/shard_map/pallas_call | solution.py:438
  16.5 11.1 %all-to-all-done = bf16[8,2,4,8,1280]{4,3,2,1,0:T(8,128)(2,1)S(1)} async-done(((bf16[8,2,4,8,1280]{4,3,2,1,0:T(8,128)(2,1)}), bf16[8,2,4,8,1280]{4,3,2,1,0:T(8,128)(2,1)S(1)}, u32[]{:S(2)}, u32[]{:S(2)}) %all-to-all-start) | async-done | bytes 1310752 | tf_op jit(solution)/shard_map/all_to_all | solution.py:444
  27.6 6.3 %shard_map.86 = (bf16[256,1280]{1,0:T(8,128)(2,1)S(1)}, bf16[256,3840]{1,0:T(8,128)(2,1)S(1)}, bf16[256,640]{1,0:T(8,128)(2,1)S(1)}, bf16[1280,3840]{1,0:T(8,128...) custom-call(s32[4]{0:T(128)S(1)} %pad_add_fusion.place_ref.refs_0_, ...), custom_call_target="tpu_custom_call" | custom-call | flops 2516582400 | bytes 7980292 | tf_op jit(solution)/shard_map/pallas_call | solution.py:54
  34.0 4.2 %shard_map.87 = (bf16[256,2560]{1,0:T(8,128)(2,1)S(1)}, f32[8,128]{1,0:T(8,128)S(1)}) custom-call(s32[1]{0:T(128)S(6)} %sub.3.refs_0_, bf16[256,3840]{1,0:T(8,128)(2,1)S(1)} %get-tuple-element.90.refs_1_, bf16[8,64,1280]{2,1,0:T(8,128)(2,1)S(1)} %bitcast.11, bf16[1280,1280]{1,0:T(8,128)(2,1)S(1)} %get-tuple-element.91.refs_3_, ...), custom_call_target="tpu_custom_call" | custom-call | flops 5000000000 | bytes 1966081 | tf_op jit(solution)/shard_map/pallas_call | solution.py:54
  38.1 1.9 %collective-permute-start.2 = (bf16[256,2560]{1,0:T(8,128)(2,1)S(1)}, bf16[256,2560]{1,0:T(8,128)(2,1)S(1)}, u32[]{:S(2)}, u32[]{:S(2)}) collective-permute-start(bf16[256,2560]{1,0:T(8,128)(2,1)S(1)} %get-tuple-element.95.refs_2_.refs_7_), channel_id=1, source_target_pairs={{0,1},{1,0},{2,3},{3,2},{4,5},{5,4},{6,7},{7,6},{8,9},{9,8},{10,11... | collective-permute-start | bytes 3932168 | tf_op jit(solution)/shard_map/ppermute | solution.py:397
  40.1 0.3 collective-permute-start.3
  40.4 4.2 %shard_map.88 = (bf16[256,640]{1,0:T(8,128)(2,1)S(1)}, bf16[256,1920]{1,0:T(8,128)(2,1)S(1)}, f32[8,128]{1,0:T(8,128)S(1)}) custom-call(s32[1]{0:T(128)} %bitcast.3.refs_0_, bf16[256,3840]{1,0:T(8,128)(2,1)S(1)} %get-tuple-element.90.refs_1_, bf16[8,64,1280]{2,1,0:T(8,128)(2,1)S(1)} %bitcast.12, bf16[1280,1280]{1,0:T(8,128)(2,1)S(1)} %get-tuple-element.91.refs_3_, ...), custom_call_target="tpu_custom_call" | custom-call | flops 5000000000 | bytes 1966081 | tf_op jit(solution)/shard_map/pallas_call | solution.py:54
  44.5 0.3 collective-permute-start.1
  44.8 1.9 %shard_map.89 = (bf16[1280,512]{1,0:T(8,128)(2,1)S(1)}, f32[8,128]{1,0:T(8,128)S(1)}) custom-call(bf16[1280,1280]{1,0:T(8,128)(2,1)S(1)} %copy-done.2, bf16[256,1280]{1,0:T(8,128)(2,1)S(1)} %get-tuple-element.101.refs_1_, bf16[256,1280]{1,0:T(8,128)(2,1)S(1)} %collective-permute-done.3.refs_2_, f32[8,128]{1,0:T(8,128)S(1)} %get-tuple-element.102.refs_3_), custom_call_target="tpu_custom_call" | custom-call | flops 1677721600 | bytes 1474560 | tf_op jit(solution)/shard_map/pallas_call | solution.py:54
  46.8 1.5 %shard_map.90 = (bf16[320,1920]{1,0:T(8,128)(2,1)S(1)}, bf16[320,1920]{1,0:T(8,128)(2,1)S(1)}, f32[8,128]{1,0:T(8,128)S(1)}) custom-call(bf16[1280,512]{1,0:T(8,128)(2,1)S(1)} %get-tuple-element.103.refs_0_, bf16[256,1920]{1,0:T(8,128)(2,1)S(1)} %get-tuple-element.94.refs_1_.refs_6_, bf16[256,2560]{1,0:T(8,128)(2,1)S(1)} %collective-permute-done.2.refs_2_.refs_4_, ...), custom_call_target="tpu_custom_call" | custom-call | flops 10000000 | bytes 1515520 | tf_op jit(solution)/shard_map/pallas_call | solution.py:54
  48.3 1.4 %collective-permute-start.6 = (bf16[320,1920]{1,0:T(8,128)(2,1)S(1)}, bf16[320,1920]{1,0:T(8,128)(2,1)S(1)}, u32[]{:S(2)}, u32[]{:S(2)}) collective-permute-start(bf16[320,1920]{1,0:T(8,128)(2,1)S(1)} %get-tuple-element.112), channel_id=1, source_target_pairs={{0,32},{1,3},{2,34},{3,5},{4,36},{5,7},{6,38},{7,1},{8,40},{9,11},... | collective-permute-start | bytes 3686408 | tf_op jit(solution)/shard_map/ppermute | solution.py:393
  49.7 1.5 %collective-permute-start.7 = (bf16[320,1920]{1,0:T(8,128)(2,1)S(1)}, bf16[320,1920]{1,0:T(8,128)(2,1)S(1)}, u32[]{:S(2)}, u32[]{:S(2)}) collective-permute-start(bf16[320,1920]{1,0:T(8,128)(2,1)S(1)} %get-tuple-element.113), channel_id=1, source_target_pairs={{0,96},{1,7},{2,98},{3,1},{4,100},{5,3},{6,102},{7,5},{8,104},{9,1... | collective-permute-start | bytes 3686408 | tf_op jit(solution)/shard_map/ppermute | solution.py:393
  51.2 0.7 collective-permute-start
  51.9 2.2 %shard_map.91 = (bf16[1280,512]{1,0:T(8,128)(2,1)S(1)}, f32[8,128]{1,0:T(8,128)S(1)}) custom-call(bf16[1280,1280]{1,0:T(8,128)(2,1)S(1)} %copy-done.1, bf16[256,640]{1,0:T(8,128)(2,1)S(1)} %get-tuple-element.99.refs_1_, bf16[256,2560]{1,0:T(8,128)(2,1)S(1)} %get-tuple-element.95.refs_2_.refs_7_, bf16[256,640]{1,0:T(8,128)(2,1)S(1)} %collective-permute-done.1.refs_4_.refs_3_, ...), custom_call_target="tpu_custom_call" | custom-call | bytes 1 | tf_op jit(solution)/shard_map/pallas_call | solution.py:54
  54.1 1.2 %shard_map.92 = (bf16[320,640]{1,0:T(8,128)(2,1)S(1)}, bf16[320,640]{1,0:T(8,128)(2,1)S(1)}, f32[8,128]{1,0:T(8,128)S(1)}) custom-call(s32[4]{0:T(128)S(1)} %pad_add_fusion.place_ref.refs_0_, bf16[8,64,1280]{2,1,0:T(8,128)(2,1)S(1)} %bitcast.13, bf16[256,640]{1,0:T(8,128)(2,1)S(1)} %collective-permute-done.refs_2_, ...), custom_call_target="tpu_custom_call" | custom-call | flops 1500000000 | bytes 942084 | tf_op jit(solution)/shard_map/pallas_call | solution.py:54
  55.4 0.6 collective-permute-start.4
  56.0 2.1 %collective-permute-start.5 = (bf16[320,640]{1,0:T(8,128)(2,1)S(1)}, bf16[320,640]{1,0:T(8,128)(2,1)S(1)}, u32[]{:S(2)}, u32[]{:S(2)}) collective-permute-start(bf16[320,640]{1,0:T(8,128)(2,1)S(1)} %get-tuple-element.111), channel_id=1, source_target_pairs={{0,24},{1,25},{2,26},{3,27},{4,28},{5,29},{6,30},{7,31},{8,16},{9,... | collective-permute-start | bytes 1228808 | tf_op jit(solution)/shard_map/ppermute | solution.py:393
  58.1 5.1 %shard_map.93 = (bf16[256,1280]{1,0:T(8,128)(2,1)}, f32[8,384]{1,0:T(8,128)S(1)}, f32[8,384]{1,0:T(8,128)S(1)}, f32[8,128]{1,0:T(8,128)S(1)}) custom-call(s32[4]{0:T(128)S(1)} %pad_add_fusion.place_ref.refs_0_, bf16[8,64,1280]{2,1,0:T(8,128)(2,1)S(1)} %bitcast.14, f32[256,1280]{1,0:T(8,128)S(1)} %get-tuple-element.87.refs_2_, ...), custom_call_target="tpu_custom_call" | custom-call | bytes 1 | tf_op jit(solution)/shard_map/pallas_call | solution.py:54
  63.3 2.3 %collective-permute-done.6.refs_3_ = bf16[320,1920]{1,0:T(8,128)(2,1)S(1)} collective-permute-done((bf16[320,1920]{1,0:T(8,128)(2,1)S(1)}, bf16[320,1920]{1,0:T(8,128)(2,1)S(1)}, u32[]{:S(2)}, u32[]{:S(2)}) %collective-permute-start.6) | collective-permute-done | bytes 1228832 | tf_op jit(solution)/shard_map/ppermute | solution.py:393
  65.5 0.9 shard_map.94
  66.4 1.4 %collective-permute-start.12 = (bf16[160,1920]{1,0:T(8,128)(2,1)S(1)}, bf16[160,1920]{1,0:T(8,128)(2,1)S(1)}, u32[]{:S(2)}, u32[]{:S(2)}) collective-permute-start(bf16[160,1920]{1,0:T(8,128)(2,1)S(1)} %get-tuple-element.127), channel_id=1, source_target_pairs={{0,32},{1,3},{2,34},{3,5},{4,36},{5,7},{6,38},{7,1},{8,40},{9,11},... | collective-permute-start | bytes 1843208 | tf_op jit(solution)/shard_map/ppermute | solution.py:393
  67.8 1.5 %collective-permute-start.13 = (bf16[160,1920]{1,0:T(8,128)(2,1)S(1)}, bf16[160,1920]{1,0:T(8,128)(2,1)S(1)}, u32[]{:S(2)}, u32[]{:S(2)}) collective-permute-start(bf16[160,1920]{1,0:T(8,128)(2,1)S(1)} %get-tuple-element.128), channel_id=1, source_target_pairs={{0,96},{1,7},{2,98},{3,1},{4,100},{5,3},{6,102},{7,5},{8,104},{9,1... | collective-permute-start | bytes 1843208 | tf_op jit(solution)/shard_map/ppermute | solution.py:393
  69.3 1.0 shard_map.95
  70.3 0.6 collective-permute-start.8
  70.9 2.1 %collective-permute-start.9 = (bf16[160,640]{1,0:T(8,128)(2,1)S(1)}, bf16[160,640]{1,0:T(8,128)(2,1)S(1)}, u32[]{:S(2)}, u32[]{:S(2)}) collective-permute-start(bf16[160,640]{1,0:T(8,128)(2,1)S(1)} %get-tuple-element.120), channel_id=1, source_target_pairs={{0,24},{1,25},{2,26},{3,27},{4,28},{5,29},{6,30},{7,31},{8,16},{9,... | collective-permute-start | bytes 614408 | tf_op jit(solution)/shard_map/ppermute | solution.py:393
  73.0 1.2 %collective-permute-start.10 = (f32[8,384]{1,0:T(8,128)S(1)}, f32[8,384]{1,0:T(8,128)S(1)}, u32[]{:S(2)}, u32[]{:S(2)}) collective-permute-start(f32[8,384]{1,0:T(8,128)S(1)} %get-tuple-element.122), channel_id=1, source_target_pairs={{0,8},{8,0},{1,9},{9,1},{2,10},{10,2},{3,11},{11,3},{4,12},{12,4},... | collective-permute-start | bytes 36872 | tf_op jit(solution)/shard_map/ppermute | solution.py:552
  74.3 0.8 shard_map.96
  75.1 1.0 shard_map.97
  76.1 1.1 collective-permute-done.10.refs_1_
  77.2 0.6 collective-permute-start.11
  77.8 1.3 %shard_map.99 = (f32[160,1920]{1,0:T(8,128)S(1)}, f32[80,1920]{1,0:T(8,128)}, f32[80,1920]{1,0:T(8,128)}, f32[8,128]{1,0:T(8,128)S(1)}) custom-call(f32[320,1920]{1,0:T(8,128)S(1)} %get-tuple-element.126.refs_0_, bf16[160,1920]{1,0:T(8,128)(2,1)S(1)} %collective-permute-done.12.refs_1_, bf16[160,1920]{1,0:T(8,128)(2,1)S(1)} %collective-permute-done.13.refs_2_, ...), custom_call_target="tpu_custom_call" | custom-call | flops 10000000 | bytes 1536000 | tf_op jit(solution)/shard_map/pallas_call | solution.py:54
  79.1 0.9 collective-permute-start.14
  80.0 1.8 %collective-permute-start.15 = (f32[80,1920]{1,0:T(8,128)}, f32[80,1920]{1,0:T(8,128)S(1)}, u32[]{:S(2)}, u32[]{:S(2)}) collective-permute-start(f32[80,1920]{1,0:T(8,128)} %get-tuple-element.135), channel_id=1, source_target_pairs={{0,6},{1,25},{2,0},{3,27},{4,2},{5,29},{6,4},{7,31},{8,14},{9,17},... | collective-permute-start | bytes 1843208 | tf_op jit(solution)/shard_map/ppermute | solution.py:393
  81.8 0.8 shard_map.100
  82.6 0.3 collective-permute-start.18
  83.0 2.4 %collective-permute-start.19 = (f32[80,768]{1,0:T(8,128)S(1)}, f32[80,768]{1,0:T(8,128)}, u32[]{:S(2)}, u32[]{:S(2)}) collective-permute-start(f32[80,768]{1,0:T(8,128)S(1)} %get-tuple-element.142), channel_id=1, source_target_pairs={{0,6},{1,7},{2,0},{3,1},{4,2},{5,3},{6,4},{7,5},{8,14},{9,15},{10,... | collective-permute-start | bytes 737288 | tf_op jit(solution)/shard_map/ppermute | solution.py:393
  85.3 3.5 %all-to-all-start.1 = ((bf16[8,4,8,1280]{3,2,1,0:T(8,128)(2,1)}), bf16[8,4,8,1280]{3,2,1,0:T(8,128)(2,1)S(1)}, u32[]{:S(2)}, u32[]{:S(2)}) async-start(bf16[8,4,8,1280]{3,2,1,0:T(8,128)(2,1)} %bitcast.7), calls=%async_computation.1 | async-start | bytes 1310720 | tf_op jit(solution)/shard_map/all_to_all | solution.py:559
  88.9 1.0 collective-permute-done.14.refs_1_
  89.8 0.2 shard_map.102
  90.0 0.5 collective-permute-start.16
  90.5 2.3 %collective-permute-start.17 = (f32[40,1920]{1,0:T(8,128)S(1)}, f32[40,1920]{1,0:T(8,128)S(1)}, u32[]{:S(2)}, u32[]{:S(2)}) collective-permute-start(f32[40,1920]{1,0:T(8,128)S(1)} %get-tuple-element.139), channel_id=1, source_target_pairs={{0,6},{1,25},{2,0},{3,27},{4,2},{5,29},{6,4},{7,31},{8,14},{9,17},... | collective-permute-start | bytes 921608 | tf_op jit(solution)/shard_map/ppermute | solution.py:393
  92.8 1.1 shard_map.103
  94.0 0.1 collective-permute-start.23
  94.1 2.6 %collective-permute-start.24 = (f32[40,768]{1,0:T(8,128)S(1)}, f32[40,768]{1,0:T(8,128)S(1)}, u32[]{:S(2)}, u32[]{:S(2)}) collective-permute-start(f32[40,768]{1,0:T(8,128)S(1)} %get-tuple-element.151), channel_id=1, source_target_pairs={{0,6},{1,7},{2,0},{3,1},{4,2},{5,3},{6,4},{7,5},{8,14},{9,15},{10,... | collective-permute-start | bytes 368648 | tf_op jit(solution)/shard_map/ppermute | solution.py:393
  96.7 1.3 %collective-permute-done.16.refs_1_ = f32[40,1920]{1,0:T(8,128)S(1)} collective-permute-done((f32[40,1920]{1,0:T(8,128)S(1)}, f32[40,1920]{1,0:T(8,128)S(1)}, u32[]{:S(2)}, u32[]{:S(2)}) %collective-permute-start.16) | collective-permute-done | bytes 307232 | tf_op jit(solution)/shard_map/ppermute | solution.py:393
  98.0 1.7 %collective-permute-done.17.refs_2_ = f32[40,1920]{1,0:T(8,128)S(1)} collective-permute-done((f32[40,1920]{1,0:T(8,128)S(1)}, f32[40,1920]{1,0:T(8,128)S(1)}, u32[]{:S(2)}, u32[]{:S(2)}) %collective-permute-start.17) | collective-permute-done | bytes 307232 | tf_op jit(solution)/shard_map/ppermute | solution.py:393
  99.8 1.4 %collective-permute-start.20 = (f32[20,1920]{1,0:T(8,128)S(1)}, f32[20,1920]{1,0:T(8,128)S(1)}, u32[]{:S(2)}, u32[]{:S(2)}) collective-permute-start(f32[20,1920]{1,0:T(8,128)S(1)} %get-tuple-element.146), channel_id=1, source_target_pairs={{0,16},{1,33},{2,18},{3,35},{4,20},{5,37},{6,22},{7,39},{8,24},{9,... | collective-permute-start | bytes 460808 | tf_op jit(solution)/shard_map/ppermute | solution.py:393
  101.2 2.4 %collective-permute-start.21 = (f32[20,1920]{1,0:T(8,128)S(1)}, f32[20,1920]{1,0:T(8,128)S(1)}, u32[]{:S(2)}, u32[]{:S(2)}) collective-permute-start(f32[20,1920]{1,0:T(8,128)S(1)} %get-tuple-element.147), channel_id=1, source_target_pairs={{0,8},{1,65},{2,10},{3,67},{4,12},{5,69},{6,14},{7,71},{8,0},{9,73... | collective-permute-start | bytes 460808 | tf_op jit(solution)/shard_map/ppermute | solution.py:393
  103.5 1.2 collective-permute-start.22
  104.8 0.4 collective-permute-start.25
  105.1 0.9 collective-permute-start.26
  106.0 0.1 collective-permute-done.20.refs_1_
  106.1 1.5 %collective-permute-start.27 = (f32[20,768]{1,0:T(8,128)S(1)}, f32[20,768]{1,0:T(8,128)S(1)}, u32[]{:S(2)}, u32[]{:S(2)}) collective-permute-start(f32[20,768]{1,0:T(8,128)S(1)} %get-tuple-element.160), channel_id=1, source_target_pairs={{0,96},{1,97},{2,98},{3,99},{4,100},{5,101},{6,102},{7,103},{8,104... | collective-permute-start | bytes 184328 | tf_op jit(solution)/shard_map/ppermute | solution.py:393
  107.6 0.8 collective-permute-done.21.refs_2_
  108.5 0.9 shard_map.107
  109.4 0.1 collective-permute-done.25.refs_3_
  109.5 0.8 collective-permute-done.26.refs_4_
  110.3 0.6 collective-permute-done.27.refs_5_
  110.9 0.6 shard_map.108
  111.5 7.0 %collective-permute-start.28 = (f32[10,2688]{1,0:T(8,128)S(1)}, f32[10,2688]{1,0:T(8,128)S(1)}, u32[]{:S(2)}, u32[]{:S(2)}) collective-permute-start(f32[10,2688]{1,0:T(8,128)S(1)} %get-tuple-element.163), channel_id=1, source_target_pairs={{0,1},{1,0},{2,3},{3,2},{4,5},{5,4},{6,7},{7,6},{8,9},{9,8},{10,11... | collective-permute-start | bytes 322568 | tf_op jit(solution)/shard_map/ppermute | solution.py:397
  118.6 1.0 collective-permute-done.28.refs_2_
  119.6 1.3 %shard_map.109 = (f32[10,3840]{1,0:T(8,128)}, f32[10,1280]{1,0:T(8,128)}, f32[1,10]{1,0:T(1,128)}) custom-call(s32[4]{0:T(128)S(1)} %pad_add_fusion.place_ref.refs_0_, f32[10,2688]{1,0:T(8,128)S(1)} %get-tuple-element.162.refs_1_, f32[10,2688]{1,0:T(8,128)S(1)} %collective-permute-done.28.refs_2_, f32[8,128]{1,0:T(8,128)S(1)} %get-tuple-element.164.refs_3_), custom_call_target="tpu_custom_call" | custom-call | bytes 1 | tf_op jit(solution)/shard_map/pallas_call | solution.py:54
  (38 shorter events, 0.4 us)
Async XLA Ops:
  3.1 6.8 %copy-start.5 = (f32[1280]{0:T(1024)S(1)}, f32[1280]{0:T(1024)}, u32[]{:S(2)}) copy-start(f32[1280]{0:T(1024)} %param.7) | copy-start | bytes 15364
  3.2 24.4 %all-to-all-start = ((bf16[8,2,4,8,1280]{4,3,2,1,0:T(8,128)(2,1)}), bf16[8,2,4,8,1280]{4,3,2,1,0:T(8,128)(2,1)S(1)}, u32[]{:S(2)}, u32[]{:S(2)}) async-start(bf16[8,2,4,8,1280]{4,3,2,1,0:T(8,128)(2,1)} %shard_map.84), calls=%async_computation | async-start | bytes 2621440 | tf_op jit(solution)/shard_map/all_to_all | solution.py:444
  38.1 8.6 %collective-permute-start.2 = (bf16[256,2560]{1,0:T(8,128)(2,1)S(1)}, bf16[256,2560]{1,0:T(8,128)(2,1)S(1)}, u32[]{:S(2)}, u32[]{:S(2)}) collective-permute-start(bf16[256,2560]{1,0:T(8,128)(2,1)S(1)} %get-tuple-element.95.refs_2_.refs_7_), channel_id=1, source_target_pairs={{0,1},{1,0},{2,3},{3,2},{4,5},{5,4},{6,7},{7,6},{8,9},{9,8},{10,11... | collective-permute-start | bytes 3932168 | tf_op jit(solution)/shard_map/ppermute | solution.py:397
  40.1 4.8 %collective-permute-start.3 = (bf16[256,1280]{1,0:T(8,128)(2,1)S(1)}, bf16[256,1280]{1,0:T(8,128)(2,1)S(1)}, u32[]{:S(2)}, u32[]{:S(2)}) collective-permute-start(bf16[256,1280]{1,0:T(8,128)(2,1)S(1)} %get-tuple-element.101.refs_1_), channel_id=1, source_target_pairs={{0,1},{1,0},{2,3},{3,2},{4,5},{5,4},{6,7},{7,6},{8,9},{9,8},{10,11... | collective-permute-start | bytes 1966088 | tf_op jit(solution)/shard_map/ppermute | solution.py:397
  40.4 4.5 %copy-start.2 = (bf16[1280,1280]{1,0:T(8,128)(2,1)S(1)}, bf16[1280,1280]{1,0:T(8,128)(2,1)}, u32[]{:S(2)}) copy-start(bf16[1280,1280]{1,0:T(8,128)(2,1)} %get-tuple-element.100.refs_0_) | copy-start | bytes 9830404
  44.5 2.2 %collective-permute-start.1 = (bf16[256,640]{1,0:T(8,128)(2,1)S(1)}, bf16[256,640]{1,0:T(8,128)(2,1)S(1)}, u32[]{:S(2)}, u32[]{:S(2)}) collective-permute-start(bf16[256,640]{1,0:T(8,128)(2,1)S(1)} %get-tuple-element.99.refs_1_), channel_id=1, source_target_pairs={{0,1},{1,0},{2,3},{3,2},{4,5},{5,4},{6,7},{7,6},{8,9},{9,8},{10,11... | collective-permute-start | bytes 983048 | tf_op jit(solution)/shard_map/ppermute | solution.py:397
  46.8 5.1 %copy-start.1 = (bf16[1280,1280]{1,0:T(8,128)(2,1)S(1)}, bf16[1280,1280]{1,0:T(8,128)(2,1)}, u32[]{:S(2)}) copy-start(bf16[1280,1280]{1,0:T(8,128)(2,1)} %get-tuple-element.98.refs_0_) | copy-start | bytes 9830404
  48.3 17.2 %collective-permute-start.6 = (bf16[320,1920]{1,0:T(8,128)(2,1)S(1)}, bf16[320,1920]{1,0:T(8,128)(2,1)S(1)}, u32[]{:S(2)}, u32[]{:S(2)}) collective-permute-start(bf16[320,1920]{1,0:T(8,128)(2,1)S(1)} %get-tuple-element.112), channel_id=1, source_target_pairs={{0,32},{1,3},{2,34},{3,5},{4,36},{5,7},{6,38},{7,1},{8,40},{9,11},... | collective-permute-start | bytes 3686408 | tf_op jit(solution)/shard_map/ppermute | solution.py:393
  49.7 15.9 %collective-permute-start.7 = (bf16[320,1920]{1,0:T(8,128)(2,1)S(1)}, bf16[320,1920]{1,0:T(8,128)(2,1)S(1)}, u32[]{:S(2)}, u32[]{:S(2)}) collective-permute-start(bf16[320,1920]{1,0:T(8,128)(2,1)S(1)} %get-tuple-element.113), channel_id=1, source_target_pairs={{0,96},{1,7},{2,98},{3,1},{4,100},{5,3},{6,102},{7,5},{8,104},{9,1... | collective-permute-start | bytes 3686408 | tf_op jit(solution)/shard_map/ppermute | solution.py:393
  51.2 2.9 %collective-permute-start = (bf16[256,640]{1,0:T(8,128)(2,1)S(1)}, bf16[256,640]{1,0:T(8,128)(2,1)S(1)}, u32[]{:S(2)}, u32[]{:S(2)}) collective-permute-start(bf16[256,640]{1,0:T(8,128)(2,1)S(1)} %get-tuple-element.97), channel_id=1, source_target_pairs={{0,1},{1,0},{2,3},{3,2},{4,5},{5,4},{6,7},{7,6},{8,9},{9,8},{10,11... | collective-permute-start | bytes 983048 | tf_op jit(solution)/shard_map/ppermute | solution.py:397
  54.1 4.0 %copy-start = (bf16[1280,1280]{1,0:T(8,128)(2,1)S(1)}, bf16[1280,1280]{1,0:T(8,128)(2,1)}, u32[]{:S(2)}) copy-start(bf16[1280,1280]{1,0:T(8,128)(2,1)} %get-tuple-element.96.refs_8_) | copy-start | bytes 9830404
  55.4 13.9 %collective-permute-start.4 = (bf16[320,640]{1,0:T(8,128)(2,1)S(1)}, bf16[320,640]{1,0:T(8,128)(2,1)S(1)}, u32[]{:S(2)}, u32[]{:S(2)}) collective-permute-start(bf16[320,640]{1,0:T(8,128)(2,1)S(1)} %get-tuple-element.110), channel_id=1, source_target_pairs={{0,16},{1,17},{2,18},{3,19},{4,20},{5,21},{6,22},{7,23},{8,24},{9,... | collective-permute-start | bytes 1228808 | tf_op jit(solution)/shard_map/ppermute | solution.py:393
  56.0 13.3 %collective-permute-start.5 = (bf16[320,640]{1,0:T(8,128)(2,1)S(1)}, bf16[320,640]{1,0:T(8,128)(2,1)S(1)}, u32[]{:S(2)}, u32[]{:S(2)}) collective-permute-start(bf16[320,640]{1,0:T(8,128)(2,1)S(1)} %get-tuple-element.111), channel_id=1, source_target_pairs={{0,24},{1,25},{2,26},{3,27},{4,28},{5,29},{6,30},{7,31},{8,16},{9,... | collective-permute-start | bytes 1228808 | tf_op jit(solution)/shard_map/ppermute | solution.py:393
  66.4 11.4 %collective-permute-start.12 = (bf16[160,1920]{1,0:T(8,128)(2,1)S(1)}, bf16[160,1920]{1,0:T(8,128)(2,1)S(1)}, u32[]{:S(2)}, u32[]{:S(2)}) collective-permute-start(bf16[160,1920]{1,0:T(8,128)(2,1)S(1)} %get-tuple-element.127), channel_id=1, source_target_pairs={{0,32},{1,3},{2,34},{3,5},{4,36},{5,7},{6,38},{7,1},{8,40},{9,11},... | collective-permute-start | bytes 1843208 | tf_op jit(solution)/shard_map/ppermute | solution.py:393
  67.8 10.0 %collective-permute-start.13 = (bf16[160,1920]{1,0:T(8,128)(2,1)S(1)}, bf16[160,1920]{1,0:T(8,128)(2,1)S(1)}, u32[]{:S(2)}, u32[]{:S(2)}) collective-permute-start(bf16[160,1920]{1,0:T(8,128)(2,1)S(1)} %get-tuple-element.128), channel_id=1, source_target_pairs={{0,96},{1,7},{2,98},{3,1},{4,100},{5,3},{6,102},{7,5},{8,104},{9,1... | collective-permute-start | bytes 1843208 | tf_op jit(solution)/shard_map/ppermute | solution.py:393
  70.3 11.5 %collective-permute-start.8 = (bf16[160,640]{1,0:T(8,128)(2,1)S(1)}, bf16[160,640]{1,0:T(8,128)(2,1)S(1)}, u32[]{:S(2)}, u32[]{:S(2)}) collective-permute-start(bf16[160,640]{1,0:T(8,128)(2,1)S(1)} %get-tuple-element.119), channel_id=1, source_target_pairs={{0,16},{1,17},{2,18},{3,19},{4,20},{5,21},{6,22},{7,23},{8,24},{9,... | collective-permute-start | bytes 614408 | tf_op jit(solution)/shard_map/ppermute | solution.py:393
  70.9 10.9 %collective-permute-start.9 = (bf16[160,640]{1,0:T(8,128)(2,1)S(1)}, bf16[160,640]{1,0:T(8,128)(2,1)S(1)}, u32[]{:S(2)}, u32[]{:S(2)}) collective-permute-start(bf16[160,640]{1,0:T(8,128)(2,1)S(1)} %get-tuple-element.120), channel_id=1, source_target_pairs={{0,24},{1,25},{2,26},{3,27},{4,28},{5,29},{6,30},{7,31},{8,16},{9,... | collective-permute-start | bytes 614408 | tf_op jit(solution)/shard_map/ppermute | solution.py:393
  73.0 4.2 %collective-permute-start.10 = (f32[8,384]{1,0:T(8,128)S(1)}, f32[8,384]{1,0:T(8,128)S(1)}, u32[]{:S(2)}, u32[]{:S(2)}) collective-permute-start(f32[8,384]{1,0:T(8,128)S(1)} %get-tuple-element.122), channel_id=1, source_target_pairs={{0,8},{8,0},{1,9},{9,1},{2,10},{10,2},{3,11},{11,3},{4,12},{12,4},... | collective-permute-start | bytes 36872 | tf_op jit(solution)/shard_map/ppermute | solution.py:552
  77.2 4.6 %collective-permute-start.11 = (f32[8,384]{1,0:T(8,128)S(1)}, f32[8,384]{1,0:T(8,128)S(1)}, u32[]{:S(2)}, u32[]{:S(2)}) collective-permute-start(f32[8,384]{1,0:T(8,128)S(1)} %get-tuple-element.125), channel_id=1, source_target_pairs={{0,16},{16,0},{1,17},{17,1},{2,18},{18,2},{3,19},{19,3},{4,20},{20... | collective-permute-start | bytes 36872 | tf_op jit(solution)/shard_map/ppermute | solution.py:556
  79.1 10.7 %collective-permute-start.14 = (f32[80,1920]{1,0:T(8,128)}, f32[80,1920]{1,0:T(8,128)S(1)}, u32[]{:S(2)}, u32[]{:S(2)}) collective-permute-start(f32[80,1920]{1,0:T(8,128)} %get-tuple-element.134), channel_id=1, source_target_pairs={{0,2},{1,17},{2,4},{3,19},{4,6},{5,21},{6,0},{7,23},{8,10},{9,25},... | collective-permute-start | bytes 1843208 | tf_op jit(solution)/shard_map/ppermute | solution.py:393
  80.0 9.8 %collective-permute-start.15 = (f32[80,1920]{1,0:T(8,128)}, f32[80,1920]{1,0:T(8,128)S(1)}, u32[]{:S(2)}, u32[]{:S(2)}) collective-permute-start(f32[80,1920]{1,0:T(8,128)} %get-tuple-element.135), channel_id=1, source_target_pairs={{0,6},{1,25},{2,0},{3,27},{4,2},{5,29},{6,4},{7,31},{8,14},{9,17},... | collective-permute-start | bytes 1843208 | tf_op jit(solution)/shard_map/ppermute | solution.py:393
  82.6 2.7 %copy-start.3 = (f32[160,768]{1,0:T(8,128)}, f32[160,768]{1,0:T(8,128)S(1)}, u32[]{:S(2)}) copy-start(f32[160,768]{1,0:T(8,128)S(1)} %get-tuple-element.140.refs_0_) | copy-start | bytes 1474564
  82.6 10.2 %collective-permute-start.18 = (f32[80,768]{1,0:T(8,128)}, f32[80,768]{1,0:T(8,128)}, u32[]{:S(2)}, u32[]{:S(2)}) collective-permute-start(f32[80,768]{1,0:T(8,128)} %get-tuple-element.141), channel_id=1, source_target_pairs={{0,2},{1,3},{2,4},{3,5},{4,6},{5,7},{6,0},{7,1},{8,10},{9,11},{10,... | collective-permute-start | bytes 737288 | tf_op jit(solution)/shard_map/ppermute | solution.py:393
  83.0 9.9 %collective-permute-start.19 = (f32[80,768]{1,0:T(8,128)S(1)}, f32[80,768]{1,0:T(8,128)}, u32[]{:S(2)}, u32[]{:S(2)}) collective-permute-start(f32[80,768]{1,0:T(8,128)S(1)} %get-tuple-element.142), channel_id=1, source_target_pairs={{0,6},{1,7},{2,0},{3,1},{4,2},{5,3},{6,4},{7,5},{8,14},{9,15},{10,... | collective-permute-start | bytes 737288 | tf_op jit(solution)/shard_map/ppermute | solution.py:393
  85.3 23.2 %all-to-all-start.1 = ((bf16[8,4,8,1280]{3,2,1,0:T(8,128)(2,1)}), bf16[8,4,8,1280]{3,2,1,0:T(8,128)(2,1)S(1)}, u32[]{:S(2)}, u32[]{:S(2)}) async-start(bf16[8,4,8,1280]{3,2,1,0:T(8,128)(2,1)} %bitcast.7), calls=%async_computation.1 | async-start | bytes 1310720 | tf_op jit(solution)/shard_map/all_to_all | solution.py:559
  88.9 4.0 %copy-start.4 = (f32[160,768]{1,0:T(8,128)S(1)}, f32[160,768]{1,0:T(8,128)}, u32[]{:S(2)}) copy-start(f32[160,768]{1,0:T(8,128)} %copy-done.3) | copy-start | bytes 1474564
  90.0 8.0 %collective-permute-start.16 = (f32[40,1920]{1,0:T(8,128)S(1)}, f32[40,1920]{1,0:T(8,128)S(1)}, u32[]{:S(2)}, u32[]{:S(2)}) collective-permute-start(f32[40,1920]{1,0:T(8,128)S(1)} %get-tuple-element.138), channel_id=1, source_target_pairs={{0,2},{1,17},{2,4},{3,19},{4,6},{5,21},{6,0},{7,23},{8,10},{9,25},... | collective-permute-start | bytes 921608 | tf_op jit(solution)/shard_map/ppermute | solution.py:393
  90.5 9.2 %collective-permute-start.17 = (f32[40,1920]{1,0:T(8,128)S(1)}, f32[40,1920]{1,0:T(8,128)S(1)}, u32[]{:S(2)}, u32[]{:S(2)}) collective-permute-start(f32[40,1920]{1,0:T(8,128)S(1)} %get-tuple-element.139), channel_id=1, source_target_pairs={{0,6},{1,25},{2,0},{3,27},{4,2},{5,29},{6,4},{7,31},{8,14},{9,17},... | collective-permute-start | bytes 921608 | tf_op jit(solution)/shard_map/ppermute | solution.py:393
  94.0 10.7 %collective-permute-start.23 = (f32[40,768]{1,0:T(8,128)S(1)}, f32[40,768]{1,0:T(8,128)S(1)}, u32[]{:S(2)}, u32[]{:S(2)}) collective-permute-start(f32[40,768]{1,0:T(8,128)S(1)} %get-tuple-element.150), channel_id=1, source_target_pairs={{0,2},{1,3},{2,4},{3,5},{4,6},{5,7},{6,0},{7,1},{8,10},{9,11},{10,... | collective-permute-start | bytes 368648 | tf_op jit(solution)/shard_map/ppermute | solution.py:393
  94.1 10.6 %collective-permute-start.24 = (f32[40,768]{1,0:T(8,128)S(1)}, f32[40,768]{1,0:T(8,128)S(1)}, u32[]{:S(2)}, u32[]{:S(2)}) collective-permute-start(f32[40,768]{1,0:T(8,128)S(1)} %get-tuple-element.151), channel_id=1, source_target_pairs={{0,6},{1,7},{2,0},{3,1},{4,2},{5,3},{6,4},{7,5},{8,14},{9,15},{10,... | collective-permute-start | bytes 368648 | tf_op jit(solution)/shard_map/ppermute | solution.py:393
  99.8 6.3 %collective-permute-start.20 = (f32[20,1920]{1,0:T(8,128)S(1)}, f32[20,1920]{1,0:T(8,128)S(1)}, u32[]{:S(2)}, u32[]{:S(2)}) collective-permute-start(f32[20,1920]{1,0:T(8,128)S(1)} %get-tuple-element.146), channel_id=1, source_target_pairs={{0,16},{1,33},{2,18},{3,35},{4,20},{5,37},{6,22},{7,39},{8,24},{9,... | collective-permute-start | bytes 460808 | tf_op jit(solution)/shard_map/ppermute | solution.py:393
  101.2 7.2 %collective-permute-start.21 = (f32[20,1920]{1,0:T(8,128)S(1)}, f32[20,1920]{1,0:T(8,128)S(1)}, u32[]{:S(2)}, u32[]{:S(2)}) collective-permute-start(f32[20,1920]{1,0:T(8,128)S(1)} %get-tuple-element.147), channel_id=1, source_target_pairs={{0,8},{1,65},{2,10},{3,67},{4,12},{5,69},{6,14},{7,71},{8,0},{9,73... | collective-permute-start | bytes 460808 | tf_op jit(solution)/shard_map/ppermute | solution.py:393
  103.5 4.9 %collective-permute-start.22 = (f32[20,1920]{1,0:T(8,128)S(1)}, f32[20,1920]{1,0:T(8,128)S(1)}, u32[]{:S(2)}, u32[]{:S(2)}) collective-permute-start(f32[20,1920]{1,0:T(8,128)S(1)} %get-tuple-element.148), channel_id=1, source_target_pairs={{0,24},{1,97},{2,26},{3,99},{4,28},{5,101},{6,30},{7,103},{8,16},{... | collective-permute-start | bytes 460808 | tf_op jit(solution)/shard_map/ppermute | solution.py:393
  104.8 4.8 %collective-permute-start.25 = (f32[20,768]{1,0:T(8,128)S(1)}, f32[20,768]{1,0:T(8,128)S(1)}, u32[]{:S(2)}, u32[]{:S(2)}) collective-permute-start(f32[20,768]{1,0:T(8,128)S(1)} %get-tuple-element.158), channel_id=1, source_target_pairs={{0,32},{1,33},{2,34},{3,35},{4,36},{5,37},{6,38},{7,39},{8,40},{9,... | collective-permute-start | bytes 184328 | tf_op jit(solution)/shard_map/ppermute | solution.py:393
  105.1 5.2 %collective-permute-start.26 = (f32[20,768]{1,0:T(8,128)S(1)}, f32[20,768]{1,0:T(8,128)S(1)}, u32[]{:S(2)}, u32[]{:S(2)}) collective-permute-start(f32[20,768]{1,0:T(8,128)S(1)} %get-tuple-element.159), channel_id=1, source_target_pairs={{0,64},{1,65},{2,66},{3,67},{4,68},{5,69},{6,70},{7,71},{8,72},{9,... | collective-permute-start | bytes 184328 | tf_op jit(solution)/shard_map/ppermute | solution.py:393
  106.1 4.8 %collective-permute-start.27 = (f32[20,768]{1,0:T(8,128)S(1)}, f32[20,768]{1,0:T(8,128)S(1)}, u32[]{:S(2)}, u32[]{:S(2)}) collective-permute-start(f32[20,768]{1,0:T(8,128)S(1)} %get-tuple-element.160), channel_id=1, source_target_pairs={{0,96},{1,97},{2,98},{3,99},{4,100},{5,101},{6,102},{7,103},{8,104... | collective-permute-start | bytes 184328 | tf_op jit(solution)/shard_map/ppermute | solution.py:393
  111.5 8.1 %collective-permute-start.28 = (f32[10,2688]{1,0:T(8,128)S(1)}, f32[10,2688]{1,0:T(8,128)S(1)}, u32[]{:S(2)}, u32[]{:S(2)}) collective-permute-start(f32[10,2688]{1,0:T(8,128)S(1)} %get-tuple-element.163), channel_id=1, source_target_pairs={{0,1},{1,0},{2,3},{3,2},{4,5},{5,4},{6,7},{7,6},{8,9},{9,8},{10,11... | collective-permute-start | bytes 322568 | tf_op jit(solution)/shard_map/ppermute | solution.py:397

commit v4 on v3

--- a/solution.py
+++ b/solution.py
@@ -17,7 +17,7 @@
 FACTOR = 1.0 / math.sqrt(32 * 1024)
 BF16, F32 = jnp.bfloat16, jnp.float32
 ORDER_A = (("z", "y", "x"), ("y", "x", "z"))
-ORDER_B = (("x", "y", "z"), ("x", "y", "z"))
+ORDER_B = (("x", "y", "z"), ("x", "z", "y"))
 WIDTH_A, WIDTH_B = 1920, 768
 NN = (((1,), (0,)), ((), ()))
 NT = (((1,), (1,)), ((), ()))

time: 121 us -> 120 us (level)
    ppermute x5, starting transfers between devices: 10.3 us -> 6.2 us  [swap(): return lax.ppermute(value, 'c', [(0, 1), (1, 0)])]
    ppermute x22, starting transfers between devices: 29.8 us -> 32.7 us  [send(): return lax.ppermute(value, ('z', 'xl', 'xh', 'y', 'c'), pairs)]
  transfers between devices with their start and end apart: 31 -> 31, of which waited for: 12 -> 9; matrix products, arithmetic and copies ran while one was open for 0% -> 0% of each run, Pallas kernels for 24% -> 25%
where the time goes in v4:
time: 120 us; the launch traced here: 119 us
  starting transfers between devices  51.1 us (43%)
  Pallas kernels  45.7 us (38%)
  waiting for transfers between devices  21.5 us (18%)
    pallas_call x22, Pallas kernels, call(): pl.pallas_call(run, out_shape=[results(o.shape, o.dtype) for o in outs] +...  35.9 us
    ppermute x22, starting transfers between devices, send(): return lax.ppermute(value, ('z', 'xl', 'xh', 'y', 'c'), pairs)  32.7 us
    all_to_all x1, waiting for transfers between devices, on_device(): lax.all_to_all(both, ('z', 'xl'), split_axis=0, concat_axis=0, tiled=True)  11.1 us
    ppermute x22, waiting for transfers between devices, send(): return lax.ppermute(value, ('z', 'xl', 'xh', 'y', 'c'), pairs)  8.26 us
    all_to_all x1, starting transfers between devices, on_device(): lax.all_to_all(both, ('z', 'xl'), split_axis=0, concat_axis=0, tiled=True)  6.8 us
    pallas_call x1, Pallas kernels, on_device(): pl.pallas_call(ready_body, out_shape=[pltpu.HBM((D, D), BF16)] * 3 + [sha...  6.43 us
    ppermute x5, starting transfers between devices, swap(): return lax.ppermute(value, 'c', [(0, 1), (1, 0)])  6.2 us
    all_to_all x1, starting transfers between devices, on_device(): lax.all_to_all(grad_here.reshape(8, 4, 8, D), ('z', 'xl'), split_axis=0,...  3.54 us
  transfers between devices with their start and end apart: 31, of which 9 were waited for; matrix products, arithmetic and copies ran while one was open for 0% of the time, Pallas kernels for 25%

profile of v4, /device:TPU:1, one launch (start us, length us, event | category | flops | bytes accessed | tf_op | source)
XLA Modules:
  0.0 119.2 jit_solution(3805046623166421865)
XLA Ops:
  0.6 2.5 %shard_map.84 = bf16[8,2,4,8,1280]{4,3,2,1,0:T(8,128)(2,1)} custom-call(bf16[4,8,8,1280]{3,2,1,0:T(8,128)(2,1)} %bitcast.17, bf16[4,8,8,1280]{3,2,1,0:T(8,128)(2,1)} %bitcast.18), custom_call_target="tpu_custom_call" | custom-call | tf_op jit(solution)/shard_map/pallas_call | solution.py:433
  3.2 6.8 %all-to-all-start = ((bf16[8,2,4,8,1280]{4,3,2,1,0:T(8,128)(2,1)}), bf16[8,2,4,8,1280]{4,3,2,1,0:T(8,128)(2,1)S(1)}, u32[]{:S(2)}, u32[]{:S(2)}) async-start(bf16[8,2,4,8,1280]{4,3,2,1,0:T(8,128)(2,1)} %shard_map.84), calls=%async_computation | async-start | bytes 2621440 | tf_op jit(solution)/shard_map/all_to_all | solution.py:444
  10.0 0.1 pad_add_fusion.place_ref.refs_0_
  10.1 6.4 %shard_map.85 = (bf16[1280,1280]{1,0:T(8,128)(2,1)}, bf16[1280,1280]{1,0:T(8,128)(2,1)}, bf16[1280,1280]{1,0:T(8,128)(2,1)}, f32[8,128]{1,0:T(8,128)S(1)}) custom-call(s32[4]{0:T(128)S(1)} %pad_add_fusion.place_ref.refs_0_), custom_call_target="tpu_custom_call" | custom-call | flops 1000000000 | bytes 20000000 | tf_op jit(solution)/shard_map/pallas_call | solution.py:438
  16.5 11.1 %all-to-all-done = bf16[8,2,4,8,1280]{4,3,2,1,0:T(8,128)(2,1)S(1)} async-done(((bf16[8,2,4,8,1280]{4,3,2,1,0:T(8,128)(2,1)}), bf16[8,2,4,8,1280]{4,3,2,1,0:T(8,128)(2,1)S(1)}, u32[]{:S(2)}, u32[]{:S(2)}) %all-to-all-start) | async-done | bytes 1310752 | tf_op jit(solution)/shard_map/all_to_all | solution.py:444
  27.6 6.3 %shard_map.86 = (bf16[256,1280]{1,0:T(8,128)(2,1)S(1)}, bf16[256,3840]{1,0:T(8,128)(2,1)S(1)}, bf16[256,640]{1,0:T(8,128)(2,1)S(1)}, bf16[1280,3840]{1,0:T(8,128...) custom-call(s32[4]{0:T(128)S(1)} %pad_add_fusion.place_ref.refs_0_, ...), custom_call_target="tpu_custom_call" | custom-call | flops 2516582400 | bytes 7980292 | tf_op jit(solution)/shard_map/pallas_call | solution.py:54
  34.0 4.2 %shard_map.87 = (bf16[256,2560]{1,0:T(8,128)(2,1)S(1)}, f32[8,128]{1,0:T(8,128)S(1)}) custom-call(s32[1]{0:T(128)S(6)} %sub.3.refs_0_, bf16[256,3840]{1,0:T(8,128)(2,1)S(1)} %get-tuple-element.90.refs_1_, bf16[8,64,1280]{2,1,0:T(8,128)(2,1)S(1)} %bitcast.11, bf16[1280,1280]{1,0:T(8,128)(2,1)S(1)} %get-tuple-element.91.refs_3_, ...), custom_call_target="tpu_custom_call" | custom-call | flops 5000000000 | bytes 1966081 | tf_op jit(solution)/shard_map/pallas_call | solution.py:54
  38.1 1.9 %collective-permute-start.2 = (bf16[256,2560]{1,0:T(8,128)(2,1)S(1)}, bf16[256,2560]{1,0:T(8,128)(2,1)S(1)}, u32[]{:S(2)}, u32[]{:S(2)}) collective-permute-start(bf16[256,2560]{1,0:T(8,128)(2,1)S(1)} %get-tuple-element.95.refs_2_.refs_7_), channel_id=1, source_target_pairs={{0,1},{1,0},{2,3},{3,2},{4,5},{5,4},{6,7},{7,6},{8,9},{9,8},{10,11... | collective-permute-start | bytes 3932168 | tf_op jit(solution)/shard_map/ppermute | solution.py:397
  40.1 0.3 collective-permute-start.3
  40.4 4.2 %shard_map.88 = (bf16[256,640]{1,0:T(8,128)(2,1)S(1)}, bf16[256,1920]{1,0:T(8,128)(2,1)S(1)}, f32[8,128]{1,0:T(8,128)S(1)}) custom-call(s32[1]{0:T(128)} %bitcast.3.refs_0_, bf16[256,3840]{1,0:T(8,128)(2,1)S(1)} %get-tuple-element.90.refs_1_, bf16[8,64,1280]{2,1,0:T(8,128)(2,1)S(1)} %bitcast.12, bf16[1280,1280]{1,0:T(8,128)(2,1)S(1)} %get-tuple-element.91.refs_3_, ...), custom_call_target="tpu_custom_call" | custom-call | flops 5000000000 | bytes 1966081 | tf_op jit(solution)/shard_map/pallas_call | solution.py:54
  44.5 0.3 collective-permute-start.1
  44.8 1.9 %shard_map.89 = (bf16[1280,512]{1,0:T(8,128)(2,1)S(1)}, f32[8,128]{1,0:T(8,128)S(1)}) custom-call(bf16[1280,1280]{1,0:T(8,128)(2,1)S(1)} %copy-done.2, bf16[256,1280]{1,0:T(8,128)(2,1)S(1)} %get-tuple-element.101.refs_1_, bf16[256,1280]{1,0:T(8,128)(2,1)S(1)} %collective-permute-done.3.refs_2_, f32[8,128]{1,0:T(8,128)S(1)} %get-tuple-element.102.refs_3_), custom_call_target="tpu_custom_call" | custom-call | flops 1677721600 | bytes 1474560 | tf_op jit(solution)/shard_map/pallas_call | solution.py:54
  46.8 1.5 %shard_map.90 = (bf16[320,1920]{1,0:T(8,128)(2,1)S(1)}, bf16[320,1920]{1,0:T(8,128)(2,1)S(1)}, f32[8,128]{1,0:T(8,128)S(1)}) custom-call(bf16[1280,512]{1,0:T(8,128)(2,1)S(1)} %get-tuple-element.103.refs_0_, bf16[256,1920]{1,0:T(8,128)(2,1)S(1)} %get-tuple-element.94.refs_1_.refs_6_, bf16[256,2560]{1,0:T(8,128)(2,1)S(1)} %collective-permute-done.2.refs_2_.refs_4_, ...), custom_call_target="tpu_custom_call" | custom-call | flops 10000000 | bytes 1515520 | tf_op jit(solution)/shard_map/pallas_call | solution.py:54
  48.3 1.4 %collective-permute-start.6 = (bf16[320,1920]{1,0:T(8,128)(2,1)S(1)}, bf16[320,1920]{1,0:T(8,128)(2,1)S(1)}, u32[]{:S(2)}, u32[]{:S(2)}) collective-permute-start(bf16[320,1920]{1,0:T(8,128)(2,1)S(1)} %get-tuple-element.112), channel_id=1, source_target_pairs={{0,32},{1,3},{2,34},{3,5},{4,36},{5,7},{6,38},{7,1},{8,40},{9,11},... | collective-permute-start | bytes 3686408 | tf_op jit(solution)/shard_map/ppermute | solution.py:393
  49.7 1.5 %collective-permute-start.7 = (bf16[320,1920]{1,0:T(8,128)(2,1)S(1)}, bf16[320,1920]{1,0:T(8,128)(2,1)S(1)}, u32[]{:S(2)}, u32[]{:S(2)}) collective-permute-start(bf16[320,1920]{1,0:T(8,128)(2,1)S(1)} %get-tuple-element.113), channel_id=1, source_target_pairs={{0,96},{1,7},{2,98},{3,1},{4,100},{5,3},{6,102},{7,5},{8,104},{9,1... | collective-permute-start | bytes 3686408 | tf_op jit(solution)/shard_map/ppermute | solution.py:393
  51.2 0.7 collective-permute-start
  51.9 2.2 %shard_map.91 = (bf16[1280,512]{1,0:T(8,128)(2,1)S(1)}, f32[8,128]{1,0:T(8,128)S(1)}) custom-call(bf16[1280,1280]{1,0:T(8,128)(2,1)S(1)} %copy-done.1, bf16[256,640]{1,0:T(8,128)(2,1)S(1)} %get-tuple-element.99.refs_1_, bf16[256,2560]{1,0:T(8,128)(2,1)S(1)} %get-tuple-element.95.refs_2_.refs_7_, bf16[256,640]{1,0:T(8,128)(2,1)S(1)} %collective-permute-done.1.refs_4_.refs_3_, ...), custom_call_target="tpu_custom_call" | custom-call | bytes 1 | tf_op jit(solution)/shard_map/pallas_call | solution.py:54
  54.1 1.2 %shard_map.92 = (bf16[320,640]{1,0:T(8,128)(2,1)S(1)}, bf16[320,640]{1,0:T(8,128)(2,1)S(1)}, f32[8,128]{1,0:T(8,128)S(1)}) custom-call(s32[4]{0:T(128)S(1)} %pad_add_fusion.place_ref.refs_0_, bf16[8,64,1280]{2,1,0:T(8,128)(2,1)S(1)} %bitcast.13, bf16[256,640]{1,0:T(8,128)(2,1)S(1)} %collective-permute-done.refs_2_, ...), custom_call_target="tpu_custom_call" | custom-call | flops 1500000000 | bytes 942084 | tf_op jit(solution)/shard_map/pallas_call | solution.py:54
  55.4 0.6 collective-permute-start.4
  56.0 2.1 %collective-permute-start.5 = (bf16[320,640]{1,0:T(8,128)(2,1)S(1)}, bf16[320,640]{1,0:T(8,128)(2,1)S(1)}, u32[]{:S(2)}, u32[]{:S(2)}) collective-permute-start(bf16[320,640]{1,0:T(8,128)(2,1)S(1)} %get-tuple-element.111), channel_id=1, source_target_pairs={{0,24},{1,25},{2,26},{3,27},{4,28},{5,29},{6,30},{7,31},{8,16},{9,... | collective-permute-start | bytes 1228808 | tf_op jit(solution)/shard_map/ppermute | solution.py:393
  58.1 5.1 %shard_map.93 = (bf16[256,1280]{1,0:T(8,128)(2,1)}, f32[8,384]{1,0:T(8,128)S(1)}, f32[8,384]{1,0:T(8,128)S(1)}, f32[8,128]{1,0:T(8,128)S(1)}) custom-call(s32[4]{0:T(128)S(1)} %pad_add_fusion.place_ref.refs_0_, bf16[8,64,1280]{2,1,0:T(8,128)(2,1)S(1)} %bitcast.14, f32[256,1280]{1,0:T(8,128)S(1)} %get-tuple-element.87.refs_2_, ...), custom_call_target="tpu_custom_call" | custom-call | bytes 1 | tf_op jit(solution)/shard_map/pallas_call | solution.py:54
  63.3 2.3 %collective-permute-done.6.refs_3_ = bf16[320,1920]{1,0:T(8,128)(2,1)S(1)} collective-permute-done((bf16[320,1920]{1,0:T(8,128)(2,1)S(1)}, bf16[320,1920]{1,0:T(8,128)(2,1)S(1)}, u32[]{:S(2)}, u32[]{:S(2)}) %collective-permute-start.6) | collective-permute-done | bytes 1228832 | tf_op jit(solution)/shard_map/ppermute | solution.py:393
  65.5 0.9 shard_map.94
  66.4 1.4 %collective-permute-start.12 = (bf16[160,1920]{1,0:T(8,128)(2,1)S(1)}, bf16[160,1920]{1,0:T(8,128)(2,1)S(1)}, u32[]{:S(2)}, u32[]{:S(2)}) collective-permute-start(bf16[160,1920]{1,0:T(8,128)(2,1)S(1)} %get-tuple-element.127), channel_id=1, source_target_pairs={{0,32},{1,3},{2,34},{3,5},{4,36},{5,7},{6,38},{7,1},{8,40},{9,11},... | collective-permute-start | bytes 1843208 | tf_op jit(solution)/shard_map/ppermute | solution.py:393
  67.8 1.5 %collective-permute-start.13 = (bf16[160,1920]{1,0:T(8,128)(2,1)S(1)}, bf16[160,1920]{1,0:T(8,128)(2,1)S(1)}, u32[]{:S(2)}, u32[]{:S(2)}) collective-permute-start(bf16[160,1920]{1,0:T(8,128)(2,1)S(1)} %get-tuple-element.128), channel_id=1, source_target_pairs={{0,96},{1,7},{2,98},{3,1},{4,100},{5,3},{6,102},{7,5},{8,104},{9,1... | collective-permute-start | bytes 1843208 | tf_op jit(solution)/shard_map/ppermute | solution.py:393
  69.3 1.0 shard_map.95
  70.3 0.6 collective-permute-start.8
  70.9 2.1 %collective-permute-start.9 = (bf16[160,640]{1,0:T(8,128)(2,1)S(1)}, bf16[160,640]{1,0:T(8,128)(2,1)S(1)}, u32[]{:S(2)}, u32[]{:S(2)}) collective-permute-start(bf16[160,640]{1,0:T(8,128)(2,1)S(1)} %get-tuple-element.120), channel_id=1, source_target_pairs={{0,24},{1,25},{2,26},{3,27},{4,28},{5,29},{6,30},{7,31},{8,16},{9,... | collective-permute-start | bytes 614408 | tf_op jit(solution)/shard_map/ppermute | solution.py:393
  73.0 1.2 %collective-permute-start.10 = (f32[8,384]{1,0:T(8,128)S(1)}, f32[8,384]{1,0:T(8,128)S(1)}, u32[]{:S(2)}, u32[]{:S(2)}) collective-permute-start(f32[8,384]{1,0:T(8,128)S(1)} %get-tuple-element.122), channel_id=1, source_target_pairs={{0,8},{8,0},{1,9},{9,1},{2,10},{10,2},{3,11},{11,3},{4,12},{12,4},... | collective-permute-start | bytes 36872 | tf_op jit(solution)/shard_map/ppermute | solution.py:552
  74.3 0.8 shard_map.96
  75.1 1.0 shard_map.97
  76.1 1.1 collective-permute-done.10.refs_1_
  77.2 0.6 collective-permute-start.11
  77.8 1.3 %shard_map.99 = (f32[160,1920]{1,0:T(8,128)S(1)}, f32[80,1920]{1,0:T(8,128)}, f32[80,1920]{1,0:T(8,128)}, f32[8,128]{1,0:T(8,128)S(1)}) custom-call(f32[320,1920]{1,0:T(8,128)S(1)} %get-tuple-element.126.refs_0_, bf16[160,1920]{1,0:T(8,128)(2,1)S(1)} %collective-permute-done.12.refs_1_, bf16[160,1920]{1,0:T(8,128)(2,1)S(1)} %collective-permute-done.13.refs_2_, ...), custom_call_target="tpu_custom_call" | custom-call | flops 10000000 | bytes 1536000 | tf_op jit(solution)/shard_map/pallas_call | solution.py:54
  79.1 0.9 collective-permute-start.14
  80.0 1.8 %collective-permute-start.15 = (f32[80,1920]{1,0:T(8,128)}, f32[80,1920]{1,0:T(8,128)S(1)}, u32[]{:S(2)}, u32[]{:S(2)}) collective-permute-start(f32[80,1920]{1,0:T(8,128)} %get-tuple-element.135), channel_id=1, source_target_pairs={{0,6},{1,25},{2,0},{3,27},{4,2},{5,29},{6,4},{7,31},{8,14},{9,17},... | collective-permute-start | bytes 1843208 | tf_op jit(solution)/shard_map/ppermute | solution.py:393
  81.8 0.8 shard_map.100
  82.6 1.9 %collective-permute-start.18 = (f32[80,768]{1,0:T(8,128)}, f32[80,768]{1,0:T(8,128)}, u32[]{:S(2)}, u32[]{:S(2)}) collective-permute-start(f32[80,768]{1,0:T(8,128)} %get-tuple-element.141), channel_id=1, source_target_pairs={{0,2},{1,33},{2,4},{3,35},{4,6},{5,37},{6,0},{7,39},{8,10},{9,41},... | collective-permute-start | bytes 737288 | tf_op jit(solution)/shard_map/ppermute | solution.py:393
  84.5 0.8 collective-permute-start.19
  85.3 3.5 %all-to-all-start.1 = ((bf16[8,4,8,1280]{3,2,1,0:T(8,128)(2,1)}), bf16[8,4,8,1280]{3,2,1,0:T(8,128)(2,1)S(1)}, u32[]{:S(2)}, u32[]{:S(2)}) async-start(bf16[8,4,8,1280]{3,2,1,0:T(8,128)(2,1)} %bitcast.7), calls=%async_computation.1 | async-start | bytes 1310720 | tf_op jit(solution)/shard_map/all_to_all | solution.py:559
  88.9 1.0 collective-permute-done.14.refs_1_
  89.8 0.2 shard_map.102
  90.0 0.5 collective-permute-start.16
  90.5 2.3 %collective-permute-start.17 = (f32[40,1920]{1,0:T(8,128)S(1)}, f32[40,1920]{1,0:T(8,128)S(1)}, u32[]{:S(2)}, u32[]{:S(2)}) collective-permute-start(f32[40,1920]{1,0:T(8,128)S(1)} %get-tuple-element.139), channel_id=1, source_target_pairs={{0,6},{1,25},{2,0},{3,27},{4,2},{5,29},{6,4},{7,31},{8,14},{9,17},... | collective-permute-start | bytes 921608 | tf_op jit(solution)/shard_map/ppermute | solution.py:393
  92.8 1.1 shard_map.103
  94.0 2.0 %collective-permute-start.23 = (f32[40,768]{1,0:T(8,128)S(1)}, f32[40,768]{1,0:T(8,128)S(1)}, u32[]{:S(2)}, u32[]{:S(2)}) collective-permute-start(f32[40,768]{1,0:T(8,128)S(1)} %get-tuple-element.150), channel_id=1, source_target_pairs={{0,2},{1,33},{2,4},{3,35},{4,6},{5,37},{6,0},{7,39},{8,10},{9,41},... | collective-permute-start | bytes 368648 | tf_op jit(solution)/shard_map/ppermute | solution.py:393
  96.0 0.7 collective-permute-start.24
  96.7 1.3 %collective-permute-done.16.refs_1_ = f32[40,1920]{1,0:T(8,128)S(1)} collective-permute-done((f32[40,1920]{1,0:T(8,128)S(1)}, f32[40,1920]{1,0:T(8,128)S(1)}, u32[]{:S(2)}, u32[]{:S(2)}) %collective-permute-start.16) | collective-permute-done | bytes 307232 | tf_op jit(solution)/shard_map/ppermute | solution.py:393
  98.0 1.7 %collective-permute-done.17.refs_2_ = f32[40,1920]{1,0:T(8,128)S(1)} collective-permute-done((f32[40,1920]{1,0:T(8,128)S(1)}, f32[40,1920]{1,0:T(8,128)S(1)}, u32[]{:S(2)}, u32[]{:S(2)}) %collective-permute-start.17) | collective-permute-done | bytes 307232 | tf_op jit(solution)/shard_map/ppermute | solution.py:393
  99.7 0.1 shard_map.104
  99.8 1.3 %collective-permute-start.20 = (f32[20,1920]{1,0:T(8,128)S(1)}, f32[20,1920]{1,0:T(8,128)S(1)}, u32[]{:S(2)}, u32[]{:S(2)}) collective-permute-start(f32[20,1920]{1,0:T(8,128)S(1)} %get-tuple-element.146), channel_id=1, source_target_pairs={{0,16},{1,33},{2,18},{3,35},{4,20},{5,37},{6,22},{7,39},{8,24},{9,... | collective-permute-start | bytes 460808 | tf_op jit(solution)/shard_map/ppermute | solution.py:393
  101.1 2.4 %collective-permute-start.21 = (f32[20,1920]{1,0:T(8,128)S(1)}, f32[20,1920]{1,0:T(8,128)S(1)}, u32[]{:S(2)}, u32[]{:S(2)}) collective-permute-start(f32[20,1920]{1,0:T(8,128)S(1)} %get-tuple-element.147), channel_id=1, source_target_pairs={{0,8},{1,65},{2,10},{3,67},{4,12},{5,69},{6,14},{7,71},{8,0},{9,73... | collective-permute-start | bytes 460808 | tf_op jit(solution)/shard_map/ppermute | solution.py:393
  103.5 1.2 collective-permute-start.22
  104.8 1.9 %collective-permute-start.25 = (f32[20,768]{1,0:T(8,128)S(1)}, f32[20,768]{1,0:T(8,128)S(1)}, u32[]{:S(2)}, u32[]{:S(2)}) collective-permute-start(f32[20,768]{1,0:T(8,128)S(1)} %get-tuple-element.158), channel_id=1, source_target_pairs={{0,32},{1,3},{2,34},{3,5},{4,36},{5,7},{6,38},{7,1},{8,40},{9,11},... | collective-permute-start | bytes 184328 | tf_op jit(solution)/shard_map/ppermute | solution.py:393
  106.7 3.1 %collective-permute-start.26 = (f32[20,768]{1,0:T(8,128)S(1)}, f32[20,768]{1,0:T(8,128)S(1)}, u32[]{:S(2)}, u32[]{:S(2)}) collective-permute-start(f32[20,768]{1,0:T(8,128)S(1)} %get-tuple-element.159), channel_id=1, source_target_pairs={{0,64},{1,5},{2,66},{3,7},{4,68},{5,1},{6,70},{7,3},{8,72},{9,13},... | collective-permute-start | bytes 184328 | tf_op jit(solution)/shard_map/ppermute | solution.py:393
  109.8 0.6 collective-permute-start.27
  110.4 0.1 shard_map.106
  110.5 0.9 shard_map.107
  111.4 1.0 collective-permute-done.26.refs_4_
  112.3 1.0 collective-permute-done.27.refs_5_
  113.3 0.6 shard_map.108
  113.9 3.0 %collective-permute-start.28 = (f32[10,2688]{1,0:T(8,128)S(1)}, f32[10,2688]{1,0:T(8,128)S(1)}, u32[]{:S(2)}, u32[]{:S(2)}) collective-permute-start(f32[10,2688]{1,0:T(8,128)S(1)} %get-tuple-element.163), channel_id=1, source_target_pairs={{0,1},{1,0},{2,3},{3,2},{4,5},{5,4},{6,7},{7,6},{8,9},{9,8},{10,11... | collective-permute-start | bytes 322568 | tf_op jit(solution)/shard_map/ppermute | solution.py:397
  116.9 1.0 collective-permute-done.28.refs_2_
  117.9 1.3 %shard_map.109 = (f32[10,3840]{1,0:T(8,128)}, f32[10,1280]{1,0:T(8,128)}, f32[1,10]{1,0:T(1,128)}) custom-call(s32[4]{0:T(128)S(1)} %pad_add_fusion.place_ref.refs_0_, f32[10,2688]{1,0:T(8,128)S(1)} %get-tuple-element.162.refs_1_, f32[10,2688]{1,0:T(8,128)S(1)} %collective-permute-done.28.refs_2_, f32[8,128]{1,0:T(8,128)S(1)} %get-tuple-element.164.refs_3_), custom_call_target="tpu_custom_call" | custom-call | bytes 1 | tf_op jit(solution)/shard_map/pallas_call | solution.py:54
  (38 shorter events, 0.2 us)
Async XLA Ops:
  3.1 6.8 %copy-start.5 = (f32[1280]{0:T(1024)S(1)}, f32[1280]{0:T(1024)}, u32[]{:S(2)}) copy-start(f32[1280]{0:T(1024)} %param.7) | copy-start | bytes 15364
  3.2 24.4 %all-to-all-start = ((bf16[8,2,4,8,1280]{4,3,2,1,0:T(8,128)(2,1)}), bf16[8,2,4,8,1280]{4,3,2,1,0:T(8,128)(2,1)S(1)}, u32[]{:S(2)}, u32[]{:S(2)}) async-start(bf16[8,2,4,8,1280]{4,3,2,1,0:T(8,128)(2,1)} %shard_map.84), calls=%async_computation | async-start | bytes 2621440 | tf_op jit(solution)/shard_map/all_to_all | solution.py:444
  38.1 8.6 %collective-permute-start.2 = (bf16[256,2560]{1,0:T(8,128)(2,1)S(1)}, bf16[256,2560]{1,0:T(8,128)(2,1)S(1)}, u32[]{:S(2)}, u32[]{:S(2)}) collective-permute-start(bf16[256,2560]{1,0:T(8,128)(2,1)S(1)} %get-tuple-element.95.refs_2_.refs_7_), channel_id=1, source_target_pairs={{0,1},{1,0},{2,3},{3,2},{4,5},{5,4},{6,7},{7,6},{8,9},{9,8},{10,11... | collective-permute-start | bytes 3932168 | tf_op jit(solution)/shard_map/ppermute | solution.py:397
  40.1 4.8 %collective-permute-start.3 = (bf16[256,1280]{1,0:T(8,128)(2,1)S(1)}, bf16[256,1280]{1,0:T(8,128)(2,1)S(1)}, u32[]{:S(2)}, u32[]{:S(2)}) collective-permute-start(bf16[256,1280]{1,0:T(8,128)(2,1)S(1)} %get-tuple-element.101.refs_1_), channel_id=1, source_target_pairs={{0,1},{1,0},{2,3},{3,2},{4,5},{5,4},{6,7},{7,6},{8,9},{9,8},{10,11... | collective-permute-start | bytes 1966088 | tf_op jit(solution)/shard_map/ppermute | solution.py:397
  40.4 4.5 %copy-start.2 = (bf16[1280,1280]{1,0:T(8,128)(2,1)S(1)}, bf16[1280,1280]{1,0:T(8,128)(2,1)}, u32[]{:S(2)}) copy-start(bf16[1280,1280]{1,0:T(8,128)(2,1)} %get-tuple-element.100.refs_0_) | copy-start | bytes 9830404
  44.5 2.2 %collective-permute-start.1 = (bf16[256,640]{1,0:T(8,128)(2,1)S(1)}, bf16[256,640]{1,0:T(8,128)(2,1)S(1)}, u32[]{:S(2)}, u32[]{:S(2)}) collective-permute-start(bf16[256,640]{1,0:T(8,128)(2,1)S(1)} %get-tuple-element.99.refs_1_), channel_id=1, source_target_pairs={{0,1},{1,0},{2,3},{3,2},{4,5},{5,4},{6,7},{7,6},{8,9},{9,8},{10,11... | collective-permute-start | bytes 983048 | tf_op jit(solution)/shard_map/ppermute | solution.py:397
  46.8 5.1 %copy-start.1 = (bf16[1280,1280]{1,0:T(8,128)(2,1)S(1)}, bf16[1280,1280]{1,0:T(8,128)(2,1)}, u32[]{:S(2)}) copy-start(bf16[1280,1280]{1,0:T(8,128)(2,1)} %get-tuple-element.98.refs_0_) | copy-start | bytes 9830404
  48.3 17.2 %collective-permute-start.6 = (bf16[320,1920]{1,0:T(8,128)(2,1)S(1)}, bf16[320,1920]{1,0:T(8,128)(2,1)S(1)}, u32[]{:S(2)}, u32[]{:S(2)}) collective-permute-start(bf16[320,1920]{1,0:T(8,128)(2,1)S(1)} %get-tuple-element.112), channel_id=1, source_target_pairs={{0,32},{1,3},{2,34},{3,5},{4,36},{5,7},{6,38},{7,1},{8,40},{9,11},... | collective-permute-start | bytes 3686408 | tf_op jit(solution)/shard_map/ppermute | solution.py:393
  49.7 15.9 %collective-permute-start.7 = (bf16[320,1920]{1,0:T(8,128)(2,1)S(1)}, bf16[320,1920]{1,0:T(8,128)(2,1)S(1)}, u32[]{:S(2)}, u32[]{:S(2)}) collective-permute-start(bf16[320,1920]{1,0:T(8,128)(2,1)S(1)} %get-tuple-element.113), channel_id=1, source_target_pairs={{0,96},{1,7},{2,98},{3,1},{4,100},{5,3},{6,102},{7,5},{8,104},{9,1... | collective-permute-start | bytes 3686408 | tf_op jit(solution)/shard_map/ppermute | solution.py:393
  51.2 2.9 %collective-permute-start = (bf16[256,640]{1,0:T(8,128)(2,1)S(1)}, bf16[256,640]{1,0:T(8,128)(2,1)S(1)}, u32[]{:S(2)}, u32[]{:S(2)}) collective-permute-start(bf16[256,640]{1,0:T(8,128)(2,1)S(1)} %get-tuple-element.97), channel_id=1, source_target_pairs={{0,1},{1,0},{2,3},{3,2},{4,5},{5,4},{6,7},{7,6},{8,9},{9,8},{10,11... | collective-permute-start | bytes 983048 | tf_op jit(solution)/shard_map/ppermute | solution.py:397
  54.1 4.0 %copy-start = (bf16[1280,1280]{1,0:T(8,128)(2,1)S(1)}, bf16[1280,1280]{1,0:T(8,128)(2,1)}, u32[]{:S(2)}) copy-start(bf16[1280,1280]{1,0:T(8,128)(2,1)} %get-tuple-element.96.refs_8_) | copy-start | bytes 9830404
  55.4 13.9 %collective-permute-start.4 = (bf16[320,640]{1,0:T(8,128)(2,1)S(1)}, bf16[320,640]{1,0:T(8,128)(2,1)S(1)}, u32[]{:S(2)}, u32[]{:S(2)}) collective-permute-start(bf16[320,640]{1,0:T(8,128)(2,1)S(1)} %get-tuple-element.110), channel_id=1, source_target_pairs={{0,16},{1,17},{2,18},{3,19},{4,20},{5,21},{6,22},{7,23},{8,24},{9,... | collective-permute-start | bytes 1228808 | tf_op jit(solution)/shard_map/ppermute | solution.py:393
  56.0 13.3 %collective-permute-start.5 = (bf16[320,640]{1,0:T(8,128)(2,1)S(1)}, bf16[320,640]{1,0:T(8,128)(2,1)S(1)}, u32[]{:S(2)}, u32[]{:S(2)}) collective-permute-start(bf16[320,640]{1,0:T(8,128)(2,1)S(1)} %get-tuple-element.111), channel_id=1, source_target_pairs={{0,24},{1,25},{2,26},{3,27},{4,28},{5,29},{6,30},{7,31},{8,16},{9,... | collective-permute-start | bytes 1228808 | tf_op jit(solution)/shard_map/ppermute | solution.py:393
  66.4 11.4 %collective-permute-start.12 = (bf16[160,1920]{1,0:T(8,128)(2,1)S(1)}, bf16[160,1920]{1,0:T(8,128)(2,1)S(1)}, u32[]{:S(2)}, u32[]{:S(2)}) collective-permute-start(bf16[160,1920]{1,0:T(8,128)(2,1)S(1)} %get-tuple-element.127), channel_id=1, source_target_pairs={{0,32},{1,3},{2,34},{3,5},{4,36},{5,7},{6,38},{7,1},{8,40},{9,11},... | collective-permute-start | bytes 1843208 | tf_op jit(solution)/shard_map/ppermute | solution.py:393
  67.8 10.0 %collective-permute-start.13 = (bf16[160,1920]{1,0:T(8,128)(2,1)S(1)}, bf16[160,1920]{1,0:T(8,128)(2,1)S(1)}, u32[]{:S(2)}, u32[]{:S(2)}) collective-permute-start(bf16[160,1920]{1,0:T(8,128)(2,1)S(1)} %get-tuple-element.128), channel_id=1, source_target_pairs={{0,96},{1,7},{2,98},{3,1},{4,100},{5,3},{6,102},{7,5},{8,104},{9,1... | collective-permute-start | bytes 1843208 | tf_op jit(solution)/shard_map/ppermute | solution.py:393
  70.3 11.5 %collective-permute-start.8 = (bf16[160,640]{1,0:T(8,128)(2,1)S(1)}, bf16[160,640]{1,0:T(8,128)(2,1)S(1)}, u32[]{:S(2)}, u32[]{:S(2)}) collective-permute-start(bf16[160,640]{1,0:T(8,128)(2,1)S(1)} %get-tuple-element.119), channel_id=1, source_target_pairs={{0,16},{1,17},{2,18},{3,19},{4,20},{5,21},{6,22},{7,23},{8,24},{9,... | collective-permute-start | bytes 614408 | tf_op jit(solution)/shard_map/ppermute | solution.py:393
  70.9 10.9 %collective-permute-start.9 = (bf16[160,640]{1,0:T(8,128)(2,1)S(1)}, bf16[160,640]{1,0:T(8,128)(2,1)S(1)}, u32[]{:S(2)}, u32[]{:S(2)}) collective-permute-start(bf16[160,640]{1,0:T(8,128)(2,1)S(1)} %get-tuple-element.120), channel_id=1, source_target_pairs={{0,24},{1,25},{2,26},{3,27},{4,28},{5,29},{6,30},{7,31},{8,16},{9,... | collective-permute-start | bytes 614408 | tf_op jit(solution)/shard_map/ppermute | solution.py:393
  73.0 4.2 %collective-permute-start.10 = (f32[8,384]{1,0:T(8,128)S(1)}, f32[8,384]{1,0:T(8,128)S(1)}, u32[]{:S(2)}, u32[]{:S(2)}) collective-permute-start(f32[8,384]{1,0:T(8,128)S(1)} %get-tuple-element.122), channel_id=1, source_target_pairs={{0,8},{8,0},{1,9},{9,1},{2,10},{10,2},{3,11},{11,3},{4,12},{12,4},... | collective-permute-start | bytes 36872 | tf_op jit(solution)/shard_map/ppermute | solution.py:552
  77.2 4.6 %collective-permute-start.11 = (f32[8,384]{1,0:T(8,128)S(1)}, f32[8,384]{1,0:T(8,128)S(1)}, u32[]{:S(2)}, u32[]{:S(2)}) collective-permute-start(f32[8,384]{1,0:T(8,128)S(1)} %get-tuple-element.125), channel_id=1, source_target_pairs={{0,16},{16,0},{1,17},{17,1},{2,18},{18,2},{3,19},{19,3},{4,20},{20... | collective-permute-start | bytes 36872 | tf_op jit(solution)/shard_map/ppermute | solution.py:556
  79.1 10.7 %collective-permute-start.14 = (f32[80,1920]{1,0:T(8,128)}, f32[80,1920]{1,0:T(8,128)S(1)}, u32[]{:S(2)}, u32[]{:S(2)}) collective-permute-start(f32[80,1920]{1,0:T(8,128)} %get-tuple-element.134), channel_id=1, source_target_pairs={{0,2},{1,17},{2,4},{3,19},{4,6},{5,21},{6,0},{7,23},{8,10},{9,25},... | collective-permute-start | bytes 1843208 | tf_op jit(solution)/shard_map/ppermute | solution.py:393
  80.0 9.8 %collective-permute-start.15 = (f32[80,1920]{1,0:T(8,128)}, f32[80,1920]{1,0:T(8,128)S(1)}, u32[]{:S(2)}, u32[]{:S(2)}) collective-permute-start(f32[80,1920]{1,0:T(8,128)} %get-tuple-element.135), channel_id=1, source_target_pairs={{0,6},{1,25},{2,0},{3,27},{4,2},{5,29},{6,4},{7,31},{8,14},{9,17},... | collective-permute-start | bytes 1843208 | tf_op jit(solution)/shard_map/ppermute | solution.py:393
  82.6 2.7 %copy-start.3 = (f32[160,768]{1,0:T(8,128)}, f32[160,768]{1,0:T(8,128)S(1)}, u32[]{:S(2)}) copy-start(f32[160,768]{1,0:T(8,128)S(1)} %get-tuple-element.140.refs_0_) | copy-start | bytes 1474564
  82.6 10.2 %collective-permute-start.18 = (f32[80,768]{1,0:T(8,128)}, f32[80,768]{1,0:T(8,128)}, u32[]{:S(2)}, u32[]{:S(2)}) collective-permute-start(f32[80,768]{1,0:T(8,128)} %get-tuple-element.141), channel_id=1, source_target_pairs={{0,2},{1,33},{2,4},{3,35},{4,6},{5,37},{6,0},{7,39},{8,10},{9,41},... | collective-permute-start | bytes 737288 | tf_op jit(solution)/shard_map/ppermute | solution.py:393
  84.5 8.4 %collective-permute-start.19 = (f32[80,768]{1,0:T(8,128)S(1)}, f32[80,768]{1,0:T(8,128)}, u32[]{:S(2)}, u32[]{:S(2)}) collective-permute-start(f32[80,768]{1,0:T(8,128)S(1)} %get-tuple-element.142), channel_id=1, source_target_pairs={{0,6},{1,97},{2,0},{3,99},{4,2},{5,101},{6,4},{7,103},{8,14},{9,10... | collective-permute-start | bytes 737288 | tf_op jit(solution)/shard_map/ppermute | solution.py:393
  85.3 25.1 %all-to-all-start.1 = ((bf16[8,4,8,1280]{3,2,1,0:T(8,128)(2,1)}), bf16[8,4,8,1280]{3,2,1,0:T(8,128)(2,1)S(1)}, u32[]{:S(2)}, u32[]{:S(2)}) async-start(bf16[8,4,8,1280]{3,2,1,0:T(8,128)(2,1)} %bitcast.7), calls=%async_computation.1 | async-start | bytes 1310720 | tf_op jit(solution)/shard_map/all_to_all | solution.py:559
  88.9 4.0 %copy-start.4 = (f32[160,768]{1,0:T(8,128)S(1)}, f32[160,768]{1,0:T(8,128)}, u32[]{:S(2)}) copy-start(f32[160,768]{1,0:T(8,128)} %copy-done.3) | copy-start | bytes 1474564
  90.0 8.0 %collective-permute-start.16 = (f32[40,1920]{1,0:T(8,128)S(1)}, f32[40,1920]{1,0:T(8,128)S(1)}, u32[]{:S(2)}, u32[]{:S(2)}) collective-permute-start(f32[40,1920]{1,0:T(8,128)S(1)} %get-tuple-element.138), channel_id=1, source_target_pairs={{0,2},{1,17},{2,4},{3,19},{4,6},{5,21},{6,0},{7,23},{8,10},{9,25},... | collective-permute-start | bytes 921608 | tf_op jit(solution)/shard_map/ppermute | solution.py:393
  90.5 9.2 %collective-permute-start.17 = (f32[40,1920]{1,0:T(8,128)S(1)}, f32[40,1920]{1,0:T(8,128)S(1)}, u32[]{:S(2)}, u32[]{:S(2)}) collective-permute-start(f32[40,1920]{1,0:T(8,128)S(1)} %get-tuple-element.139), channel_id=1, source_target_pairs={{0,6},{1,25},{2,0},{3,27},{4,2},{5,29},{6,4},{7,31},{8,14},{9,17},... | collective-permute-start | bytes 921608 | tf_op jit(solution)/shard_map/ppermute | solution.py:393
  94.0 10.7 %collective-permute-start.23 = (f32[40,768]{1,0:T(8,128)S(1)}, f32[40,768]{1,0:T(8,128)S(1)}, u32[]{:S(2)}, u32[]{:S(2)}) collective-permute-start(f32[40,768]{1,0:T(8,128)S(1)} %get-tuple-element.150), channel_id=1, source_target_pairs={{0,2},{1,33},{2,4},{3,35},{4,6},{5,37},{6,0},{7,39},{8,10},{9,41},... | collective-permute-start | bytes 368648 | tf_op jit(solution)/shard_map/ppermute | solution.py:393
  96.0 8.7 %collective-permute-start.24 = (f32[40,768]{1,0:T(8,128)S(1)}, f32[40,768]{1,0:T(8,128)S(1)}, u32[]{:S(2)}, u32[]{:S(2)}) collective-permute-start(f32[40,768]{1,0:T(8,128)S(1)} %get-tuple-element.151), channel_id=1, source_target_pairs={{0,6},{1,97},{2,0},{3,99},{4,2},{5,101},{6,4},{7,103},{8,14},{9,10... | collective-permute-start | bytes 368648 | tf_op jit(solution)/shard_map/ppermute | solution.py:393
  99.8 10.0 %collective-permute-start.20 = (f32[20,1920]{1,0:T(8,128)S(1)}, f32[20,1920]{1,0:T(8,128)S(1)}, u32[]{:S(2)}, u32[]{:S(2)}) collective-permute-start(f32[20,1920]{1,0:T(8,128)S(1)} %get-tuple-element.146), channel_id=1, source_target_pairs={{0,16},{1,33},{2,18},{3,35},{4,20},{5,37},{6,22},{7,39},{8,24},{9,... | collective-permute-start | bytes 460808 | tf_op jit(solution)/shard_map/ppermute | solution.py:393
  101.1 9.3 %collective-permute-start.21 = (f32[20,1920]{1,0:T(8,128)S(1)}, f32[20,1920]{1,0:T(8,128)S(1)}, u32[]{:S(2)}, u32[]{:S(2)}) collective-permute-start(f32[20,1920]{1,0:T(8,128)S(1)} %get-tuple-element.147), channel_id=1, source_target_pairs={{0,8},{1,65},{2,10},{3,67},{4,12},{5,69},{6,14},{7,71},{8,0},{9,73... | collective-permute-start | bytes 460808 | tf_op jit(solution)/shard_map/ppermute | solution.py:393
  103.5 6.9 %collective-permute-start.22 = (f32[20,1920]{1,0:T(8,128)S(1)}, f32[20,1920]{1,0:T(8,128)S(1)}, u32[]{:S(2)}, u32[]{:S(2)}) collective-permute-start(f32[20,1920]{1,0:T(8,128)S(1)} %get-tuple-element.148), channel_id=1, source_target_pairs={{0,24},{1,97},{2,26},{3,99},{4,28},{5,101},{6,30},{7,103},{8,16},{... | collective-permute-start | bytes 460808 | tf_op jit(solution)/shard_map/ppermute | solution.py:393
  104.8 6.6 %collective-permute-start.25 = (f32[20,768]{1,0:T(8,128)S(1)}, f32[20,768]{1,0:T(8,128)S(1)}, u32[]{:S(2)}, u32[]{:S(2)}) collective-permute-start(f32[20,768]{1,0:T(8,128)S(1)} %get-tuple-element.158), channel_id=1, source_target_pairs={{0,32},{1,3},{2,34},{3,5},{4,36},{5,7},{6,38},{7,1},{8,40},{9,11},... | collective-permute-start | bytes 184328 | tf_op jit(solution)/shard_map/ppermute | solution.py:393
  106.7 5.6 %collective-permute-start.26 = (f32[20,768]{1,0:T(8,128)S(1)}, f32[20,768]{1,0:T(8,128)S(1)}, u32[]{:S(2)}, u32[]{:S(2)}) collective-permute-start(f32[20,768]{1,0:T(8,128)S(1)} %get-tuple-element.159), channel_id=1, source_target_pairs={{0,64},{1,5},{2,66},{3,7},{4,68},{5,1},{6,70},{7,3},{8,72},{9,13},... | collective-permute-start | bytes 184328 | tf_op jit(solution)/shard_map/ppermute | solution.py:393
  109.8 3.5 %collective-permute-start.27 = (f32[20,768]{1,0:T(8,128)S(1)}, f32[20,768]{1,0:T(8,128)S(1)}, u32[]{:S(2)}, u32[]{:S(2)}) collective-permute-start(f32[20,768]{1,0:T(8,128)S(1)} %get-tuple-element.160), channel_id=1, source_target_pairs={{0,96},{1,7},{2,98},{3,1},{4,100},{5,3},{6,102},{7,5},{8,104},{9,1... | collective-permute-start | bytes 184328 | tf_op jit(solution)/shard_map/ppermute | solution.py:393
  113.9 4.0 %collective-permute-start.28 = (f32[10,2688]{1,0:T(8,128)S(1)}, f32[10,2688]{1,0:T(8,128)S(1)}, u32[]{:S(2)}, u32[]{:S(2)}) collective-permute-start(f32[10,2688]{1,0:T(8,128)S(1)} %get-tuple-element.163), channel_id=1, source_target_pairs={{0,1},{1,0},{2,3},{3,2},{4,5},{5,4},{6,7},{7,6},{8,9},{9,8},{10,11... | collective-permute-start | bytes 322568 | tf_op jit(solution)/shard_map/ppermute | solution.py:397

commit v5 on v4

--- a/solution.py
+++ b/solution.py
@@ -17,7 +17,7 @@
 FACTOR = 1.0 / math.sqrt(32 * 1024)
 BF16, F32 = jnp.bfloat16, jnp.float32
 ORDER_A = (("z", "y", "x"), ("y", "x", "z"))
-ORDER_B = (("x", "y", "z"), ("x", "z", "y"))
+ORDER_B = (("x", "z", "y"), ("x", "z", "y"))
 WIDTH_A, WIDTH_B = 1920, 768
 NN = (((1,), (0,)), ((), ()))
 NT = (((1,), (1,)), ((), ()))

time: 120 us -> 120 us (level)
    ppermute x22, starting transfers between devices: 32.7 us -> 31.4 us  [send(): return lax.ppermute(value, ('z', 'xl', 'xh', 'y', 'c'), pairs)]
  transfers between devices with their start and end apart: 31 -> 31, of which waited for: 9 -> 9; matrix products, arithmetic and copies ran while one was open for 0% -> 0% of each run, Pallas kernels for 25% -> 24%
where the time goes in v5:
time: 120 us
  starting transfers between devices  50.6 us (42%)
  Pallas kernels  45.7 us (38%)
  waiting for transfers between devices  22.3 us (19%)
    pallas_call x22, Pallas kernels, call(): pl.pallas_call(run, out_shape=[results(o.shape, o.dtype) for o in outs] +...  35.9 us
    ppermute x22, starting transfers between devices, send(): return lax.ppermute(value, ('z', 'xl', 'xh', 'y', 'c'), pairs)  31.4 us
    all_to_all x1, waiting for transfers between devices, on_device(): lax.all_to_all(both, ('z', 'xl'), split_axis=0, concat_axis=0, tiled=True)  11.1 us
    ppermute x22, waiting for transfers between devices, send(): return lax.ppermute(value, ('z', 'xl', 'xh', 'y', 'c'), pairs)  9.05 us
    ppermute x5, starting transfers between devices, swap(): return lax.ppermute(value, 'c', [(0, 1), (1, 0)])  7.07 us
    all_to_all x1, starting transfers between devices, on_device(): lax.all_to_all(both, ('z', 'xl'), split_axis=0, concat_axis=0, tiled=True)  6.8 us
    pallas_call x1, Pallas kernels, on_device(): pl.pallas_call(ready_body, out_shape=[pltpu.HBM((D, D), BF16)] * 3 + [sha...  6.43 us
    all_to_all x1, starting transfers between devices, on_device(): lax.all_to_all(grad_here.reshape(8, 4, 8, D), ('z', 'xl'), split_axis=0,...  3.54 us
  transfers between devices with their start and end apart: 31, of which 9 were waited for; matrix products, arithmetic and copies ran while one was open for 0% of the time, Pallas kernels for 24%

profile of v5, /device:TPU:1, one launch (start us, length us, event | category | flops | bytes accessed | tf_op | source)
XLA Modules:
  0.0 119.6 jit_solution(4373367689145805736)
XLA Ops:
  0.6 2.5 %shard_map.84 = bf16[8,2,4,8,1280]{4,3,2,1,0:T(8,128)(2,1)} custom-call(bf16[4,8,8,1280]{3,2,1,0:T(8,128)(2,1)} %bitcast.17, bf16[4,8,8,1280]{3,2,1,0:T(8,128)(2,1)} %bitcast.18), custom_call_target="tpu_custom_call" | custom-call | tf_op jit(solution)/shard_map/pallas_call | solution.py:433
  3.2 6.8 %all-to-all-start = ((bf16[8,2,4,8,1280]{4,3,2,1,0:T(8,128)(2,1)}), bf16[8,2,4,8,1280]{4,3,2,1,0:T(8,128)(2,1)S(1)}, u32[]{:S(2)}, u32[]{:S(2)}) async-start(bf16[8,2,4,8,1280]{4,3,2,1,0:T(8,128)(2,1)} %shard_map.84), calls=%async_computation | async-start | bytes 2621440 | tf_op jit(solution)/shard_map/all_to_all | solution.py:444
  10.0 0.1 pad_add_fusion.place_ref.refs_0_
  10.1 6.4 %shard_map.85 = (bf16[1280,1280]{1,0:T(8,128)(2,1)}, bf16[1280,1280]{1,0:T(8,128)(2,1)}, bf16[1280,1280]{1,0:T(8,128)(2,1)}, f32[8,128]{1,0:T(8,128)S(1)}) custom-call(s32[4]{0:T(128)S(1)} %pad_add_fusion.place_ref.refs_0_), custom_call_target="tpu_custom_call" | custom-call | flops 1000000000 | bytes 20000000 | tf_op jit(solution)/shard_map/pallas_call | solution.py:438
  16.5 11.1 %all-to-all-done = bf16[8,2,4,8,1280]{4,3,2,1,0:T(8,128)(2,1)S(1)} async-done(((bf16[8,2,4,8,1280]{4,3,2,1,0:T(8,128)(2,1)}), bf16[8,2,4,8,1280]{4,3,2,1,0:T(8,128)(2,1)S(1)}, u32[]{:S(2)}, u32[]{:S(2)}) %all-to-all-start) | async-done | bytes 1310752 | tf_op jit(solution)/shard_map/all_to_all | solution.py:444
  27.6 6.3 %shard_map.86 = (bf16[256,1280]{1,0:T(8,128)(2,1)S(1)}, bf16[256,3840]{1,0:T(8,128)(2,1)S(1)}, bf16[256,640]{1,0:T(8,128)(2,1)S(1)}, bf16[1280,3840]{1,0:T(8,128...) custom-call(s32[4]{0:T(128)S(1)} %pad_add_fusion.place_ref.refs_0_, ...), custom_call_target="tpu_custom_call" | custom-call | flops 2516582400 | bytes 7980292 | tf_op jit(solution)/shard_map/pallas_call | solution.py:54
  34.0 4.2 %shard_map.87 = (bf16[256,2560]{1,0:T(8,128)(2,1)S(1)}, f32[8,128]{1,0:T(8,128)S(1)}) custom-call(s32[1]{0:T(128)S(6)} %sub.3.refs_0_, bf16[256,3840]{1,0:T(8,128)(2,1)S(1)} %get-tuple-element.90.refs_1_, bf16[8,64,1280]{2,1,0:T(8,128)(2,1)S(1)} %bitcast.11, bf16[1280,1280]{1,0:T(8,128)(2,1)S(1)} %get-tuple-element.91.refs_3_, ...), custom_call_target="tpu_custom_call" | custom-call | flops 5000000000 | bytes 1966081 | tf_op jit(solution)/shard_map/pallas_call | solution.py:54
  38.1 1.9 %collective-permute-start.2 = (bf16[256,2560]{1,0:T(8,128)(2,1)S(1)}, bf16[256,2560]{1,0:T(8,128)(2,1)S(1)}, u32[]{:S(2)}, u32[]{:S(2)}) collective-permute-start(bf16[256,2560]{1,0:T(8,128)(2,1)S(1)} %get-tuple-element.95.refs_2_.refs_7_), channel_id=1, source_target_pairs={{0,1},{1,0},{2,3},{3,2},{4,5},{5,4},{6,7},{7,6},{8,9},{9,8},{10,11... | collective-permute-start | bytes 3932168 | tf_op jit(solution)/shard_map/ppermute | solution.py:397
  40.1 0.3 collective-permute-start.3
  40.4 4.2 %shard_map.88 = (bf16[256,640]{1,0:T(8,128)(2,1)S(1)}, bf16[256,1920]{1,0:T(8,128)(2,1)S(1)}, f32[8,128]{1,0:T(8,128)S(1)}) custom-call(s32[1]{0:T(128)} %bitcast.3.refs_0_, bf16[256,3840]{1,0:T(8,128)(2,1)S(1)} %get-tuple-element.90.refs_1_, bf16[8,64,1280]{2,1,0:T(8,128)(2,1)S(1)} %bitcast.12, bf16[1280,1280]{1,0:T(8,128)(2,1)S(1)} %get-tuple-element.91.refs_3_, ...), custom_call_target="tpu_custom_call" | custom-call | flops 5000000000 | bytes 1966081 | tf_op jit(solution)/shard_map/pallas_call | solution.py:54
  44.5 0.3 collective-permute-start.1
  44.8 1.9 %shard_map.89 = (bf16[1280,512]{1,0:T(8,128)(2,1)S(1)}, f32[8,128]{1,0:T(8,128)S(1)}) custom-call(bf16[1280,1280]{1,0:T(8,128)(2,1)S(1)} %copy-done.2, bf16[256,1280]{1,0:T(8,128)(2,1)S(1)} %get-tuple-element.101.refs_1_, bf16[256,1280]{1,0:T(8,128)(2,1)S(1)} %collective-permute-done.3.refs_2_, f32[8,128]{1,0:T(8,128)S(1)} %get-tuple-element.102.refs_3_), custom_call_target="tpu_custom_call" | custom-call | flops 1677721600 | bytes 1474560 | tf_op jit(solution)/shard_map/pallas_call | solution.py:54
  46.8 1.5 %shard_map.90 = (bf16[320,1920]{1,0:T(8,128)(2,1)S(1)}, bf16[320,1920]{1,0:T(8,128)(2,1)S(1)}, f32[8,128]{1,0:T(8,128)S(1)}) custom-call(bf16[1280,512]{1,0:T(8,128)(2,1)S(1)} %get-tuple-element.103.refs_0_, bf16[256,1920]{1,0:T(8,128)(2,1)S(1)} %get-tuple-element.94.refs_1_.refs_6_, bf16[256,2560]{1,0:T(8,128)(2,1)S(1)} %collective-permute-done.2.refs_2_.refs_4_, ...), custom_call_target="tpu_custom_call" | custom-call | flops 10000000 | bytes 1515520 | tf_op jit(solution)/shard_map/pallas_call | solution.py:54
  48.3 1.4 %collective-permute-start.6 = (bf16[320,1920]{1,0:T(8,128)(2,1)S(1)}, bf16[320,1920]{1,0:T(8,128)(2,1)S(1)}, u32[]{:S(2)}, u32[]{:S(2)}) collective-permute-start(bf16[320,1920]{1,0:T(8,128)(2,1)S(1)} %get-tuple-element.112), channel_id=1, source_target_pairs={{0,32},{1,3},{2,34},{3,5},{4,36},{5,7},{6,38},{7,1},{8,40},{9,11},... | collective-permute-start | bytes 3686408 | tf_op jit(solution)/shard_map/ppermute | solution.py:393
  49.7 1.5 %collective-permute-start.7 = (bf16[320,1920]{1,0:T(8,128)(2,1)S(1)}, bf16[320,1920]{1,0:T(8,128)(2,1)S(1)}, u32[]{:S(2)}, u32[]{:S(2)}) collective-permute-start(bf16[320,1920]{1,0:T(8,128)(2,1)S(1)} %get-tuple-element.113), channel_id=1, source_target_pairs={{0,96},{1,7},{2,98},{3,1},{4,100},{5,3},{6,102},{7,5},{8,104},{9,1... | collective-permute-start | bytes 3686408 | tf_op jit(solution)/shard_map/ppermute | solution.py:393
  51.2 0.7 collective-permute-start
  51.9 2.2 %shard_map.91 = (bf16[1280,512]{1,0:T(8,128)(2,1)S(1)}, f32[8,128]{1,0:T(8,128)S(1)}) custom-call(bf16[1280,1280]{1,0:T(8,128)(2,1)S(1)} %copy-done.1, bf16[256,640]{1,0:T(8,128)(2,1)S(1)} %get-tuple-element.99.refs_1_, bf16[256,2560]{1,0:T(8,128)(2,1)S(1)} %get-tuple-element.95.refs_2_.refs_7_, bf16[256,640]{1,0:T(8,128)(2,1)S(1)} %collective-permute-done.1.refs_4_.refs_3_, ...), custom_call_target="tpu_custom_call" | custom-call | bytes 1 | tf_op jit(solution)/shard_map/pallas_call | solution.py:54
  54.1 1.2 %shard_map.92 = (bf16[320,640]{1,0:T(8,128)(2,1)S(1)}, bf16[320,640]{1,0:T(8,128)(2,1)S(1)}, f32[8,128]{1,0:T(8,128)S(1)}) custom-call(s32[4]{0:T(128)S(1)} %pad_add_fusion.place_ref.refs_0_, bf16[8,64,1280]{2,1,0:T(8,128)(2,1)S(1)} %bitcast.13, bf16[256,640]{1,0:T(8,128)(2,1)S(1)} %collective-permute-done.refs_2_, ...), custom_call_target="tpu_custom_call" | custom-call | flops 1500000000 | bytes 942084 | tf_op jit(solution)/shard_map/pallas_call | solution.py:54
  55.4 0.6 collective-permute-start.4
  56.0 2.1 %collective-permute-start.5 = (bf16[320,640]{1,0:T(8,128)(2,1)S(1)}, bf16[320,640]{1,0:T(8,128)(2,1)S(1)}, u32[]{:S(2)}, u32[]{:S(2)}) collective-permute-start(bf16[320,640]{1,0:T(8,128)(2,1)S(1)} %get-tuple-element.111), channel_id=1, source_target_pairs={{0,24},{1,25},{2,26},{3,27},{4,28},{5,29},{6,30},{7,31},{8,16},{9,... | collective-permute-start | bytes 1228808 | tf_op jit(solution)/shard_map/ppermute | solution.py:393
  58.1 5.1 %shard_map.93 = (bf16[256,1280]{1,0:T(8,128)(2,1)}, f32[8,384]{1,0:T(8,128)S(1)}, f32[8,384]{1,0:T(8,128)S(1)}, f32[8,128]{1,0:T(8,128)S(1)}) custom-call(s32[4]{0:T(128)S(1)} %pad_add_fusion.place_ref.refs_0_, bf16[8,64,1280]{2,1,0:T(8,128)(2,1)S(1)} %bitcast.14, f32[256,1280]{1,0:T(8,128)S(1)} %get-tuple-element.87.refs_2_, ...), custom_call_target="tpu_custom_call" | custom-call | bytes 1 | tf_op jit(solution)/shard_map/pallas_call | solution.py:54
  63.3 2.3 %collective-permute-done.6.refs_3_ = bf16[320,1920]{1,0:T(8,128)(2,1)S(1)} collective-permute-done((bf16[320,1920]{1,0:T(8,128)(2,1)S(1)}, bf16[320,1920]{1,0:T(8,128)(2,1)S(1)}, u32[]{:S(2)}, u32[]{:S(2)}) %collective-permute-start.6) | collective-permute-done | bytes 1228832 | tf_op jit(solution)/shard_map/ppermute | solution.py:393
  65.5 0.9 shard_map.94
  66.4 1.4 %collective-permute-start.12 = (bf16[160,1920]{1,0:T(8,128)(2,1)S(1)}, bf16[160,1920]{1,0:T(8,128)(2,1)S(1)}, u32[]{:S(2)}, u32[]{:S(2)}) collective-permute-start(bf16[160,1920]{1,0:T(8,128)(2,1)S(1)} %get-tuple-element.127), channel_id=1, source_target_pairs={{0,32},{1,3},{2,34},{3,5},{4,36},{5,7},{6,38},{7,1},{8,40},{9,11},... | collective-permute-start | bytes 1843208 | tf_op jit(solution)/shard_map/ppermute | solution.py:393
  67.8 1.5 %collective-permute-start.13 = (bf16[160,1920]{1,0:T(8,128)(2,1)S(1)}, bf16[160,1920]{1,0:T(8,128)(2,1)S(1)}, u32[]{:S(2)}, u32[]{:S(2)}) collective-permute-start(bf16[160,1920]{1,0:T(8,128)(2,1)S(1)} %get-tuple-element.128), channel_id=1, source_target_pairs={{0,96},{1,7},{2,98},{3,1},{4,100},{5,3},{6,102},{7,5},{8,104},{9,1... | collective-permute-start | bytes 1843208 | tf_op jit(solution)/shard_map/ppermute | solution.py:393
  69.3 1.0 shard_map.95
  70.3 0.6 collective-permute-start.8
  70.9 2.1 %collective-permute-start.9 = (bf16[160,640]{1,0:T(8,128)(2,1)S(1)}, bf16[160,640]{1,0:T(8,128)(2,1)S(1)}, u32[]{:S(2)}, u32[]{:S(2)}) collective-permute-start(bf16[160,640]{1,0:T(8,128)(2,1)S(1)} %get-tuple-element.120), channel_id=1, source_target_pairs={{0,24},{1,25},{2,26},{3,27},{4,28},{5,29},{6,30},{7,31},{8,16},{9,... | collective-permute-start | bytes 614408 | tf_op jit(solution)/shard_map/ppermute | solution.py:393
  73.0 1.2 %collective-permute-start.10 = (f32[8,384]{1,0:T(8,128)S(1)}, f32[8,384]{1,0:T(8,128)S(1)}, u32[]{:S(2)}, u32[]{:S(2)}) collective-permute-start(f32[8,384]{1,0:T(8,128)S(1)} %get-tuple-element.122), channel_id=1, source_target_pairs={{0,8},{8,0},{1,9},{9,1},{2,10},{10,2},{3,11},{11,3},{4,12},{12,4},... | collective-permute-start | bytes 36872 | tf_op jit(solution)/shard_map/ppermute | solution.py:552
  74.3 0.8 shard_map.96
  75.1 1.0 shard_map.97
  76.1 1.1 collective-permute-done.10.refs_1_
  77.2 0.6 collective-permute-start.11
  77.8 1.3 %shard_map.99 = (f32[160,1920]{1,0:T(8,128)S(1)}, f32[80,1920]{1,0:T(8,128)}, f32[80,1920]{1,0:T(8,128)}, f32[8,128]{1,0:T(8,128)S(1)}) custom-call(f32[320,1920]{1,0:T(8,128)S(1)} %get-tuple-element.126.refs_0_, bf16[160,1920]{1,0:T(8,128)(2,1)S(1)} %collective-permute-done.12.refs_1_, bf16[160,1920]{1,0:T(8,128)(2,1)S(1)} %collective-permute-done.13.refs_2_, ...), custom_call_target="tpu_custom_call" | custom-call | flops 10000000 | bytes 1536000 | tf_op jit(solution)/shard_map/pallas_call | solution.py:54
  79.1 0.9 collective-permute-start.14
  80.0 1.8 %collective-permute-start.15 = (f32[80,1920]{1,0:T(8,128)}, f32[80,1920]{1,0:T(8,128)S(1)}, u32[]{:S(2)}, u32[]{:S(2)}) collective-permute-start(f32[80,1920]{1,0:T(8,128)} %get-tuple-element.135), channel_id=1, source_target_pairs={{0,6},{1,25},{2,0},{3,27},{4,2},{5,29},{6,4},{7,31},{8,14},{9,17},... | collective-permute-start | bytes 1843208 | tf_op jit(solution)/shard_map/ppermute | solution.py:393
  81.8 0.8 shard_map.100
  82.6 1.9 %collective-permute-start.18 = (f32[80,768]{1,0:T(8,128)}, f32[80,768]{1,0:T(8,128)}, u32[]{:S(2)}, u32[]{:S(2)}) collective-permute-start(f32[80,768]{1,0:T(8,128)} %get-tuple-element.141), channel_id=1, source_target_pairs={{0,32},{1,33},{2,34},{3,35},{4,36},{5,37},{6,38},{7,39},{8,40},{9,... | collective-permute-start | bytes 737288 | tf_op jit(solution)/shard_map/ppermute | solution.py:393
  84.5 0.8 collective-permute-start.19
  85.3 3.5 %all-to-all-start.1 = ((bf16[8,4,8,1280]{3,2,1,0:T(8,128)(2,1)}), bf16[8,4,8,1280]{3,2,1,0:T(8,128)(2,1)S(1)}, u32[]{:S(2)}, u32[]{:S(2)}) async-start(bf16[8,4,8,1280]{3,2,1,0:T(8,128)(2,1)} %bitcast.7), calls=%async_computation.1 | async-start | bytes 1310720 | tf_op jit(solution)/shard_map/all_to_all | solution.py:559
  88.9 1.0 collective-permute-done.14.refs_1_
  89.8 0.2 shard_map.102
  90.0 0.5 collective-permute-start.16
  90.5 2.4 %collective-permute-start.17 = (f32[40,1920]{1,0:T(8,128)S(1)}, f32[40,1920]{1,0:T(8,128)S(1)}, u32[]{:S(2)}, u32[]{:S(2)}) collective-permute-start(f32[40,1920]{1,0:T(8,128)S(1)} %get-tuple-element.139), channel_id=1, source_target_pairs={{0,6},{1,25},{2,0},{3,27},{4,2},{5,29},{6,4},{7,31},{8,14},{9,17},... | collective-permute-start | bytes 921608 | tf_op jit(solution)/shard_map/ppermute | solution.py:393
  93.0 1.1 shard_map.103
  94.1 1.8 %collective-permute-start.23 = (f32[40,768]{1,0:T(8,128)S(1)}, f32[40,768]{1,0:T(8,128)S(1)}, u32[]{:S(2)}, u32[]{:S(2)}) collective-permute-start(f32[40,768]{1,0:T(8,128)S(1)} %get-tuple-element.150), channel_id=1, source_target_pairs={{0,32},{1,33},{2,34},{3,35},{4,36},{5,37},{6,38},{7,39},{8,40},{9,... | collective-permute-start | bytes 368648 | tf_op jit(solution)/shard_map/ppermute | solution.py:393
  95.9 1.0 collective-permute-start.24
  96.8 2.0 %collective-permute-done.16.refs_1_ = f32[40,1920]{1,0:T(8,128)S(1)} collective-permute-done((f32[40,1920]{1,0:T(8,128)S(1)}, f32[40,1920]{1,0:T(8,128)S(1)}, u32[]{:S(2)}, u32[]{:S(2)}) %collective-permute-start.16) | collective-permute-done | bytes 307232 | tf_op jit(solution)/shard_map/ppermute | solution.py:393
  98.9 1.8 %collective-permute-done.17.refs_2_ = f32[40,1920]{1,0:T(8,128)S(1)} collective-permute-done((f32[40,1920]{1,0:T(8,128)S(1)}, f32[40,1920]{1,0:T(8,128)S(1)}, u32[]{:S(2)}, u32[]{:S(2)}) %collective-permute-start.17) | collective-permute-done | bytes 307232 | tf_op jit(solution)/shard_map/ppermute | solution.py:393
  100.6 0.1 shard_map.104
  100.7 1.4 %collective-permute-start.20 = (f32[20,1920]{1,0:T(8,128)S(1)}, f32[20,1920]{1,0:T(8,128)S(1)}, u32[]{:S(2)}, u32[]{:S(2)}) collective-permute-start(f32[20,1920]{1,0:T(8,128)S(1)} %get-tuple-element.146), channel_id=1, source_target_pairs={{0,16},{1,33},{2,18},{3,35},{4,20},{5,37},{6,22},{7,39},{8,24},{9,... | collective-permute-start | bytes 460808 | tf_op jit(solution)/shard_map/ppermute | solution.py:393
  102.1 2.4 %collective-permute-start.21 = (f32[20,1920]{1,0:T(8,128)S(1)}, f32[20,1920]{1,0:T(8,128)S(1)}, u32[]{:S(2)}, u32[]{:S(2)}) collective-permute-start(f32[20,1920]{1,0:T(8,128)S(1)} %get-tuple-element.147), channel_id=1, source_target_pairs={{0,8},{1,65},{2,10},{3,67},{4,12},{5,69},{6,14},{7,71},{8,0},{9,73... | collective-permute-start | bytes 460808 | tf_op jit(solution)/shard_map/ppermute | solution.py:393
  104.5 1.1 collective-permute-start.22
  105.6 0.5 collective-permute-start.25
  106.2 3.1 %collective-permute-start.26 = (f32[20,768]{1,0:T(8,128)S(1)}, f32[20,768]{1,0:T(8,128)S(1)}, u32[]{:S(2)}, u32[]{:S(2)}) collective-permute-start(f32[20,768]{1,0:T(8,128)S(1)} %get-tuple-element.159), channel_id=1, source_target_pairs={{0,4},{1,5},{2,6},{3,7},{4,0},{5,1},{6,2},{7,3},{8,12},{9,13},{10,... | collective-permute-start | bytes 184328 | tf_op jit(solution)/shard_map/ppermute | solution.py:393
  109.3 0.6 collective-permute-start.27
  109.9 0.1 shard_map.106
  109.9 0.9 shard_map.107
  110.8 1.0 collective-permute-done.26.refs_4_
  111.8 1.0 collective-permute-done.27.refs_5_
  112.8 0.6 shard_map.108
  113.4 3.8 %collective-permute-start.28 = (f32[10,2688]{1,0:T(8,128)S(1)}, f32[10,2688]{1,0:T(8,128)S(1)}, u32[]{:S(2)}, u32[]{:S(2)}) collective-permute-start(f32[10,2688]{1,0:T(8,128)S(1)} %get-tuple-element.163), channel_id=1, source_target_pairs={{0,1},{1,0},{2,3},{3,2},{4,5},{5,4},{6,7},{7,6},{8,9},{9,8},{10,11... | collective-permute-start | bytes 322568 | tf_op jit(solution)/shard_map/ppermute | solution.py:397
  117.2 1.0 collective-permute-done.28.refs_2_
  118.3 1.3 %shard_map.109 = (f32[10,3840]{1,0:T(8,128)}, f32[10,1280]{1,0:T(8,128)}, f32[1,10]{1,0:T(1,128)}) custom-call(s32[4]{0:T(128)S(1)} %pad_add_fusion.place_ref.refs_0_, f32[10,2688]{1,0:T(8,128)S(1)} %get-tuple-element.162.refs_1_, f32[10,2688]{1,0:T(8,128)S(1)} %collective-permute-done.28.refs_2_, f32[8,128]{1,0:T(8,128)S(1)} %get-tuple-element.164.refs_3_), custom_call_target="tpu_custom_call" | custom-call | bytes 1 | tf_op jit(solution)/shard_map/pallas_call | solution.py:54
  (38 shorter events, 0.2 us)
Async XLA Ops:
  3.1 6.8 %copy-start.5 = (f32[1280]{0:T(1024)S(1)}, f32[1280]{0:T(1024)}, u32[]{:S(2)}) copy-start(f32[1280]{0:T(1024)} %param.7) | copy-start | bytes 15364
  3.2 24.4 %all-to-all-start = ((bf16[8,2,4,8,1280]{4,3,2,1,0:T(8,128)(2,1)}), bf16[8,2,4,8,1280]{4,3,2,1,0:T(8,128)(2,1)S(1)}, u32[]{:S(2)}, u32[]{:S(2)}) async-start(bf16[8,2,4,8,1280]{4,3,2,1,0:T(8,128)(2,1)} %shard_map.84), calls=%async_computation | async-start | bytes 2621440 | tf_op jit(solution)/shard_map/all_to_all | solution.py:444
  38.1 8.6 %collective-permute-start.2 = (bf16[256,2560]{1,0:T(8,128)(2,1)S(1)}, bf16[256,2560]{1,0:T(8,128)(2,1)S(1)}, u32[]{:S(2)}, u32[]{:S(2)}) collective-permute-start(bf16[256,2560]{1,0:T(8,128)(2,1)S(1)} %get-tuple-element.95.refs_2_.refs_7_), channel_id=1, source_target_pairs={{0,1},{1,0},{2,3},{3,2},{4,5},{5,4},{6,7},{7,6},{8,9},{9,8},{10,11... | collective-permute-start | bytes 3932168 | tf_op jit(solution)/shard_map/ppermute | solution.py:397
  40.1 4.8 %collective-permute-start.3 = (bf16[256,1280]{1,0:T(8,128)(2,1)S(1)}, bf16[256,1280]{1,0:T(8,128)(2,1)S(1)}, u32[]{:S(2)}, u32[]{:S(2)}) collective-permute-start(bf16[256,1280]{1,0:T(8,128)(2,1)S(1)} %get-tuple-element.101.refs_1_), channel_id=1, source_target_pairs={{0,1},{1,0},{2,3},{3,2},{4,5},{5,4},{6,7},{7,6},{8,9},{9,8},{10,11... | collective-permute-start | bytes 1966088 | tf_op jit(solution)/shard_map/ppermute | solution.py:397
  40.4 4.5 %copy-start.2 = (bf16[1280,1280]{1,0:T(8,128)(2,1)S(1)}, bf16[1280,1280]{1,0:T(8,128)(2,1)}, u32[]{:S(2)}) copy-start(bf16[1280,1280]{1,0:T(8,128)(2,1)} %get-tuple-element.100.refs_0_) | copy-start | bytes 9830404
  44.5 2.2 %collective-permute-start.1 = (bf16[256,640]{1,0:T(8,128)(2,1)S(1)}, bf16[256,640]{1,0:T(8,128)(2,1)S(1)}, u32[]{:S(2)}, u32[]{:S(2)}) collective-permute-start(bf16[256,640]{1,0:T(8,128)(2,1)S(1)} %get-tuple-element.99.refs_1_), channel_id=1, source_target_pairs={{0,1},{1,0},{2,3},{3,2},{4,5},{5,4},{6,7},{7,6},{8,9},{9,8},{10,11... | collective-permute-start | bytes 983048 | tf_op jit(solution)/shard_map/ppermute | solution.py:397
  46.8 5.1 %copy-start.1 = (bf16[1280,1280]{1,0:T(8,128)(2,1)S(1)}, bf16[1280,1280]{1,0:T(8,128)(2,1)}, u32[]{:S(2)}) copy-start(bf16[1280,1280]{1,0:T(8,128)(2,1)} %get-tuple-element.98.refs_0_) | copy-start | bytes 9830404
  48.3 17.2 %collective-permute-start.6 = (bf16[320,1920]{1,0:T(8,128)(2,1)S(1)}, bf16[320,1920]{1,0:T(8,128)(2,1)S(1)}, u32[]{:S(2)}, u32[]{:S(2)}) collective-permute-start(bf16[320,1920]{1,0:T(8,128)(2,1)S(1)} %get-tuple-element.112), channel_id=1, source_target_pairs={{0,32},{1,3},{2,34},{3,5},{4,36},{5,7},{6,38},{7,1},{8,40},{9,11},... | collective-permute-start | bytes 3686408 | tf_op jit(solution)/shard_map/ppermute | solution.py:393
  49.7 15.9 %collective-permute-start.7 = (bf16[320,1920]{1,0:T(8,128)(2,1)S(1)}, bf16[320,1920]{1,0:T(8,128)(2,1)S(1)}, u32[]{:S(2)}, u32[]{:S(2)}) collective-permute-start(bf16[320,1920]{1,0:T(8,128)(2,1)S(1)} %get-tuple-element.113), channel_id=1, source_target_pairs={{0,96},{1,7},{2,98},{3,1},{4,100},{5,3},{6,102},{7,5},{8,104},{9,1... | collective-permute-start | bytes 3686408 | tf_op jit(solution)/shard_map/ppermute | solution.py:393
  51.2 2.9 %collective-permute-start = (bf16[256,640]{1,0:T(8,128)(2,1)S(1)}, bf16[256,640]{1,0:T(8,128)(2,1)S(1)}, u32[]{:S(2)}, u32[]{:S(2)}) collective-permute-start(bf16[256,640]{1,0:T(8,128)(2,1)S(1)} %get-tuple-element.97), channel_id=1, source_target_pairs={{0,1},{1,0},{2,3},{3,2},{4,5},{5,4},{6,7},{7,6},{8,9},{9,8},{10,11... | collective-permute-start | bytes 983048 | tf_op jit(solution)/shard_map/ppermute | solution.py:397
  54.1 4.0 %copy-start = (bf16[1280,1280]{1,0:T(8,128)(2,1)S(1)}, bf16[1280,1280]{1,0:T(8,128)(2,1)}, u32[]{:S(2)}) copy-start(bf16[1280,1280]{1,0:T(8,128)(2,1)} %get-tuple-element.96.refs_8_) | copy-start | bytes 9830404
  55.4 13.9 %collective-permute-start.4 = (bf16[320,640]{1,0:T(8,128)(2,1)S(1)}, bf16[320,640]{1,0:T(8,128)(2,1)S(1)}, u32[]{:S(2)}, u32[]{:S(2)}) collective-permute-start(bf16[320,640]{1,0:T(8,128)(2,1)S(1)} %get-tuple-element.110), channel_id=1, source_target_pairs={{0,16},{1,17},{2,18},{3,19},{4,20},{5,21},{6,22},{7,23},{8,24},{9,... | collective-permute-start | bytes 1228808 | tf_op jit(solution)/shard_map/ppermute | solution.py:393
  56.0 13.3 %collective-permute-start.5 = (bf16[320,640]{1,0:T(8,128)(2,1)S(1)}, bf16[320,640]{1,0:T(8,128)(2,1)S(1)}, u32[]{:S(2)}, u32[]{:S(2)}) collective-permute-start(bf16[320,640]{1,0:T(8,128)(2,1)S(1)} %get-tuple-element.111), channel_id=1, source_target_pairs={{0,24},{1,25},{2,26},{3,27},{4,28},{5,29},{6,30},{7,31},{8,16},{9,... | collective-permute-start | bytes 1228808 | tf_op jit(solution)/shard_map/ppermute | solution.py:393
  66.4 11.4 %collective-permute-start.12 = (bf16[160,1920]{1,0:T(8,128)(2,1)S(1)}, bf16[160,1920]{1,0:T(8,128)(2,1)S(1)}, u32[]{:S(2)}, u32[]{:S(2)}) collective-permute-start(bf16[160,1920]{1,0:T(8,128)(2,1)S(1)} %get-tuple-element.127), channel_id=1, source_target_pairs={{0,32},{1,3},{2,34},{3,5},{4,36},{5,7},{6,38},{7,1},{8,40},{9,11},... | collective-permute-start | bytes 1843208 | tf_op jit(solution)/shard_map/ppermute | solution.py:393
  67.8 10.0 %collective-permute-start.13 = (bf16[160,1920]{1,0:T(8,128)(2,1)S(1)}, bf16[160,1920]{1,0:T(8,128)(2,1)S(1)}, u32[]{:S(2)}, u32[]{:S(2)}) collective-permute-start(bf16[160,1920]{1,0:T(8,128)(2,1)S(1)} %get-tuple-element.128), channel_id=1, source_target_pairs={{0,96},{1,7},{2,98},{3,1},{4,100},{5,3},{6,102},{7,5},{8,104},{9,1... | collective-permute-start | bytes 1843208 | tf_op jit(solution)/shard_map/ppermute | solution.py:393
  70.3 11.5 %collective-permute-start.8 = (bf16[160,640]{1,0:T(8,128)(2,1)S(1)}, bf16[160,640]{1,0:T(8,128)(2,1)S(1)}, u32[]{:S(2)}, u32[]{:S(2)}) collective-permute-start(bf16[160,640]{1,0:T(8,128)(2,1)S(1)} %get-tuple-element.119), channel_id=1, source_target_pairs={{0,16},{1,17},{2,18},{3,19},{4,20},{5,21},{6,22},{7,23},{8,24},{9,... | collective-permute-start | bytes 614408 | tf_op jit(solution)/shard_map/ppermute | solution.py:393
  70.9 10.9 %collective-permute-start.9 = (bf16[160,640]{1,0:T(8,128)(2,1)S(1)}, bf16[160,640]{1,0:T(8,128)(2,1)S(1)}, u32[]{:S(2)}, u32[]{:S(2)}) collective-permute-start(bf16[160,640]{1,0:T(8,128)(2,1)S(1)} %get-tuple-element.120), channel_id=1, source_target_pairs={{0,24},{1,25},{2,26},{3,27},{4,28},{5,29},{6,30},{7,31},{8,16},{9,... | collective-permute-start | bytes 614408 | tf_op jit(solution)/shard_map/ppermute | solution.py:393
  73.0 4.2 %collective-permute-start.10 = (f32[8,384]{1,0:T(8,128)S(1)}, f32[8,384]{1,0:T(8,128)S(1)}, u32[]{:S(2)}, u32[]{:S(2)}) collective-permute-start(f32[8,384]{1,0:T(8,128)S(1)} %get-tuple-element.122), channel_id=1, source_target_pairs={{0,8},{8,0},{1,9},{9,1},{2,10},{10,2},{3,11},{11,3},{4,12},{12,4},... | collective-permute-start | bytes 36872 | tf_op jit(solution)/shard_map/ppermute | solution.py:552
  77.2 4.6 %collective-permute-start.11 = (f32[8,384]{1,0:T(8,128)S(1)}, f32[8,384]{1,0:T(8,128)S(1)}, u32[]{:S(2)}, u32[]{:S(2)}) collective-permute-start(f32[8,384]{1,0:T(8,128)S(1)} %get-tuple-element.125), channel_id=1, source_target_pairs={{0,16},{16,0},{1,17},{17,1},{2,18},{18,2},{3,19},{19,3},{4,20},{20... | collective-permute-start | bytes 36872 | tf_op jit(solution)/shard_map/ppermute | solution.py:556
  79.1 10.7 %collective-permute-start.14 = (f32[80,1920]{1,0:T(8,128)}, f32[80,1920]{1,0:T(8,128)S(1)}, u32[]{:S(2)}, u32[]{:S(2)}) collective-permute-start(f32[80,1920]{1,0:T(8,128)} %get-tuple-element.134), channel_id=1, source_target_pairs={{0,2},{1,17},{2,4},{3,19},{4,6},{5,21},{6,0},{7,23},{8,10},{9,25},... | collective-permute-start | bytes 1843208 | tf_op jit(solution)/shard_map/ppermute | solution.py:393
  80.0 9.8 %collective-permute-start.15 = (f32[80,1920]{1,0:T(8,128)}, f32[80,1920]{1,0:T(8,128)S(1)}, u32[]{:S(2)}, u32[]{:S(2)}) collective-permute-start(f32[80,1920]{1,0:T(8,128)} %get-tuple-element.135), channel_id=1, source_target_pairs={{0,6},{1,25},{2,0},{3,27},{4,2},{5,29},{6,4},{7,31},{8,14},{9,17},... | collective-permute-start | bytes 1843208 | tf_op jit(solution)/shard_map/ppermute | solution.py:393
  82.6 2.7 %copy-start.3 = (f32[160,768]{1,0:T(8,128)}, f32[160,768]{1,0:T(8,128)S(1)}, u32[]{:S(2)}) copy-start(f32[160,768]{1,0:T(8,128)S(1)} %get-tuple-element.140.refs_0_) | copy-start | bytes 1474564
  82.6 10.3 %collective-permute-start.18 = (f32[80,768]{1,0:T(8,128)}, f32[80,768]{1,0:T(8,128)}, u32[]{:S(2)}, u32[]{:S(2)}) collective-permute-start(f32[80,768]{1,0:T(8,128)} %get-tuple-element.141), channel_id=1, source_target_pairs={{0,32},{1,33},{2,34},{3,35},{4,36},{5,37},{6,38},{7,39},{8,40},{9,... | collective-permute-start | bytes 737288 | tf_op jit(solution)/shard_map/ppermute | solution.py:393
  84.5 8.5 %collective-permute-start.19 = (f32[80,768]{1,0:T(8,128)S(1)}, f32[80,768]{1,0:T(8,128)}, u32[]{:S(2)}, u32[]{:S(2)}) collective-permute-start(f32[80,768]{1,0:T(8,128)S(1)} %get-tuple-element.142), channel_id=1, source_target_pairs={{0,96},{1,97},{2,98},{3,99},{4,100},{5,101},{6,102},{7,103},{8,104... | collective-permute-start | bytes 737288 | tf_op jit(solution)/shard_map/ppermute | solution.py:393
  85.3 24.6 %all-to-all-start.1 = ((bf16[8,4,8,1280]{3,2,1,0:T(8,128)(2,1)}), bf16[8,4,8,1280]{3,2,1,0:T(8,128)(2,1)S(1)}, u32[]{:S(2)}, u32[]{:S(2)}) async-start(bf16[8,4,8,1280]{3,2,1,0:T(8,128)(2,1)} %bitcast.7), calls=%async_computation.1 | async-start | bytes 1310720 | tf_op jit(solution)/shard_map/all_to_all | solution.py:559
  88.9 4.1 %copy-start.4 = (f32[160,768]{1,0:T(8,128)S(1)}, f32[160,768]{1,0:T(8,128)}, u32[]{:S(2)}) copy-start(f32[160,768]{1,0:T(8,128)} %copy-done.3) | copy-start | bytes 1474564
  90.0 8.9 %collective-permute-start.16 = (f32[40,1920]{1,0:T(8,128)S(1)}, f32[40,1920]{1,0:T(8,128)S(1)}, u32[]{:S(2)}, u32[]{:S(2)}) collective-permute-start(f32[40,1920]{1,0:T(8,128)S(1)} %get-tuple-element.138), channel_id=1, source_target_pairs={{0,2},{1,17},{2,4},{3,19},{4,6},{5,21},{6,0},{7,23},{8,10},{9,25},... | collective-permute-start | bytes 921608 | tf_op jit(solution)/shard_map/ppermute | solution.py:393
  90.5 10.1 %collective-permute-start.17 = (f32[40,1920]{1,0:T(8,128)S(1)}, f32[40,1920]{1,0:T(8,128)S(1)}, u32[]{:S(2)}, u32[]{:S(2)}) collective-permute-start(f32[40,1920]{1,0:T(8,128)S(1)} %get-tuple-element.139), channel_id=1, source_target_pairs={{0,6},{1,25},{2,0},{3,27},{4,2},{5,29},{6,4},{7,31},{8,14},{9,17},... | collective-permute-start | bytes 921608 | tf_op jit(solution)/shard_map/ppermute | solution.py:393
  94.1 11.5 %collective-permute-start.23 = (f32[40,768]{1,0:T(8,128)S(1)}, f32[40,768]{1,0:T(8,128)S(1)}, u32[]{:S(2)}, u32[]{:S(2)}) collective-permute-start(f32[40,768]{1,0:T(8,128)S(1)} %get-tuple-element.150), channel_id=1, source_target_pairs={{0,32},{1,33},{2,34},{3,35},{4,36},{5,37},{6,38},{7,39},{8,40},{9,... | collective-permute-start | bytes 368648 | tf_op jit(solution)/shard_map/ppermute | solution.py:393
  95.9 9.7 %collective-permute-start.24 = (f32[40,768]{1,0:T(8,128)S(1)}, f32[40,768]{1,0:T(8,128)S(1)}, u32[]{:S(2)}, u32[]{:S(2)}) collective-permute-start(f32[40,768]{1,0:T(8,128)S(1)} %get-tuple-element.151), channel_id=1, source_target_pairs={{0,96},{1,97},{2,98},{3,99},{4,100},{5,101},{6,102},{7,103},{8,104... | collective-permute-start | bytes 368648 | tf_op jit(solution)/shard_map/ppermute | solution.py:393
  100.7 8.6 %collective-permute-start.20 = (f32[20,1920]{1,0:T(8,128)S(1)}, f32[20,1920]{1,0:T(8,128)S(1)}, u32[]{:S(2)}, u32[]{:S(2)}) collective-permute-start(f32[20,1920]{1,0:T(8,128)S(1)} %get-tuple-element.146), channel_id=1, source_target_pairs={{0,16},{1,33},{2,18},{3,35},{4,20},{5,37},{6,22},{7,39},{8,24},{9,... | collective-permute-start | bytes 460808 | tf_op jit(solution)/shard_map/ppermute | solution.py:393
  102.1 7.8 %collective-permute-start.21 = (f32[20,1920]{1,0:T(8,128)S(1)}, f32[20,1920]{1,0:T(8,128)S(1)}, u32[]{:S(2)}, u32[]{:S(2)}) collective-permute-start(f32[20,1920]{1,0:T(8,128)S(1)} %get-tuple-element.147), channel_id=1, source_target_pairs={{0,8},{1,65},{2,10},{3,67},{4,12},{5,69},{6,14},{7,71},{8,0},{9,73... | collective-permute-start | bytes 460808 | tf_op jit(solution)/shard_map/ppermute | solution.py:393
  104.5 5.4 %collective-permute-start.22 = (f32[20,1920]{1,0:T(8,128)S(1)}, f32[20,1920]{1,0:T(8,128)S(1)}, u32[]{:S(2)}, u32[]{:S(2)}) collective-permute-start(f32[20,1920]{1,0:T(8,128)S(1)} %get-tuple-element.148), channel_id=1, source_target_pairs={{0,24},{1,97},{2,26},{3,99},{4,28},{5,101},{6,30},{7,103},{8,16},{... | collective-permute-start | bytes 460808 | tf_op jit(solution)/shard_map/ppermute | solution.py:393
  105.6 5.2 %collective-permute-start.25 = (f32[20,768]{1,0:T(8,128)S(1)}, f32[20,768]{1,0:T(8,128)S(1)}, u32[]{:S(2)}, u32[]{:S(2)}) collective-permute-start(f32[20,768]{1,0:T(8,128)S(1)} %get-tuple-element.158), channel_id=1, source_target_pairs={{0,2},{1,3},{2,4},{3,5},{4,6},{5,7},{6,0},{7,1},{8,10},{9,11},{10,... | collective-permute-start | bytes 184328 | tf_op jit(solution)/shard_map/ppermute | solution.py:393
  106.2 5.6 %collective-permute-start.26 = (f32[20,768]{1,0:T(8,128)S(1)}, f32[20,768]{1,0:T(8,128)S(1)}, u32[]{:S(2)}, u32[]{:S(2)}) collective-permute-start(f32[20,768]{1,0:T(8,128)S(1)} %get-tuple-element.159), channel_id=1, source_target_pairs={{0,4},{1,5},{2,6},{3,7},{4,0},{5,1},{6,2},{7,3},{8,12},{9,13},{10,... | collective-permute-start | bytes 184328 | tf_op jit(solution)/shard_map/ppermute | solution.py:393
  109.3 3.5 %collective-permute-start.27 = (f32[20,768]{1,0:T(8,128)S(1)}, f32[20,768]{1,0:T(8,128)S(1)}, u32[]{:S(2)}, u32[]{:S(2)}) collective-permute-start(f32[20,768]{1,0:T(8,128)S(1)} %get-tuple-element.160), channel_id=1, source_target_pairs={{0,6},{1,7},{2,0},{3,1},{4,2},{5,3},{6,4},{7,5},{8,14},{9,15},{10,... | collective-permute-start | bytes 184328 | tf_op jit(solution)/shard_map/ppermute | solution.py:393
  113.4 4.9 %collective-permute-start.28 = (f32[10,2688]{1,0:T(8,128)S(1)}, f32[10,2688]{1,0:T(8,128)S(1)}, u32[]{:S(2)}, u32[]{:S(2)}) collective-permute-start(f32[10,2688]{1,0:T(8,128)S(1)} %get-tuple-element.163), channel_id=1, source_target_pairs={{0,1},{1,0},{2,3},{3,2},{4,5},{5,4},{6,7},{7,6},{8,9},{9,8},{10,11... | collective-permute-start | bytes 322568 | tf_op jit(solution)/shard_map/ppermute | solution.py:397
